TPU v7x, 32 devices: a whole 2x2x4 slice. The times are simulated.
32 devices in a mesh: groups: 2 (over y), ep: 16 (over z, x, core).
Axes of the slice: x: 2, y: 2, z: 4, core: 2. Of those that a mesh axis runs over, the one named last changes fastest.
Arguments:
- hidden: bfloat16 [64, 7168], P(('groups', 'ep')), parts along dimension 0, may hold values from -6 to 6
- queries: bfloat16 [64, 128, 576], P(('groups', 'ep')), parts along dimension 0, may hold values from -40 to 40
- latent_cache: bfloat16 [64, 2048, 576], P(('groups', 'ep')), parts along dimension 0, may hold values from -8 to 8
- cache_lengths: int32 [64], P(('groups', 'ep')), parts along dimension 0, may hold values from 2 to 2048, as said below
- value_up: bfloat16 [128, 512, 128], P('ep'), may hold values from -0.25 to 0.25
- out_proj: bfloat16 [16384, 7168], P('ep'), may hold values from -0.046875 to 0.046875
- norm_gain: float32 [7168], replicated, may hold values from 0.1 to 1.9
- expert_ids: int32 [64, 8], P(('groups', 'ep')), parts along dimension 0, may hold values from 0 to 15, all different within a row; in each aligned block of 2 rows (0 to 1, 2 to 3, ...) at most 2 rows name the same one
- gate_weights: float32 [64, 8], P(('groups', 'ep')), parts along dimension 0, may hold values from 0.05 to 0.5
- gate_proj: bfloat16 [16, 7168, 1024], P('ep'), may hold values from -0.0625 to 0.0625
- up_proj: bfloat16 [16, 7168, 1024], P('ep'), may hold values from -0.0625 to 0.0625
- down_proj: bfloat16 [16, 1024, 7168], P('ep'), may hold values from -0.1875 to 0.1875
Outputs:
- layer_out: bfloat16 [64, 7168], P(('groups', 'ep')), parts along dimension 0
There are 2 independent parts, one for each index of `groups`. A program takes and returns all parts, laid end to end along the dimension named above; an argument that names none is the same for every part. Nothing has to cross between parts.
Inputs may be any that keep to these rules, and one draw needn't show every extreme that they name: `cache_lengths`: some row of each draw has exactly 2048 live positions and some row exactly 2. `expert_ids`: each row names 8 different experts. The 2 rows of one device name any one expert at most 2 times, so a device sends each expert at most 2 rows; some device of every draw reaches that.
All inputs are finite; a program needn't handle non-finite values.
Results may differ from a plain program's by a relative error of at most 0.0095.
Values may be sent and summed in bfloat16 or wider, within the bound.
No kernel may reach another device: no remote copies, remote signals or barrier semaphores. Data moves between devices by JAX's collectives and lax.ppermute only.
A program may use at most 128 MiB of HBM per device.

v0:
```python
import jax
import jax.numpy as jnp
from jax import lax
from jax.sharding import PartitionSpec as P

EXPERTS = 16


score_scale = 0.07216878364870323
norm_eps = 1e-06


def exchange(value, bit):
    return lax.ppermute(value, "ep", [(i, i ^ (1 << bit)) for i in range(lax.axis_size("ep"))])


def halve(value, bit):
    kept, sent = jnp.split(value, 2, axis=0)
    return kept + exchange(sent.astype(jnp.bfloat16), bit).astype(jnp.float32)


def relative_order(bits):
    return [sum(((p >> (bits - 1 - b)) & 1) << b for b in range(bits)) for p in range(1 << bits)]


def attend(queries, latent_cache, cache_lengths, latent):
    scores = (
        jnp.einsum("rhk,rtk->rht", queries, latent_cache, preferred_element_type=jnp.float32)
        * score_scale
    )
    positions = lax.broadcasted_iota(jnp.int32, scores.shape, 2)
    scores = jnp.where(positions < cache_lengths[:, None, None], scores, -jnp.inf)
    row_peak = jnp.max(scores, axis=2, keepdims=True)
    exp_scores = jnp.exp(scores - row_peak)
    soft_weights = (exp_scores / jnp.sum(exp_scores, axis=2, keepdims=True)).astype(jnp.bfloat16)
    return jnp.einsum(
        "rht,rtl->rhl",
        soft_weights,
        latent_cache[:, :, :latent],
        preferred_element_type=jnp.float32,
    ).astype(jnp.bfloat16)


def on_device(
    hidden,
    queries,
    latent_cache,
    cache_lengths,
    value_up,
    out_proj,
    norm_gain,
    expert_ids,
    gate_weights,
    gate_proj,
    up_proj,
    down_proj,
):
    rows_dev, width = hidden.shape
    heads_dev, latent, _ = value_up.shape
    ep_size = lax.axis_size("ep")
    me = lax.axis_index("ep")
    bits = ep_size.bit_length() - 1
    split_ways = ep_size // EXPERTS
    scatter_bits = min(2, bits)

    latent_out = attend(queries, latent_cache, cache_lengths, latent)

    experts_iota = lax.broadcasted_iota(jnp.int32, (1, 1, EXPERTS), 2)
    named = expert_ids[:, :, None] == experts_iota
    weight = jnp.sum(jnp.where(named, gate_weights[:, :, None], 0.0), axis=1)
    weight = jnp.tile(weight, (1, split_ways))
    weight_top = weight.astype(jnp.bfloat16)
    weight_rest = (weight - weight_top.astype(jnp.float32)).astype(jnp.bfloat16)
    tail = jnp.stack((weight_top, weight_rest), axis=2)
    tail = jnp.pad(tail, ((0, 0), (0, 0), (0, 126)))
    outgoing = latent_out.reshape(rows_dev, ep_size, heads_dev * latent)
    outgoing = jnp.concatenate((outgoing, tail), axis=2).transpose(1, 0, 2)
    incoming = lax.all_to_all(outgoing, "ep", split_axis=0, concat_axis=0, tiled=True)

    order = jnp.array(relative_order(bits), jnp.int32)
    place = (jnp.arange(ep_size)[None, :] == (order ^ me)[:, None]).astype(jnp.float32)
    place = jnp.kron(place, jnp.eye(rows_dev, dtype=jnp.float32)).astype(jnp.bfloat16)
    incoming = incoming.reshape(ep_size * rows_dev, -1)
    rows_in = incoming.shape[0]
    by_head = incoming[:, : heads_dev * latent].reshape(rows_in, heads_dev, latent)
    head_out = jnp.einsum(
        "rhl,hlv->rhv", by_head, value_up, preferred_element_type=jnp.float32
    ).astype(jnp.bfloat16)
    head_rows = jnp.dot(
        place, head_out.reshape(rows_in, -1), preferred_element_type=jnp.float32
    ).astype(jnp.bfloat16)
    tail_in = jnp.dot(
        place, incoming[:, heads_dev * latent :], preferred_element_type=jnp.float32
    )
    row_weight = tail_in[:, 0:1] + tail_in[:, 1:2]

    summed = jnp.dot(head_rows, out_proj, preferred_element_type=jnp.float32)
    own = summed[:rows_dev] + hidden.astype(jnp.float32)
    summed = jnp.concatenate((own, summed[rows_dev:]), axis=0)
    for bit in range(scatter_bits):
        summed = halve(summed, bit)
    for bit in range(scatter_bits, bits):
        shape = summed.shape
        swapped = summed.astype(jnp.bfloat16).reshape(1 << (bit - scatter_bits), 2, -1, width)
        swapped = jnp.concatenate((swapped[:, 1:], swapped[:, :1]), axis=1).reshape(shape)
        summed = summed + exchange(swapped, bit).astype(jnp.float32)
    residual = summed[:rows_dev]
    inv_rms = lax.rsqrt(jnp.mean(summed * summed, axis=1, keepdims=True) + norm_eps)
    moe_in = (summed * inv_rms * norm_gain[None, :]).astype(jnp.bfloat16)
    for bit in reversed(range(scatter_bits)):
        moe_in = jnp.concatenate((moe_in, exchange(moe_in, bit)), axis=0)

    slice_width = width // split_ways
    part = me // EXPERTS
    if split_ways > 1:
        moe_in = lax.dynamic_slice_in_dim(moe_in, part * slice_width, slice_width, axis=1)
    gate_act = jnp.dot(moe_in, gate_proj[0], preferred_element_type=jnp.float32)
    up_act = jnp.dot(moe_in, up_proj[0], preferred_element_type=jnp.float32)
    if split_ways > 1:
        to_one = place.astype(jnp.float32)
        stacked = jnp.stack((gate_act, up_act)).astype(jnp.bfloat16).astype(jnp.float32)
        stacked = jnp.einsum("sr,asf->arf", to_one, stacked)
        for bit in range(EXPERTS.bit_length() - 1, bits):
            stacked = stacked + exchange(stacked.astype(jnp.bfloat16), bit).astype(jnp.float32)
        stacked = jnp.einsum("sr,arf->asf", to_one, stacked, precision=lax.Precision.HIGHEST)
        gate_act, up_act = stacked[0], stacked[1]
    units = (jax.nn.silu(gate_act) * up_act).astype(jnp.bfloat16)
    weighted = jnp.dot(units, down_proj[0], preferred_element_type=jnp.float32) * row_weight
    if split_ways > 1:
        wide = jnp.zeros((rows_in, width), jnp.float32)
        weighted = lax.dynamic_update_slice_in_dim(wide, weighted, part * slice_width, axis=1)
    for bit in range(bits):
        weighted = halve(weighted, bit)
    return (residual + weighted).astype(jnp.bfloat16)


def solution(mesh):
    return jax.shard_map(
        on_device,
        mesh=mesh,
        in_specs=(
            P(("groups", "ep"), None),
            P(("groups", "ep"), None, None),
            P(("groups", "ep"), None, None),
            P(("groups", "ep")),
            P("ep", None, None),
            P("ep", None),
            P(),
            P(("groups", "ep"), None),
            P(("groups", "ep"), None),
            P("ep", None, None),
            P("ep", None, None),
            P("ep", None, None),
        ),
        out_specs=P(("groups", "ep"), None),
        check_vma=False,
    )
```

profile of v0, /device:TPU:0, one launch (start us, length us, event | category | flops | bytes accessed | tf_op | source)
XLA Modules:
  0.0 100.2 jit_solution(10125817070390331835)
XLA Ops:
  0.0 0.0 copy-start
  0.0 0.9 select_reduce_fusion
  0.9 0.1 copy.27
  1.0 3.5 %fusion.14 = f32[2,128,2048]{2,1,0:T(8,128)S(1)} fusion(bf16[2,128,576]{1,2,0:T(8,128)(2,1)} %param.14, bf16[2,2048,576]{1,2,0:T(8,128)(2,1)} %param.15, s32[2]{0:T(128)} %param.16), kind=kOutput, calls=%fused_computation.13 | convolution fusion | flops 605552640 | bytes 7110664 | tf_op jit(solution)/shard_map/rhk,rtk->rht/dot_general | solution.py:28
  4.5 0.5 fusion.51
  4.9 0.0 copy-start.4
  5.0 3.8 %fusion.15 = bf16[2,128,512]{2,1,0:T(8,128)(2,1)S(1)} fusion(bf16[2,2048,576]{1,2,0:T(8,128)(2,1)} %param.15, f32[2,128]{1,0:T(2,128)S(1)} %fusion.51, f32[2,128,2048]{2,1,0:T(8,128)S(1)} %fusion.14), kind=kOutput, calls=%fused_computation.16 | convolution fusion | flops 538577152 | bytes 8651776 | tf_op jit(solution)/shard_map/rht,rtl->rhl/dot_general | solution.py:36
  8.8 0.1 reshape.103
  8.9 0.3 copy.22
  9.2 0.9 fusion.23
  10.1 7.4 %all-to-all-start = ((bf16[16,2,4224]{2,1,0:T(2,128)(2,1)}), bf16[16,2,4224]{2,1,0:T(2,128)(2,1)S(1)}, u32[]{:S(2)}, u32[]{:S(2)}) async-start(bf16[16,2,4224]{2,1,0:T(2,128)(2,1)} %fusion.23), calls=%async_computation | async-start | bytes 540672 | tf_op jit(solution)/shard_map/all_to_all | solution.py:78
  17.5 0.0 copy-done.4
  17.5 0.1 fusion.42
  17.6 0.1 multiply_convert_fusion
  17.7 0.2 convert_element_type.129
  17.9 9.8 %all-to-all-done = bf16[16,2,4224]{2,1,0:T(2,128)(2,1)S(1)} async-done(((bf16[16,2,4224]{2,1,0:T(2,128)(2,1)}), bf16[16,2,4224]{2,1,0:T(2,128)(2,1)S(1)}, u32[]{:S(2)}, u32[]{:S(2)}) %all-to-all-start) | async-done | bytes 270368 | tf_op jit(solution)/shard_map/all_to_all | solution.py:78
  27.7 0.1 reshape.104
  27.8 0.0 copy-done
  27.8 0.3 fusion.18
  28.1 0.0 copy-start.3
  28.1 6.6 %fusion.19 = f32[32,7168]{1,0:T(8,128)S(1)} fusion(bf16[1024,7168]{1,0:T(8,128)(2,1)} %param.18, bf16[32,32]{1,0:T(8,128)(2,1)S(1)} %convert_element_type.129, bf16[8,4,8,128]{3,2,1,0:T(8,128)(2,1)S(1)} %fusion.18), kind=kOutput, calls=%fused_computation.20 | convolution fusion | flops 471891968 | bytes 15665152 | tf_op jit(solution)/shard_map/dot_general | solution.py:97
  34.8 0.0 copy-start.2
  34.8 0.1 collective-permute-start
  34.9 0.0 copy-done.3
  34.9 0.1 slice.51
  35.0 1.4 %collective-permute-done = bf16[16,7168]{1,0:T(8,128)(2,1)S(1)} collective-permute-done((bf16[16,7168]{1,0:T(8,128)(2,1)S(1)}, bf16[16,7168]{1,0:T(8,128)(2,1)S(1)}, u32[]{:S(2)}, u32[]{:S(2)}) %collective-permute-start) | collective-permute-done | bytes 229408 | tf_op jit(solution)/shard_map/ppermute | solution.py:14
  36.4 0.1 fusion.21
  36.5 0.3 collective-permute-start.1
  36.7 5.0 %collective-permute-done.1 = bf16[8,7168]{1,0:T(8,128)(2,1)S(1)} collective-permute-done((bf16[8,7168]{1,0:T(8,128)(2,1)S(1)}, bf16[8,7168]{1,0:T(8,128)(2,1)S(1)}, u32[]{:S(2)}, u32[]{:S(2)}) %collective-permute-start.1) | collective-permute-done | bytes 114720 | tf_op jit(solution)/shard_map/ppermute | solution.py:14
  41.7 0.1 reshape.107
  41.8 0.1 pad_maximum_fusion.5
  42.0 0.7 collective-permute-start.2
  42.6 4.2 %collective-permute-done.2 = bf16[8,7168]{1,0:T(8,128)(2,1)S(1)} collective-permute-done((bf16[8,7168]{1,0:T(8,128)(2,1)S(1)}, bf16[8,7168]{1,0:T(8,128)(2,1)S(1)}, u32[]{:S(2)}, u32[]{:S(2)}) %collective-permute-start.2) | collective-permute-done | bytes 114720 | tf_op jit(solution)/shard_map/ppermute | solution.py:14
  46.9 0.1 fusion.49
  47.0 0.2 pad_maximum_fusion.6
  47.2 1.2 %collective-permute-start.3 = (bf16[8,7168]{1,0:T(8,128)(2,1)S(1)}, bf16[8,7168]{1,0:T(8,128)(2,1)S(1)}, u32[]{:S(2)}, u32[]{:S(2)}) collective-permute-start(bf16[8,7168]{1,0:T(8,128)(2,1)S(1)} %reshape.110), channel_id=1, source_target_pairs={{0,8},{1,9},{2,10},{3,11},{4,12},{5,13},{6,14},{7,15},{8,0},{9,1},... | collective-permute-start | bytes 344072 | tf_op jit(solution)/shard_map/ppermute | solution.py:14
  48.4 5.8 %collective-permute-done.3 = bf16[8,7168]{1,0:T(8,128)(2,1)S(1)} collective-permute-done((bf16[8,7168]{1,0:T(8,128)(2,1)S(1)}, bf16[8,7168]{1,0:T(8,128)(2,1)S(1)}, u32[]{:S(2)}, u32[]{:S(2)}) %collective-permute-start.3) | collective-permute-done | bytes 114720 | tf_op jit(solution)/shard_map/ppermute | solution.py:14
  54.2 0.2 multiply_reduce_fusion
  54.4 0.0 copy-done.2
  54.4 0.1 multiply_convert_fusion.1
  54.5 0.5 collective-permute-start.4
  55.0 4.4 %collective-permute-done.4 = bf16[8,7168]{1,0:T(8,128)(2,1)S(1)} collective-permute-done((bf16[8,7168]{1,0:T(8,128)(2,1)S(1)}, bf16[8,7168]{1,0:T(8,128)(2,1)S(1)}, u32[]{:S(2)}, u32[]{:S(2)}) %collective-permute-start.4) | collective-permute-done | bytes 114720 | tf_op jit(solution)/shard_map/ppermute | solution.py:14
  59.4 0.1 collective-permute-start.5
  59.5 0.1 fusion.40
  59.6 0.2 fusion.39
  59.8 1.2 %collective-permute-done.5 = bf16[16,7168]{1,0:T(8,128)(2,1)S(1)} collective-permute-done((bf16[16,7168]{1,0:T(8,128)(2,1)S(1)}, bf16[16,7168]{1,0:T(8,128)(2,1)S(1)}, u32[]{:S(2)}, u32[]{:S(2)}) %collective-permute-start.5) | collective-permute-done | bytes 229408 | tf_op jit(solution)/shard_map/ppermute | solution.py:14
  60.9 7.8 %fusion.3 = f32[32,1024]{1,0:T(8,128)S(1)} fusion(bf16[1,7168,1024]{2,1,0:T(8,128)(2,1)} %param.23, bf16[16,7168]{1,0:T(8,128)(2,1)S(1)} %collective-permute-done.5, bf16[8,7168]{1,0:T(8,128)(2,1)S(1)} %collective-permute-done.4, bf16[8,7168]{1,0:T(8,128)(2,1)S(1)} %multiply_convert_fusion.1), kind=kOutput, calls=%fused_computation.3 | convolution fusion | flops 471138304 | bytes 15269888 | tf_op jit(solution)/shard_map/dot_general | solution.py:118
  68.7 0.0 copy-start.1
  68.7 14.6 %fusion.7 = f32[32,7168]{1,0:T(8,128)S(1)} fusion(bf16[1,1024,7168]{2,1,0:T(8,128)(2,1)} %param.24, f32[32]{0:T(128)S(1)} %fusion.39, f32[32,1024]{1,0:T(8,128)S(1)} %fusion.3, bf16[1,7168,1024]{2,1,0:T(8,128)(2,1)} %param.22, bf16[16,7168]{1,0:T(8,128)(2,1)S(1)} %collective-permute-done.5, bf16[8,7168]{1,0:T(8,128)(2,1)S(1)} %collective-permute-done.4, ...), kind=kOutput, calls=%fused_computation.7 | convolution fusion | flops 941326336 | bytes 30867584 | tf_op jit(solution)/shard_map/dot_general | solution.py:128
  83.4 0.2 collective-permute-start.6
  83.6 1.4 %collective-permute-done.6 = bf16[16,7168]{1,0:T(8,128)(2,1)S(1)} collective-permute-done((bf16[16,7168]{1,0:T(8,128)(2,1)S(1)}, bf16[16,7168]{1,0:T(8,128)(2,1)S(1)}, u32[]{:S(2)}, u32[]{:S(2)}) %collective-permute-start.6) | collective-permute-done | bytes 229408 | tf_op jit(solution)/shard_map/ppermute | solution.py:14
  85.0 0.1 slice_add_fusion
  85.0 0.5 collective-permute-start.7
  85.5 4.8 %collective-permute-done.7 = bf16[8,7168]{1,0:T(8,128)(2,1)S(1)} collective-permute-done((bf16[8,7168]{1,0:T(8,128)(2,1)S(1)}, bf16[8,7168]{1,0:T(8,128)(2,1)S(1)}, u32[]{:S(2)}, u32[]{:S(2)}) %collective-permute-start.7) | collective-permute-done | bytes 114720 | tf_op jit(solution)/shard_map/ppermute | solution.py:14
  90.3 0.1 collective-permute-start.8
  90.4 4.2 %collective-permute-done.8 = bf16[4,7168]{1,0:T(4,128)(2,1)S(1)} collective-permute-done((bf16[4,7168]{1,0:T(4,128)(2,1)S(1)}, bf16[4,7168]{1,0:T(4,128)(2,1)S(1)}, u32[]{:S(2)}, u32[]{:S(2)}) %collective-permute-start.8) | collective-permute-done | bytes 57376 | tf_op jit(solution)/shard_map/ppermute | solution.py:14
  94.7 0.1 collective-permute-start.9
  94.7 4.8 %collective-permute-done.9 = bf16[2,7168]{1,0:T(2,128)(2,1)S(1)} collective-permute-done((bf16[2,7168]{1,0:T(2,128)(2,1)S(1)}, bf16[2,7168]{1,0:T(2,128)(2,1)S(1)}, u32[]{:S(2)}, u32[]{:S(2)}) %collective-permute-start.9) | collective-permute-done | bytes 28704 | tf_op jit(solution)/shard_map/ppermute | solution.py:14
  99.5 0.7 fusion.38
  100.2 0.0 copy-done.1
  (22 shorter events, 0.5 us)
Async XLA Ops:
  0.0 27.8 %copy-start = (bf16[8,512,128]{2,1,0:T(8,128)(2,1)S(1)}, bf16[8,512,128]{2,1,0:T(8,128)(2,1)}, u32[]{:S(2)}) copy-start(bf16[8,512,128]{2,1,0:T(8,128)(2,1)} %param.17) | copy-start | bytes 3145732
  4.9 12.6 %copy-start.4 = (s32[16]{0:T(128)S(1)}, s32[16]{0:T(128)}, u32[]{:S(2)}) copy-start(s32[16]{0:T(128)} %constant.23.clone) | copy-start | bytes 196
  10.1 17.5 %all-to-all-start = ((bf16[16,2,4224]{2,1,0:T(2,128)(2,1)}), bf16[16,2,4224]{2,1,0:T(2,128)(2,1)S(1)}, u32[]{:S(2)}, u32[]{:S(2)}) async-start(bf16[16,2,4224]{2,1,0:T(2,128)(2,1)} %fusion.23), calls=%async_computation | async-start | bytes 540672 | tf_op jit(solution)/shard_map/all_to_all | solution.py:78
  28.1 6.8 %copy-start.3 = (bf16[2,7168]{1,0:T(2,128)(2,1)S(1)}, bf16[2,7168]{1,0:T(2,128)(2,1)}, u32[]{:S(2)}) copy-start(bf16[2,7168]{1,0:T(2,128)(2,1)} %param.13) | copy-start | bytes 86020
  34.8 19.6 %copy-start.2 = (f32[7168]{0:T(1024)S(1)}, f32[7168]{0:T(1024)}, u32[]{:S(2)}) copy-start(f32[7168]{0:T(1024)} %param.19) | copy-start | bytes 86020
  34.8 1.6 %collective-permute-start = (bf16[16,7168]{1,0:T(8,128)(2,1)S(1)}, bf16[16,7168]{1,0:T(8,128)(2,1)S(1)}, u32[]{:S(2)}, u32[]{:S(2)}) collective-permute-start(bf16[16,7168]{1,0:T(8,128)(2,1)S(1)} %split.87), channel_id=1, source_target_pairs={{0,1},{1,0},{2,3},{3,2},{4,5},{5,4},{6,7},{7,6},{8,9},{9,8},{10,11... | collective-permute-start | bytes 688136 | tf_op jit(solution)/shard_map/ppermute | solution.py:14
  36.5 5.3 %collective-permute-start.1 = (bf16[8,7168]{1,0:T(8,128)(2,1)S(1)}, bf16[8,7168]{1,0:T(8,128)(2,1)S(1)}, u32[]{:S(2)}, u32[]{:S(2)}) collective-permute-start(bf16[8,7168]{1,0:T(8,128)(2,1)S(1)} %split.89), channel_id=1, source_target_pairs={{0,2},{1,3},{2,0},{3,1},{4,6},{5,7},{6,4},{7,5},{8,10},{9,11},{10,... | collective-permute-start | bytes 344072 | tf_op jit(solution)/shard_map/ppermute | solution.py:14
  42.0 4.9 %collective-permute-start.2 = (bf16[8,7168]{1,0:T(8,128)(2,1)S(1)}, bf16[8,7168]{1,0:T(8,128)(2,1)S(1)}, u32[]{:S(2)}, u32[]{:S(2)}) collective-permute-start(bf16[8,7168]{1,0:T(8,128)(2,1)S(1)} %reshape.108), channel_id=1, source_target_pairs={{0,4},{1,5},{2,6},{3,7},{4,0},{5,1},{6,2},{7,3},{8,12},{9,13},{10,... | collective-permute-start | bytes 344072 | tf_op jit(solution)/shard_map/ppermute | solution.py:14
  47.2 7.0 %collective-permute-start.3 = (bf16[8,7168]{1,0:T(8,128)(2,1)S(1)}, bf16[8,7168]{1,0:T(8,128)(2,1)S(1)}, u32[]{:S(2)}, u32[]{:S(2)}) collective-permute-start(bf16[8,7168]{1,0:T(8,128)(2,1)S(1)} %reshape.110), channel_id=1, source_target_pairs={{0,8},{1,9},{2,10},{3,11},{4,12},{5,13},{6,14},{7,15},{8,0},{9,1},... | collective-permute-start | bytes 344072 | tf_op jit(solution)/shard_map/ppermute | solution.py:14
  54.5 4.9 %collective-permute-start.4 = (bf16[8,7168]{1,0:T(8,128)(2,1)S(1)}, bf16[8,7168]{1,0:T(8,128)(2,1)S(1)}, u32[]{:S(2)}, u32[]{:S(2)}) collective-permute-start(bf16[8,7168]{1,0:T(8,128)(2,1)S(1)} %multiply_convert_fusion.1), channel_id=1, source_target_pairs={{0,2},{1,3},{2,0},{3,1},{4,6},{5,7},{6,4},{7,5},{8,10},{9,11},{10,... | collective-permute-start | bytes 344072 | tf_op jit(solution)/shard_map/ppermute | solution.py:14
  59.4 1.6 %collective-permute-start.5 = (bf16[16,7168]{1,0:T(8,128)(2,1)S(1)}, bf16[16,7168]{1,0:T(8,128)(2,1)S(1)}, u32[]{:S(2)}, u32[]{:S(2)}) collective-permute-start(bf16[16,7168]{1,0:T(8,128)(2,1)S(1)} %pad_maximum_fusion.2), channel_id=1, source_target_pairs={{0,1},{1,0},{2,3},{3,2},{4,5},{5,4},{6,7},{7,6},{8,9},{9,8},{10,11... | collective-permute-start | bytes 688136 | tf_op jit(solution)/shard_map/ppermute | solution.py:14
  68.7 31.4 %copy-start.1 = (bf16[8,512,128]{2,1,0:T(8,128)(2,1)S(1)}, bf16[8,512,128]{2,1,0:T(8,128)(2,1)}, u32[]{:S(2)}) copy-start(bf16[8,512,128]{2,1,0:T(8,128)(2,1)} %param.17) | copy-start | bytes 3145732
  83.4 1.6 %collective-permute-start.6 = (bf16[16,7168]{1,0:T(8,128)(2,1)S(1)}, bf16[16,7168]{1,0:T(8,128)(2,1)S(1)}, u32[]{:S(2)}, u32[]{:S(2)}) collective-permute-start(bf16[16,7168]{1,0:T(8,128)(2,1)S(1)} %split.86), channel_id=1, source_target_pairs={{0,1},{1,0},{2,3},{3,2},{4,5},{5,4},{6,7},{7,6},{8,9},{9,8},{10,11... | collective-permute-start | bytes 688136 | tf_op jit(solution)/shard_map/ppermute | solution.py:14
  85.0 5.3 %collective-permute-start.7 = (bf16[8,7168]{1,0:T(8,128)(2,1)S(1)}, bf16[8,7168]{1,0:T(8,128)(2,1)S(1)}, u32[]{:S(2)}, u32[]{:S(2)}) collective-permute-start(bf16[8,7168]{1,0:T(8,128)(2,1)S(1)} %split.88), channel_id=1, source_target_pairs={{0,2},{1,3},{2,0},{3,1},{4,6},{5,7},{6,4},{7,5},{8,10},{9,11},{10,... | collective-permute-start | bytes 344072 | tf_op jit(solution)/shard_map/ppermute | solution.py:14
  90.3 4.2 %collective-permute-start.8 = (bf16[4,7168]{1,0:T(4,128)(2,1)S(1)}, bf16[4,7168]{1,0:T(4,128)(2,1)S(1)}, u32[]{:S(2)}, u32[]{:S(2)}) collective-permute-start(bf16[4,7168]{1,0:T(4,128)(2,1)S(1)} %split.90), channel_id=1, source_target_pairs={{0,4},{1,5},{2,6},{3,7},{4,0},{5,1},{6,2},{7,3},{8,12},{9,13},{10,... | collective-permute-start | bytes 172040 | tf_op jit(solution)/shard_map/ppermute | solution.py:14
  94.7 4.8 %collective-permute-start.9 = (bf16[2,7168]{1,0:T(2,128)(2,1)S(1)}, bf16[2,7168]{1,0:T(2,128)(2,1)S(1)}, u32[]{:S(2)}, u32[]{:S(2)}) collective-permute-start(bf16[2,7168]{1,0:T(2,128)(2,1)S(1)} %split.91), channel_id=1, source_target_pairs={{0,8},{1,9},{2,10},{3,11},{4,12},{5,13},{6,14},{7,15},{8,0},{9,1},... | collective-permute-start | bytes 86024 | tf_op jit(solution)/shard_map/ppermute | solution.py:14
where the time goes:
time: 100 us
  waiting for transfers between devices  46.7 us (47%)
  matrix products  36.8 us (37%)
  starting transfers between devices  11 us (11%)
  other arithmetic  4.11 us (4%)
  local copies, waits for them, and re-layouts  1.32 us (1%)
    ppermute x10, waiting for transfers between devices, exchange(): lax.ppermute(value, 'ep', [(i, i ^ 1 << bit) for i in range(lax.axis_size...  36.9 us
    dot_general x1, matrix products, on_device(): jnp.dot(units, down_proj[0], preferred_element_type=jnp.float32)  14.6 us
    all_to_all x1, waiting for transfers between devices, on_device(): lax.all_to_all(outgoing, 'ep', split_axis=0, concat_axis=0, tiled=True)  9.79 us
    dot_general x1, matrix products, on_device(): up_act = jnp.dot(moe_in, up_proj[0], preferred_element_type=jnp.float32)  7.79 us
    all_to_all x1, starting transfers between devices, on_device(): lax.all_to_all(outgoing, 'ep', split_axis=0, concat_axis=0, tiled=True)  7.36 us
    dot_general x1, matrix products, on_device(): summed = jnp.dot(head_rows, out_proj, preferred_element_type=jnp.float32)  6.64 us
    dot_general x1, matrix products, attend(): jnp.einsum('rht,rtl->rhl', soft_weights, latent_cache[:, :, :latent], pre...  3.82 us
    ppermute x10, starting transfers between devices, exchange(): lax.ppermute(value, 'ep', [(i, i ^ 1 << bit) for i in range(lax.axis_size...  3.59 us
  transfers between devices with their start and end apart: 11, of which 11 were waited for; matrix products, arithmetic and copies ran while one was open for 1% of the time, Pallas kernels for 0%

commit v1 on v0

v1 whole, which is shorter than its diff:
```python
import functools

import jax
import jax.numpy as jnp
from jax import lax
from jax.experimental import pallas as pl
from jax.experimental.pallas import tpu as pltpu
from jax.sharding import PartitionSpec as P

EXPERTS = 16


score_scale = 0.07216878364870323
norm_eps = 1e-06


def exchange(value, bit):
    return trade(value, 1 << bit)


def trade(value, mask):
    return lax.ppermute(value, "ep", [(i, i ^ mask) for i in range(lax.axis_size("ep"))])


def relative_order(bits):
    return [sum(((p >> (bits - 1 - b)) & 1) << b for b in range(bits)) for p in range(1 << bits)]


LANES = 128
MIB = 1 << 20
IN_VMEM = pl.BlockSpec(memory_space=pltpu.VMEM)
IN_SMEM = pl.BlockSpec(memory_space=pltpu.SMEM)
IN_HBM = pl.BlockSpec(memory_space=pltpu.HBM)
VMEM_ARRAY = pltpu.VMEM


def in_vmem(value):
    return pltpu.with_memory_space_constraint(value, pltpu.VMEM)


def in_hbm(value):
    return pltpu.with_memory_space_constraint(value, pltpu.HBM)


def pieces(source, target, sems, first):
    count = sems.shape[0] - first
    run = source.shape[0] // count
    return [
        pltpu.make_async_copy(
            source.at[pl.ds(i * run, run)], target.at[pl.ds(i * run, run)], sems.at[first + i]
        )
        for i in range(count)
    ]


def load_kernel(source, after, target, sems):
    copies = pieces(source, target, sems, 0)
    for copy in copies:
        copy.start()
    for copy in copies:
        copy.wait()


def load(source, after):
    return pl.pallas_call(
        load_kernel,
        out_shape=VMEM_ARRAY(source.shape, source.dtype),
        in_specs=[IN_HBM, IN_VMEM],
        out_specs=IN_VMEM,
        scratch_shapes=[pltpu.SemaphoreType.DMA((4,))],
        compiler_params=pltpu.CompilerParams(vmem_limit_bytes=MIB),
        cost_estimate=pl.CostEstimate(
            flops=0, bytes_accessed=2 * source.size * source.dtype.itemsize, transcendentals=0
        ),
    )(in_hbm(source), in_vmem(after))


def attend_kernel(
    order, lengths, me, queries, cache, proj, value_up, kept, sent, proj_in, value_in, held, wide, sems
):
    rows_dev, _, heads = queries.shape
    context = cache.shape[2]
    latent = wide.shape[-1]
    caches = [pltpu.make_async_copy(cache.at[r], held.at[r], sems.at[r]) for r in range(rows_dev)]
    weights = [pltpu.make_async_copy(value_up, value_in, sems.at[rows_dev])]
    weights += pieces(proj, proj_in, sems, rows_dev + 1)
    for copy in caches + weights:
        copy.start()
    for r in range(rows_dev):
        caches[r].wait()
        scores = score_scale * lax.dot_general(
            queries[r], held[r], (((0,), (0,)), ((), ())), preferred_element_type=jnp.float32
        )
        positions = lax.broadcasted_iota(jnp.int32, (heads, context), 1)
        scores = jnp.where(positions < lengths[r], scores, -jnp.inf)
        exp_scores = jnp.exp(scores - jnp.max(scores, axis=1, keepdims=True))
        inverse = 1.0 / jnp.sum(exp_scores, axis=1, keepdims=True)
        soft_weights = (exp_scores * inverse).astype(jnp.bfloat16)
        got = lax.dot_general(
            soft_weights,
            held[r, :latent],
            (((1,), (1,)), ((), ())),
            preferred_element_type=jnp.float32,
        )
        if order:
            per = wide.shape[1] // rows_dev
            wide[:, r * per : (r + 1) * per] = got.reshape(-1, per, latent)
        else:
            kept[r] = got.astype(kept.dtype)
    half = len(order) // 2
    for p, s in enumerate(order):
        target = (kept, sent)[p // half]
        target[p % half] = wide[me[0] ^ s].astype(target.dtype)
    for copy in weights:
        copy.wait()


def attend(queries, latent_cache, cache_lengths, out_proj, value_up, order, me):
    rows_dev, heads, key_width = queries.shape
    context = latent_cache.shape[1]
    heads_dev, latent, _ = value_up.shape
    shape = (len(order) // 2, rows_dev * heads_dev, latent) if order else (rows_dev, heads, latent)
    wide = (max(2 * shape[0], 1), shape[1], latent) if order else (1, 8, latent)
    spare = shape if order else (1, 16, latent)
    return pl.pallas_call(
        functools.partial(attend_kernel, order),
        out_shape=(
            VMEM_ARRAY(shape, jnp.bfloat16),
            VMEM_ARRAY(spare, jnp.bfloat16),
            VMEM_ARRAY(out_proj.shape, out_proj.dtype),
            VMEM_ARRAY(value_up.shape, value_up.dtype),
        ),
        in_specs=[IN_SMEM, IN_SMEM, IN_VMEM, IN_HBM, IN_HBM, IN_HBM],
        out_specs=(IN_VMEM,) * 4,
        scratch_shapes=[
            pltpu.VMEM((rows_dev, key_width, context), jnp.bfloat16),
            pltpu.VMEM(wide, jnp.float32),
            pltpu.SemaphoreType.DMA((rows_dev + 5,)),
        ],
        compiler_params=pltpu.CompilerParams(vmem_limit_bytes=24 * MIB),
    )(
        cache_lengths,
        me[None],
        queries.transpose(0, 2, 1),
        in_hbm(latent_cache.transpose(0, 2, 1)),
        in_hbm(out_proj),
        in_hbm(value_up),
    )


def dealt(sources, ways, run):
    return [
        [
            (a, (g * ways + i) * run)
            for a, blocks in enumerate(sources)
            for g in range(blocks // (ways * run))
        ]
        for i in range(ways)
    ]


def deal_kernel(plan, run, count, *refs):
    sources, targets = refs[:count], refs[-len(plan) :]
    for target, runs in zip(targets, plan):
        for j, (a, first) in enumerate(runs):
            target[j * run : (j + 1) * run] = sources[a][first : first + run]


def deal(sources, ways, run):
    plan = dealt([a.shape[0] for a in sources], ways, run)
    shape = (len(plan[0]) * run, *sources[0].shape[1:])
    return pl.pallas_call(
        functools.partial(deal_kernel, plan, run, len(sources)),
        out_shape=tuple(jax.ShapeDtypeStruct(shape, sources[0].dtype) for _ in plan),
        in_specs=[IN_VMEM] * len(sources),
        out_specs=(IN_VMEM,) * ways,
        compiler_params=pltpu.CompilerParams(vmem_limit_bytes=4 * MIB),
    )(*sources)


def project_kernel(
    tile, count, *refs
):
    row_of, value_up, proj, hidden, tail = refs[count : count + 5]
    kept, sent = refs[-2:]
    heads_dev = value_up.shape[0]
    half, wide = kept.shape
    rows_dev, width = hidden.shape
    maps = jnp.concatenate([value_up[h] for h in range(heads_dev)], axis=1)
    by_head = jnp.concatenate([a[...].reshape(-1, a.shape[-1]) for a in refs[:count]], axis=0)
    mixed = jnp.dot(by_head, maps, preferred_element_type=jnp.float32)
    row_head = lax.rem(lax.broadcasted_iota(jnp.int32, mixed.shape, 0), heads_dev)
    value_dim = value_up.shape[2]
    column_head = lax.broadcasted_iota(jnp.int32, mixed.shape, 1) // value_dim
    mixed = jnp.where(row_head == column_head, mixed, 0.0).astype(jnp.bfloat16)
    source = lax.broadcasted_iota(jnp.int32, (2 * half, mixed.shape[0]), 1) // heads_dev
    select = (row_of[...] == source).astype(jnp.bfloat16)
    head_rows = jnp.dot(select, mixed, preferred_element_type=jnp.float32)
    head_rows = head_rows.astype(jnp.bfloat16)

    @pl.loop(0, width // tile)
    def _(i):
        columns = pl.ds(pl.multiple_of(i * tile, tile), tile)
        terms = jnp.dot(head_rows, proj[:, columns], preferred_element_type=jnp.float32)
        kept[:, columns] = terms[:half]
        kept[0:rows_dev, columns] += hidden[:, columns].astype(jnp.float32)
        sent[:, columns] = terms[half:].astype(sent.dtype)

    kept[:, width:] = jnp.zeros((half, wide - width), kept.dtype)
    kept[0:rows_dev, width:] = tail[...]
    sent[:, width:] = jnp.zeros((half, wide - width), sent.dtype)


def project(by_head, row_of, value_up, out_proj, hidden, tail):
    rows_in = row_of.shape[0]
    width = hidden.shape[1]
    shape = (rows_in // 2, width + LANES)
    return pl.pallas_call(
        functools.partial(project_kernel, 512, len(by_head)),
        out_shape=(
            jax.ShapeDtypeStruct(shape, jnp.float32),
            jax.ShapeDtypeStruct(shape, jnp.bfloat16),
        ),
        in_specs=[IN_VMEM] * (len(by_head) + 5),
        out_specs=(IN_VMEM, IN_VMEM),
        compiler_params=pltpu.CompilerParams(vmem_limit_bytes=8 * MIB),
    )(
        *by_head,
        row_of,
        in_vmem(value_up),
        in_vmem(out_proj),
        hidden,
        tail,
    )


def halve_kernel(kept, got, next_kept, sent):
    half = sent.shape[0]
    total = kept[...] + got[...].astype(jnp.float32)
    next_kept[...] = total[:half]
    sent[...] = total[half:].astype(sent.dtype)


def swap_kernel(shift, kept, got, total_ref, sent):
    total = kept[...] + got[...].astype(jnp.float32)
    rows = total.shape[0]
    row = lax.broadcasted_iota(jnp.int32, total.shape, 0)
    later, earlier = pltpu.roll(total, rows - shift, 0), pltpu.roll(total, shift, 0)
    total_ref[...] = total
    sent[...] = jnp.where((row & shift) == 0, later, earlier).astype(sent.dtype)


def combine(kernel, kept, got, out_rows):
    shape = (out_rows, kept.shape[1])
    return pl.pallas_call(
        kernel,
        out_shape=(
            jax.ShapeDtypeStruct(shape, jnp.float32),
            jax.ShapeDtypeStruct(shape, jnp.bfloat16),
        ),
        in_specs=[IN_VMEM] * 2,
        out_specs=(IN_VMEM, IN_VMEM),
        compiler_params=pltpu.CompilerParams(
            vmem_limit_bytes=2 * MIB + 24 * kept.size
        ),
    )(kept, got)


def norm_kernel(kept, got, gain, residual, moe_in):
    rows_dev, width = residual.shape
    total = kept[...] + got[...].astype(jnp.float32)
    body = total[:, :width]
    square = jnp.mean(body * body, axis=1, keepdims=True)
    residual[...] = body[:rows_dev]
    moe_in[:, :width] = (body * lax.rsqrt(square + norm_eps) * gain[...]).astype(moe_in.dtype)
    moe_in[:, width:] = total[:, width:].astype(moe_in.dtype)


def norm(kept, got, gain, rows_dev):
    return pl.pallas_call(
        norm_kernel,
        out_shape=(
            jax.ShapeDtypeStruct((rows_dev, gain.shape[1]), jnp.float32),
            jax.ShapeDtypeStruct(kept.shape, jnp.bfloat16),
        ),
        in_specs=[IN_VMEM] * 3,
        out_specs=(IN_VMEM, IN_VMEM),
        compiler_params=pltpu.CompilerParams(
            vmem_limit_bytes=2 * MIB + 24 * kept.size
        ),
    )(kept, got, gain)


def stack_kernel(first, second, out):
    rows = first.shape[0]
    out[:rows] = first[...]
    out[rows:] = second[...]


def stack(first, second):
    shape = (2 * first.shape[0], first.shape[1])
    return pl.pallas_call(
        stack_kernel,
        out_shape=jax.ShapeDtypeStruct(shape, first.dtype),
        in_specs=[IN_VMEM] * 2,
        out_specs=IN_VMEM,
        compiler_params=pltpu.CompilerParams(vmem_limit_bytes=2 * MIB + 8 * first.size),
    )(first, second)


def strips(source, target, sems):
    count = sems.shape[0]
    run = source.shape[1] // count
    return [
        pltpu.make_async_copy(
            source.at[:, pl.ds(i * run, run)], target.at[:, pl.ds(i * run, run)], sems.at[i]
        )
        for i in range(count)
    ]


def expert_kernel(
    expert, first, second, gate, up, down, kept, sent, moe_in, gates, units, up_in, down_in, up_sems, down_sems
):
    width, inner = gate.shape
    half = kept.shape[0]
    ups, downs = strips(up, up_in, up_sems), strips(down, down_in, down_sems)
    for copy in ups:
        copy.start()
    moe_in[:half] = first[...]
    moe_in[half:] = second[...]
    rows = moe_in[:, :width]
    strip = inner // len(ups)
    tail = moe_in[:, width:].astype(jnp.float32)
    column = lax.broadcasted_iota(jnp.int32, tail.shape, 1)
    mine = (column == expert[0]) | (column == expert[0] + EXPERTS)
    weight = jnp.sum(jnp.where(mine, tail, 0.0), axis=1, keepdims=True)

    @pl.loop(0, len(ups))
    def _(i):
        columns = pl.ds(pl.multiple_of(i * strip, strip), strip)
        gate_act = jnp.dot(rows, gate[:, columns], preferred_element_type=jnp.float32)
        gates[:, columns] = jax.nn.silu(gate_act)

    later = iter(downs)
    for i, copy in enumerate(ups):
        copy.wait()
        next(later).start()
        columns = slice(i * strip, (i + 1) * strip)
        up_act = jnp.dot(rows, up_in[:, columns], preferred_element_type=jnp.float32)
        units[:, columns] = (gates[:, columns] * up_act).astype(units.dtype)
    strip = width // len(downs)
    for i, copy in enumerate(downs):
        copy.wait()
        for ahead in later:
            ahead.start()
            break
        columns = slice(i * strip, (i + 1) * strip)
        terms = weight * jnp.dot(
            units[...], down_in[:, columns], preferred_element_type=jnp.float32
        )
        kept[:, columns] = terms[:half]
        sent[:, columns] = terms[half:].astype(sent.dtype)


def run_expert(expert, first, second, gate, up, down):
    rows = 2 * first.shape[0]
    width, inner = gate.shape
    shape = (rows // 2, width)
    return pl.pallas_call(
        expert_kernel,
        out_shape=(
            jax.ShapeDtypeStruct(shape, jnp.float32),
            jax.ShapeDtypeStruct(shape, jnp.bfloat16),
        ),
        in_specs=[IN_SMEM] + [IN_VMEM] * 3 + [IN_HBM] * 2,
        out_specs=(IN_VMEM, IN_VMEM),
        scratch_shapes=[
            pltpu.VMEM((rows, first.shape[1]), jnp.bfloat16),
            pltpu.VMEM((rows, inner), jnp.float32),
            pltpu.VMEM((rows, inner), jnp.bfloat16),
            pltpu.VMEM(up.shape, up.dtype),
            pltpu.VMEM(down.shape, down.dtype),
            pltpu.SemaphoreType.DMA((4,)),
            pltpu.SemaphoreType.DMA((7,)),
        ],
        compiler_params=pltpu.CompilerParams(
            vmem_limit_bytes=4 * MIB + 4 * width * inner + 64 * rows * inner
        ),
    )(expert, first, second, in_vmem(gate), in_hbm(up), in_hbm(down))


def on_device(
    hidden,
    queries,
    latent_cache,
    cache_lengths,
    value_up,
    out_proj,
    norm_gain,
    expert_ids,
    gate_weights,
    gate_proj,
    up_proj,
    down_proj,
):
    rows_dev, width = hidden.shape
    ep_size = lax.axis_size("ep")
    me = lax.axis_index("ep")
    bits = ep_size.bit_length() - 1
    split_ways = ep_size // EXPERTS
    scatter_bits = min(2, bits)
    heads_dev, latent, _ = value_up.shape
    rows_in = ep_size * rows_dev

    experts_iota = lax.broadcasted_iota(jnp.int32, (1, 1, EXPERTS), 2)
    named = expert_ids[:, :, None] == experts_iota
    weight = jnp.sum(jnp.where(named, gate_weights[:, :, None], 0.0), axis=1)
    weight_top = weight.astype(jnp.bfloat16).astype(jnp.float32)
    weight_rest = (weight - weight_top).astype(jnp.bfloat16).astype(jnp.float32)
    tail = jnp.concatenate((weight_top, weight_rest), axis=1)
    tail = jnp.pad(tail, ((0, 0), (0, LANES - tail.shape[1])))

    order = relative_order(bits)
    gate, up, down = gate_proj[0], up_proj[0], down_proj[0]
    if heads_dev % 8 == 0:
        kept, sent, out_proj, value_up = attend(
            queries, latent_cache, cache_lengths, out_proj, value_up, order, me
        )
        run = ep_size >> 2
        got = exchange(sent, 0)
        kept, sent = deal((kept, got), 2, run)
        got = exchange(sent, 1)
        parts = deal((kept, got), run, 1)
        masks = order[:run]
        by_head = [parts[0]] + [trade(part, mask) for part, mask in zip(parts[1:], masks[1:])]
        held = [mask | x << 1 | core for mask in masks for x in range(2) for core in range(2)]
        row_of = jnp.array([held.index(s) * rows_dev + r for s in order for r in range(rows_dev)])
    else:
        out, _, out_proj, value_up = attend(
            queries, latent_cache, cache_lengths, out_proj, value_up, (), me
        )
        out = out.reshape(rows_dev, ep_size, heads_dev, latent).transpose(1, 0, 2, 3)
        by_head = [lax.all_to_all(out, "ep", split_axis=0, concat_axis=0, tiled=True)]
        by_head = [by_head[0].reshape(rows_in * heads_dev, latent)]
        row_of = (jnp.array(order) ^ me)[:, None] * rows_dev + jnp.arange(rows_dev)[None, :]
        row_of = row_of.reshape(-1)
    row_of = row_of.astype(jnp.int32)
    kept, sent = project(by_head, row_of[:, None], value_up, out_proj, hidden, tail)

    rows = rows_in // 2
    for bit in range(scatter_bits - 1):
        rows //= 2
        kept, sent = combine(halve_kernel, kept, exchange(sent, bit), rows)
    got = exchange(sent, scatter_bits - 1)
    for bit in range(scatter_bits, bits):
        shift = rows_dev << (bits - 1 - bit)
        kept, sent = combine(functools.partial(swap_kernel, shift), kept, got, rows)
        got = exchange(sent, bit)
    residual, moe_in = norm(kept, got, norm_gain[None, :], rows_dev)
    for bit in reversed(range(1, scatter_bits)):
        got = exchange(moe_in, bit)
        moe_in = stack(moe_in, got)
    if split_ways == 1:
        gate = load(gate, moe_in)
    other = exchange(moe_in, 0)

    expert = me % EXPERTS
    if split_ways == 1:
        kept, sent = run_expert(expert[None], moe_in, other, gate, up, down)
    else:
        moe_in = jnp.concatenate((moe_in, other), axis=0)
        tail_in = moe_in[:, width:].astype(jnp.float32)
        column = lax.broadcasted_iota(jnp.int32, tail_in.shape, 1)
        mine = (column == expert) | (column == expert + EXPERTS)
        row_weight = jnp.sum(jnp.where(mine, tail_in, 0.0), axis=1, keepdims=True)
        slice_width = width // split_ways
        start = (me // EXPERTS) * slice_width
        part_in = lax.dynamic_slice_in_dim(moe_in, start, slice_width, axis=1)
        gate_act = jnp.dot(part_in, gate, preferred_element_type=jnp.float32)
        up_act = jnp.dot(part_in, up, preferred_element_type=jnp.float32)
        to_one = (row_of[:, None] == jnp.arange(rows_in)[None, :]).astype(jnp.float32)
        stacked = jnp.stack((gate_act, up_act)).astype(jnp.bfloat16).astype(jnp.float32)
        stacked = jnp.einsum("sr,asf->arf", to_one, stacked)
        for bit in range(EXPERTS.bit_length() - 1, bits):
            stacked = stacked + exchange(stacked.astype(jnp.bfloat16), bit).astype(jnp.float32)
        stacked = jnp.einsum("sr,arf->asf", to_one, stacked, precision=lax.Precision.HIGHEST)
        units = (jax.nn.silu(stacked[0]) * stacked[1]).astype(jnp.bfloat16)
        weighted = jnp.dot(units, down, preferred_element_type=jnp.float32) * row_weight
        spread = jnp.zeros((rows_in, width), jnp.float32)
        spread = lax.dynamic_update_slice_in_dim(spread, weighted, start, axis=1)
        kept, sent = spread[: rows_in // 2], spread[rows_in // 2 :].astype(jnp.bfloat16)
    rows = rows_in // 2
    for bit in range(bits - 1):
        rows //= 2
        kept, sent = combine(halve_kernel, kept, exchange(sent, bit), rows)
    routed = kept + exchange(sent, bits - 1).astype(jnp.float32)
    return (residual + routed).astype(jnp.bfloat16)


def solution(mesh):
    return jax.shard_map(
        on_device,
        mesh=mesh,
        in_specs=(
            P(("groups", "ep"), None),
            P(("groups", "ep"), None, None),
            P(("groups", "ep"), None, None),
            P(("groups", "ep")),
            P("ep", None, None),
            P("ep", None),
            P(),
            P(("groups", "ep"), None),
            P(("groups", "ep"), None),
            P("ep", None, None),
            P("ep", None, None),
            P("ep", None, None),
        ),
        out_specs=P(("groups", "ep"), None),
        check_vma=False,
    )
```

time: 100 us -> 89.7 us (0.90)
  matrix products: 36.8 us -> 0 us
  Pallas kernels: 0 us -> 29 us
  starting transfers between devices: 11 us -> 14.5 us
  waiting for transfers between devices: 46.7 us -> 43.4 us
  other arithmetic: 4.11 us -> 0.82 us
    dot_general x7 -> x0, matrix products: 36.8 us -> none  [the longest x1 14.6 us: on_device(): jnp.dot(units, down_proj[0], preferred_element_type=jnp.float32)]
    pallas_call x0 -> x14, Pallas kernels: none -> 29 us  [the longest x1 11.1 us: run_expert(): pl.pallas_call(expert_kernel, out_shape=(jax.ShapeDtypeStruct(shape, jnp....]
    ppermute x10 -> x15, starting transfers between devices: 3.59 us -> 14.5 us  [trade(): lax.ppermute(value, 'ep', [(i, i ^ mask) for i in range(lax.axis_size('ep...]
    all_to_all x1 -> x0, waiting for transfers between devices: 9.79 us -> none  [on_device(): lax.all_to_all(outgoing, 'ep', split_axis=0, concat_axis=0, tiled=True)]
    all_to_all x1 -> x0, starting transfers between devices: 7.36 us -> none  [on_device(): lax.all_to_all(outgoing, 'ep', split_axis=0, concat_axis=0, tiled=True)]
    ppermute x10 -> x15, waiting for transfers between devices: 36.9 us -> 43.4 us  [trade(): lax.ppermute(value, 'ep', [(i, i ^ mask) for i in range(lax.axis_size('ep...]
    unnamed x11 -> x14, local copies, waits for them, and re-layouts: 0.13 us -> 1.66 us
  transfers between devices with their start and end apart: 11 -> 15, of which waited for: 11 -> 14; matrix products, arithmetic and copies ran while one was open for 1% -> 0% of each run, Pallas kernels for 0% -> 6%
where the time goes in v1:
time: 89.7 us; the launch traced here: 89.6 us
  waiting for transfers between devices  43.4 us (48%)
  Pallas kernels  29 us (32%)
  starting transfers between devices  14.5 us (16%)
  local copies, waits for them, and re-layouts  1.66 us (2%)
    ppermute x15, waiting for transfers between devices, trade(): lax.ppermute(value, 'ep', [(i, i ^ mask) for i in range(lax.axis_size('ep...  43.4 us
    ppermute x15, starting transfers between devices, trade(): lax.ppermute(value, 'ep', [(i, i ^ mask) for i in range(lax.axis_size('ep...  14.5 us
    pallas_call x1, Pallas kernels, run_expert(): pl.pallas_call(expert_kernel, out_shape=(jax.ShapeDtypeStruct(shape, jnp....  11.1 us
    pallas_call x1, Pallas kernels, attend(): pl.pallas_call(functools.partial(attend_kernel, order), out_shape=(VMEM_A...  7.51 us
    pallas_call x1, Pallas kernels, load(): pl.pallas_call(load_kernel, out_shape=VMEM_ARRAY(source.shape, source.dty...  5.28 us
    pallas_call x1, Pallas kernels, project(): pl.pallas_call(functools.partial(project_kernel, 512, len(by_head)), out_...  4.64 us
  transfers between devices with their start and end apart: 15, of which 14 were waited for; matrix products, arithmetic and copies ran while one was open for 0% of the time, Pallas kernels for 6%

profile of v1, /device:TPU:0, one launch (start us, length us, event | category | flops | bytes accessed | tf_op | source)
XLA Modules:
  0.0 89.6 jit_solution(13114267556841909390)
XLA Ops:
  0.0 0.0 copy-start.3
  0.0 0.0 copy-start.5
  0.0 0.0 copy-start
  0.0 1.0 %copy-done = bf16[2,128,576]{1,2,0:T(8,128)(2,1)S(1)} copy-done((bf16[2,128,576]{1,2,0:T(8,128)(2,1)S(1)}, bf16[2,128,576]{1,2,0:T(8,128)(2,1)}, u32[]{:S(2)}) %copy-start) | copy-done | bytes 294936
  1.0 0.0 copy-start.4
  1.0 0.7 copy-done.4
  1.6 0.0 copy-start.6
  1.7 0.0 copy-start.1
  1.7 0.0 copy-start.2
  1.7 7.5 %shard_map.127 = (bf16[8,16,512]{2,1,0:T(8,128)(2,1)S(1)}, bf16[8,16,512]{2,1,0:T(8,128)(2,1)S(1)}, bf16[1024,7168]{1,0:T(8,128)(2,1)S(1)}, bf16[8,512,128]{2,1,0:T(8,128)(2,1)S(1)}) custom-call(s32[2]{0:T(128)S(1)} %copy-done.4, s32[1]{0:T(128)} %bitcast.me, bf16[2,576,128]{2,1,0:T(8,128)(2,1)S(1)} %bitcast.8, bf16[2,576,2048]{2,1,0:T(8,128)(2,1)} %bitcast.13, ...), custom_call_target="tpu_custom_call" | custom-call | tf_op jit(solution)/shard_map/pallas_call | solution.py:125
  9.2 0.5 collective-permute-start
  9.7 0.0 copy-done.5
  9.7 0.0 copy-done.6
  9.7 0.1 select_reduce_fusion
  9.8 0.9 collective-permute-done.refs_1_
  10.7 2.9 %collective-permute-start.1 = (bf16[8,16,512]{2,1,0:T(8,128)(2,1)S(1)}, bf16[8,16,512]{2,1,0:T(8,128)(2,1)S(1)}, u32[]{:S(2)}, u32[]{:S(2)}) collective-permute-start(bf16[8,16,512]{2,1,0:T(8,128)(2,1)S(1)} %get-tuple-element.36), channel_id=1, source_target_pairs={{0,2},{1,3},{2,0},{3,1},{4,6},{5,7},{6,4},{7,5},{8,10},{9,11},{10,... | collective-permute-start | bytes 393224 | tf_op jit(solution)/shard_map/ppermute | solution.py:22
  13.6 3.8 %collective-permute-done.1.refs_1_ = bf16[8,16,512]{2,1,0:T(8,128)(2,1)S(1)} collective-permute-done((bf16[8,16,512]{2,1,0:T(8,128)(2,1)S(1)}, bf16[8,16,512]{2,1,0:T(8,128)(2,1)S(1)}, u32[]{:S(2)}, u32[]{:S(2)}) %collective-permute-start.1) | collective-permute-done | bytes 131104 | tf_op jit(solution)/shard_map/ppermute | solution.py:22
  17.4 2.9 %collective-permute-start.2 = (bf16[4,16,512]{2,1,0:T(8,128)(2,1)S(1)}, bf16[4,16,512]{2,1,0:T(8,128)(2,1)S(1)}, u32[]{:S(2)}, u32[]{:S(2)}) collective-permute-start(bf16[4,16,512]{2,1,0:T(8,128)(2,1)S(1)} %get-tuple-element.38), channel_id=1, source_target_pairs={{0,8},{1,9},{2,10},{3,11},{4,12},{5,13},{6,14},{7,15},{8,0},{9,1},... | collective-permute-start | bytes 196616 | tf_op jit(solution)/shard_map/ppermute | solution.py:22
  20.3 1.6 %collective-permute-start.3 = (bf16[4,16,512]{2,1,0:T(8,128)(2,1)S(1)}, bf16[4,16,512]{2,1,0:T(8,128)(2,1)S(1)}, u32[]{:S(2)}, u32[]{:S(2)}) collective-permute-start(bf16[4,16,512]{2,1,0:T(8,128)(2,1)S(1)} %get-tuple-element.39), channel_id=1, source_target_pairs={{0,4},{1,5},{2,6},{3,7},{4,0},{5,1},{6,2},{7,3},{8,12},{9,13},{10,... | collective-permute-start | bytes 196616 | tf_op jit(solution)/shard_map/ppermute | solution.py:22
  21.9 0.0 collective-permute-start.4
  21.9 0.1 select_maximum_fusion.refs_8_
  22.0 1.1 %collective-permute-done.2.refs_1_ = bf16[4,16,512]{2,1,0:T(8,128)(2,1)S(1)} collective-permute-done((bf16[4,16,512]{2,1,0:T(8,128)(2,1)S(1)}, bf16[4,16,512]{2,1,0:T(8,128)(2,1)S(1)}, u32[]{:S(2)}, u32[]{:S(2)}) %collective-permute-start.2) | collective-permute-done | bytes 65568 | tf_op jit(solution)/shard_map/ppermute | solution.py:22
  23.1 1.5 %collective-permute-done.3.refs_2_ = bf16[4,16,512]{2,1,0:T(8,128)(2,1)S(1)} collective-permute-done((bf16[4,16,512]{2,1,0:T(8,128)(2,1)S(1)}, bf16[4,16,512]{2,1,0:T(8,128)(2,1)S(1)}, u32[]{:S(2)}, u32[]{:S(2)}) %collective-permute-start.3) | collective-permute-done | bytes 65568 | tf_op jit(solution)/shard_map/ppermute | solution.py:22
  24.6 3.4 %collective-permute-done.4.refs_3_ = bf16[4,16,512]{2,1,0:T(8,128)(2,1)S(1)} collective-permute-done((bf16[4,16,512]{2,1,0:T(8,128)(2,1)S(1)}, bf16[4,16,512]{2,1,0:T(8,128)(2,1)S(1)}, u32[]{:S(2)}, u32[]{:S(2)}) %collective-permute-start.4) | collective-permute-done | bytes 65568 | tf_op jit(solution)/shard_map/ppermute | solution.py:22
  28.0 0.0 copy-done.3
  28.0 0.0 copy-done.1
  28.0 4.6 %shard_map.130 = (f32[16,7296]{1,0:T(8,128)S(1)}, bf16[16,7296]{1,0:T(8,128)(2,1)S(1)}) custom-call(bf16[4,16,512]{2,1,0:T(8,128)(2,1)S(1)} %get-tuple-element.37.refs_0_, bf16[4,16,512]{2,1,0:T(8,128)(2,1)S(1)} %collective-permute-done.2.refs_1_, bf16[4,16,512]{2,1,0:T(8,128)(2,1)S(1)} %collective-permute-done.3.refs_2_, ...), custom_call_target="tpu_custom_call" | custom-call | tf_op jit(solution)/shard_map/pallas_call | solution.py:218
  32.6 0.0 collective-permute-start.5
  32.6 1.5 %collective-permute-done.5.got = bf16[16,7296]{1,0:T(8,128)(2,1)S(1)} collective-permute-done((bf16[16,7296]{1,0:T(8,128)(2,1)S(1)}, bf16[16,7296]{1,0:T(8,128)(2,1)S(1)}, u32[]{:S(2)}, u32[]{:S(2)}) %collective-permute-start.5) | collective-permute-done | bytes 233504 | tf_op jit(solution)/shard_map/ppermute | solution.py:22
  34.2 1.6 %collective-permute-start.6 = (bf16[8,7296]{1,0:T(8,128)(2,1)S(1)}, bf16[8,7296]{1,0:T(8,128)(2,1)S(1)}, u32[]{:S(2)}, u32[]{:S(2)}) collective-permute-start(bf16[8,7296]{1,0:T(8,128)(2,1)S(1)} %get-tuple-element.46), channel_id=1, source_target_pairs={{0,2},{1,3},{2,0},{3,1},{4,6},{5,7},{6,4},{7,5},{8,10},{9,11},{10,... | collective-permute-start | bytes 350216 | tf_op jit(solution)/shard_map/ppermute | solution.py:22
  35.7 3.7 %collective-permute-done.6.got = bf16[8,7296]{1,0:T(8,128)(2,1)S(1)} collective-permute-done((bf16[8,7296]{1,0:T(8,128)(2,1)S(1)}, bf16[8,7296]{1,0:T(8,128)(2,1)S(1)}, u32[]{:S(2)}, u32[]{:S(2)}) %collective-permute-start.6) | collective-permute-done | bytes 116768 | tf_op jit(solution)/shard_map/ppermute | solution.py:22
  39.5 0.1 collective-permute-start.7
  39.6 4.8 %collective-permute-done.7.got = bf16[8,7296]{1,0:T(8,128)(2,1)S(1)} collective-permute-done((bf16[8,7296]{1,0:T(8,128)(2,1)S(1)}, bf16[8,7296]{1,0:T(8,128)(2,1)S(1)}, u32[]{:S(2)}, u32[]{:S(2)}) %collective-permute-start.7) | collective-permute-done | bytes 116768 | tf_op jit(solution)/shard_map/ppermute | solution.py:22
  44.4 0.1 shard_map.133
  44.5 0.9 collective-permute-start.8
  45.3 5.6 %collective-permute-done.8.got = bf16[8,7296]{1,0:T(8,128)(2,1)S(1)} collective-permute-done((bf16[8,7296]{1,0:T(8,128)(2,1)S(1)}, bf16[8,7296]{1,0:T(8,128)(2,1)S(1)}, u32[]{:S(2)}, u32[]{:S(2)}) %collective-permute-start.8) | collective-permute-done | bytes 116768 | tf_op jit(solution)/shard_map/ppermute | solution.py:22
  50.9 0.0 copy-done.2
  50.9 0.2 shard_map.134
  51.1 1.6 %collective-permute-start.9 = (bf16[8,7296]{1,0:T(8,128)(2,1)S(1)}, bf16[8,7296]{1,0:T(8,128)(2,1)S(1)}, u32[]{:S(2)}, u32[]{:S(2)}) collective-permute-start(bf16[8,7296]{1,0:T(8,128)(2,1)S(1)} %get-tuple-element.52.first), channel_id=1, source_target_pairs={{0,2},{1,3},{2,0},{3,1},{4,6},{5,7},{6,4},{7,5},{8,10},{9,11},{10,... | collective-permute-start | bytes 350216 | tf_op jit(solution)/shard_map/ppermute | solution.py:22
  52.7 3.3 %collective-permute-done.9.second = bf16[8,7296]{1,0:T(8,128)(2,1)S(1)} collective-permute-done((bf16[8,7296]{1,0:T(8,128)(2,1)S(1)}, bf16[8,7296]{1,0:T(8,128)(2,1)S(1)}, u32[]{:S(2)}, u32[]{:S(2)}) %collective-permute-start.9) | collective-permute-done | bytes 116768 | tf_op jit(solution)/shard_map/ppermute | solution.py:22
  56.0 0.1 collective-permute-start.10
  56.1 5.3 %shard_map.136.gate = bf16[7168,1024]{1,0:T(8,128)(2,1)S(1)} custom-call(bf16[7168,1024]{1,0:T(8,128)(2,1)} %bitcast.10, bf16[16,7296]{1,0:T(8,128)(2,1)S(1)} %shard_map.135.after.first), custom_call_target="tpu_custom_call" | custom-call | bytes 29360128 | tf_op jit(solution)/shard_map/pallas_call | solution.py:65
  61.4 0.0 collective-permute-done.10.second
  61.4 11.1 %shard_map.137 = (f32[16,7168]{1,0:T(8,128)S(1)}, bf16[16,7168]{1,0:T(8,128)(2,1)S(1)}) custom-call(s32[1]{0:T(128)} %bitcast.4.expert, bf16[16,7296]{1,0:T(8,128)(2,1)S(1)} %shard_map.135.after.first, bf16[16,7296]{1,0:T(8,128)(2,1)S(1)} %collective-permute-done.10.second, bf16[7168,1024]{1,0:T(8,128)(2,1)S(1)} %shard_map.136.gate, ...), custom_call_target="tpu_custom_call" | custom-call | tf_op jit(solution)/shard_map/pallas_call | solution.py:370
  72.5 0.5 collective-permute-start.11
  73.1 1.1 %collective-permute-done.11.got = bf16[16,7168]{1,0:T(8,128)(2,1)S(1)} collective-permute-done((bf16[16,7168]{1,0:T(8,128)(2,1)S(1)}, bf16[16,7168]{1,0:T(8,128)(2,1)S(1)}, u32[]{:S(2)}, u32[]{:S(2)}) %collective-permute-start.11) | collective-permute-done | bytes 229408 | tf_op jit(solution)/shard_map/ppermute | solution.py:22
  74.2 1.6 %collective-permute-start.12 = (bf16[8,7168]{1,0:T(8,128)(2,1)S(1)}, bf16[8,7168]{1,0:T(8,128)(2,1)S(1)}, u32[]{:S(2)}, u32[]{:S(2)}) collective-permute-start(bf16[8,7168]{1,0:T(8,128)(2,1)S(1)} %get-tuple-element.56), channel_id=1, source_target_pairs={{0,2},{1,3},{2,0},{3,1},{4,6},{5,7},{6,4},{7,5},{8,10},{9,11},{10,... | collective-permute-start | bytes 344072 | tf_op jit(solution)/shard_map/ppermute | solution.py:22
  75.8 3.9 %collective-permute-done.12.got = bf16[8,7168]{1,0:T(8,128)(2,1)S(1)} collective-permute-done((bf16[8,7168]{1,0:T(8,128)(2,1)S(1)}, bf16[8,7168]{1,0:T(8,128)(2,1)S(1)}, u32[]{:S(2)}, u32[]{:S(2)}) %collective-permute-start.12) | collective-permute-done | bytes 114720 | tf_op jit(solution)/shard_map/ppermute | solution.py:22
  79.8 0.1 collective-permute-start.13
  79.9 4.2 %collective-permute-done.13.got = bf16[4,7168]{1,0:T(4,128)(2,1)S(1)} collective-permute-done((bf16[4,7168]{1,0:T(4,128)(2,1)S(1)}, bf16[4,7168]{1,0:T(4,128)(2,1)S(1)}, u32[]{:S(2)}, u32[]{:S(2)}) %collective-permute-start.13) | collective-permute-done | bytes 57376 | tf_op jit(solution)/shard_map/ppermute | solution.py:22
  84.1 0.3 collective-permute-start.14
  84.3 4.6 %collective-permute-done.14 = bf16[2,7168]{1,0:T(2,128)(2,1)S(1)} collective-permute-done((bf16[2,7168]{1,0:T(2,128)(2,1)S(1)}, bf16[2,7168]{1,0:T(2,128)(2,1)S(1)}, u32[]{:S(2)}, u32[]{:S(2)}) %collective-permute-start.14) | collective-permute-done | bytes 28704 | tf_op jit(solution)/shard_map/ppermute | solution.py:22
  88.9 0.7 add_convert_fusion
  (9 shorter events, 0.3 us)
Async XLA Ops:
  0.0 28.0 %copy-start.3 = (s32[32,1]{1,0:T(8,128)S(1)}, s32[32,1]{1,0:T(8,128)}, u32[]{:S(2)}) copy-start(s32[32,1]{1,0:T(8,128)} %constant.36.refs_4_) | copy-start | bytes 388
  0.0 9.7 %copy-start.5 = (f32[2,8]{1,0:T(2,128)S(1)}, f32[2,8]{1,0:T(2,128)}, u32[]{:S(2)}) copy-start(f32[2,8]{1,0:T(2,128)} %param.21) | copy-start | bytes 196
  0.0 1.0 %copy-start = (bf16[2,128,576]{1,2,0:T(8,128)(2,1)S(1)}, bf16[2,128,576]{1,2,0:T(8,128)(2,1)}, u32[]{:S(2)}) copy-start(bf16[2,128,576]{1,2,0:T(8,128)(2,1)} %param.14) | copy-start | bytes 884740
  1.0 0.7 copy-start.4
  1.6 8.0 %copy-start.6 = (s32[2,8]{1,0:T(2,128)S(1)}, s32[2,8]{1,0:T(2,128)}, u32[]{:S(2)}) copy-start(s32[2,8]{1,0:T(2,128)} %param.20) | copy-start | bytes 196
  1.7 26.3 %copy-start.1 = (bf16[2,7168]{1,0:T(2,128)(2,1)S(1)}, bf16[2,7168]{1,0:T(2,128)(2,1)}, u32[]{:S(2)}) copy-start(bf16[2,7168]{1,0:T(2,128)(2,1)} %refs_7_.1) | copy-start | bytes 86020
  1.7 49.3 %copy-start.2 = (f32[7168]{0:T(1024)S(1)}, f32[7168]{0:T(1024)}, u32[]{:S(2)}) copy-start(f32[7168]{0:T(1024)} %param.19) | copy-start | bytes 86020
  9.2 1.5 %collective-permute-start = (bf16[8,16,512]{2,1,0:T(8,128)(2,1)S(1)}, bf16[8,16,512]{2,1,0:T(8,128)(2,1)S(1)}, u32[]{:S(2)}, u32[]{:S(2)}) collective-permute-start(bf16[8,16,512]{2,1,0:T(8,128)(2,1)S(1)} %get-tuple-element.34), channel_id=1, source_target_pairs={{0,1},{1,0},{2,3},{3,2},{4,5},{5,4},{6,7},{7,6},{8,9},{9,8},{10,11... | collective-permute-start | bytes 393224 | tf_op jit(solution)/shard_map/ppermute | solution.py:22
  10.7 6.7 %collective-permute-start.1 = (bf16[8,16,512]{2,1,0:T(8,128)(2,1)S(1)}, bf16[8,16,512]{2,1,0:T(8,128)(2,1)S(1)}, u32[]{:S(2)}, u32[]{:S(2)}) collective-permute-start(bf16[8,16,512]{2,1,0:T(8,128)(2,1)S(1)} %get-tuple-element.36), channel_id=1, source_target_pairs={{0,2},{1,3},{2,0},{3,1},{4,6},{5,7},{6,4},{7,5},{8,10},{9,11},{10,... | collective-permute-start | bytes 393224 | tf_op jit(solution)/shard_map/ppermute | solution.py:22
  17.4 5.7 %collective-permute-start.2 = (bf16[4,16,512]{2,1,0:T(8,128)(2,1)S(1)}, bf16[4,16,512]{2,1,0:T(8,128)(2,1)S(1)}, u32[]{:S(2)}, u32[]{:S(2)}) collective-permute-start(bf16[4,16,512]{2,1,0:T(8,128)(2,1)S(1)} %get-tuple-element.38), channel_id=1, source_target_pairs={{0,8},{1,9},{2,10},{3,11},{4,12},{5,13},{6,14},{7,15},{8,0},{9,1},... | collective-permute-start | bytes 196616 | tf_op jit(solution)/shard_map/ppermute | solution.py:22
  20.3 4.3 %collective-permute-start.3 = (bf16[4,16,512]{2,1,0:T(8,128)(2,1)S(1)}, bf16[4,16,512]{2,1,0:T(8,128)(2,1)S(1)}, u32[]{:S(2)}, u32[]{:S(2)}) collective-permute-start(bf16[4,16,512]{2,1,0:T(8,128)(2,1)S(1)} %get-tuple-element.39), channel_id=1, source_target_pairs={{0,4},{1,5},{2,6},{3,7},{4,0},{5,1},{6,2},{7,3},{8,12},{9,13},{10,... | collective-permute-start | bytes 196616 | tf_op jit(solution)/shard_map/ppermute | solution.py:22
  21.9 6.1 %collective-permute-start.4 = (bf16[4,16,512]{2,1,0:T(8,128)(2,1)S(1)}, bf16[4,16,512]{2,1,0:T(8,128)(2,1)S(1)}, u32[]{:S(2)}, u32[]{:S(2)}) collective-permute-start(bf16[4,16,512]{2,1,0:T(8,128)(2,1)S(1)} %get-tuple-element.40), channel_id=1, source_target_pairs={{0,12},{1,13},{2,14},{3,15},{4,8},{5,9},{6,10},{7,11},{8,4},{9,5},... | collective-permute-start | bytes 196616 | tf_op jit(solution)/shard_map/ppermute | solution.py:22
  32.6 1.5 %collective-permute-start.5 = (bf16[16,7296]{1,0:T(8,128)(2,1)S(1)}, bf16[16,7296]{1,0:T(8,128)(2,1)S(1)}, u32[]{:S(2)}, u32[]{:S(2)}) collective-permute-start(bf16[16,7296]{1,0:T(8,128)(2,1)S(1)} %get-tuple-element.44), channel_id=1, source_target_pairs={{0,1},{1,0},{2,3},{3,2},{4,5},{5,4},{6,7},{7,6},{8,9},{9,8},{10,11... | collective-permute-start | bytes 700424 | tf_op jit(solution)/shard_map/ppermute | solution.py:22
  34.2 5.3 %collective-permute-start.6 = (bf16[8,7296]{1,0:T(8,128)(2,1)S(1)}, bf16[8,7296]{1,0:T(8,128)(2,1)S(1)}, u32[]{:S(2)}, u32[]{:S(2)}) collective-permute-start(bf16[8,7296]{1,0:T(8,128)(2,1)S(1)} %get-tuple-element.46), channel_id=1, source_target_pairs={{0,2},{1,3},{2,0},{3,1},{4,6},{5,7},{6,4},{7,5},{8,10},{9,11},{10,... | collective-permute-start | bytes 350216 | tf_op jit(solution)/shard_map/ppermute | solution.py:22
  39.5 4.9 %collective-permute-start.7 = (bf16[8,7296]{1,0:T(8,128)(2,1)S(1)}, bf16[8,7296]{1,0:T(8,128)(2,1)S(1)}, u32[]{:S(2)}, u32[]{:S(2)}) collective-permute-start(bf16[8,7296]{1,0:T(8,128)(2,1)S(1)} %get-tuple-element.48), channel_id=1, source_target_pairs={{0,4},{1,5},{2,6},{3,7},{4,0},{5,1},{6,2},{7,3},{8,12},{9,13},{10,... | collective-permute-start | bytes 350216 | tf_op jit(solution)/shard_map/ppermute | solution.py:22
  44.5 6.5 %collective-permute-start.8 = (bf16[8,7296]{1,0:T(8,128)(2,1)S(1)}, bf16[8,7296]{1,0:T(8,128)(2,1)S(1)}, u32[]{:S(2)}, u32[]{:S(2)}) collective-permute-start(bf16[8,7296]{1,0:T(8,128)(2,1)S(1)} %get-tuple-element.50), channel_id=1, source_target_pairs={{0,8},{1,9},{2,10},{3,11},{4,12},{5,13},{6,14},{7,15},{8,0},{9,1},... | collective-permute-start | bytes 350216 | tf_op jit(solution)/shard_map/ppermute | solution.py:22
  51.1 4.9 %collective-permute-start.9 = (bf16[8,7296]{1,0:T(8,128)(2,1)S(1)}, bf16[8,7296]{1,0:T(8,128)(2,1)S(1)}, u32[]{:S(2)}, u32[]{:S(2)}) collective-permute-start(bf16[8,7296]{1,0:T(8,128)(2,1)S(1)} %get-tuple-element.52.first), channel_id=1, source_target_pairs={{0,2},{1,3},{2,0},{3,1},{4,6},{5,7},{6,4},{7,5},{8,10},{9,11},{10,... | collective-permute-start | bytes 350216 | tf_op jit(solution)/shard_map/ppermute | solution.py:22
  56.0 5.4 %collective-permute-start.10 = (bf16[16,7296]{1,0:T(8,128)(2,1)S(1)}, bf16[16,7296]{1,0:T(8,128)(2,1)S(1)}, u32[]{:S(2)}, u32[]{:S(2)}) collective-permute-start(bf16[16,7296]{1,0:T(8,128)(2,1)S(1)} %shard_map.135.after.first), channel_id=1, source_target_pairs={{0,1},{1,0},{2,3},{3,2},{4,5},{5,4},{6,7},{7,6},{8,9},{9,8},{10,11... | collective-permute-start | bytes 700424 | tf_op jit(solution)/shard_map/ppermute | solution.py:22
  72.5 1.7 %collective-permute-start.11 = (bf16[16,7168]{1,0:T(8,128)(2,1)S(1)}, bf16[16,7168]{1,0:T(8,128)(2,1)S(1)}, u32[]{:S(2)}, u32[]{:S(2)}) collective-permute-start(bf16[16,7168]{1,0:T(8,128)(2,1)S(1)} %get-tuple-element.54), channel_id=1, source_target_pairs={{0,1},{1,0},{2,3},{3,2},{4,5},{5,4},{6,7},{7,6},{8,9},{9,8},{10,11... | collective-permute-start | bytes 688136 | tf_op jit(solution)/shard_map/ppermute | solution.py:22
  74.2 5.5 %collective-permute-start.12 = (bf16[8,7168]{1,0:T(8,128)(2,1)S(1)}, bf16[8,7168]{1,0:T(8,128)(2,1)S(1)}, u32[]{:S(2)}, u32[]{:S(2)}) collective-permute-start(bf16[8,7168]{1,0:T(8,128)(2,1)S(1)} %get-tuple-element.56), channel_id=1, source_target_pairs={{0,2},{1,3},{2,0},{3,1},{4,6},{5,7},{6,4},{7,5},{8,10},{9,11},{10,... | collective-permute-start | bytes 344072 | tf_op jit(solution)/shard_map/ppermute | solution.py:22
  79.8 4.2 %collective-permute-start.13 = (bf16[4,7168]{1,0:T(4,128)(2,1)S(1)}, bf16[4,7168]{1,0:T(4,128)(2,1)S(1)}, u32[]{:S(2)}, u32[]{:S(2)}) collective-permute-start(bf16[4,7168]{1,0:T(4,128)(2,1)S(1)} %get-tuple-element.58), channel_id=1, source_target_pairs={{0,4},{1,5},{2,6},{3,7},{4,0},{5,1},{6,2},{7,3},{8,12},{9,13},{10,... | collective-permute-start | bytes 172040 | tf_op jit(solution)/shard_map/ppermute | solution.py:22
  84.1 4.8 %collective-permute-start.14 = (bf16[2,7168]{1,0:T(2,128)(2,1)S(1)}, bf16[2,7168]{1,0:T(2,128)(2,1)S(1)}, u32[]{:S(2)}, u32[]{:S(2)}) collective-permute-start(bf16[2,7168]{1,0:T(2,128)(2,1)S(1)} %get-tuple-element.60), channel_id=1, source_target_pairs={{0,8},{1,9},{2,10},{3,11},{4,12},{5,13},{6,14},{7,15},{8,0},{9,1},... | collective-permute-start | bytes 86024 | tf_op jit(solution)/shard_map/ppermute | solution.py:22

commit v2 on v1

--- a/solution.py
+++ b/solution.py
@@ -30,6 +30,7 @@
 MIB = 1 << 20
 IN_VMEM = pl.BlockSpec(memory_space=pltpu.VMEM)
 IN_SMEM = pl.BlockSpec(memory_space=pltpu.SMEM)
+ANYWHERE = pl.BlockSpec(memory_space=pl.ANY)
 IN_HBM = pl.BlockSpec(memory_space=pltpu.HBM)
 VMEM_ARRAY = pltpu.VMEM
 
@@ -53,39 +54,69 @@
     ]
 
 
-def load_kernel(source, after, target, sems):
-    copies = pieces(source, target, sems, 0)
+def load_kernel(first, source, after, target, done, sems):
+    done[...] = jnp.zeros_like(done)
+    copies = pieces(source.at[pl.ds(first, target.shape[0])], target, sems, 0)
     for copy in copies:
         copy.start()
     for copy in copies:
         copy.wait()
 
 
-def load(source, after):
+def load(source, after, part=0, parts=1):
+    rows = source.shape[0] // parts
     return pl.pallas_call(
-        load_kernel,
-        out_shape=VMEM_ARRAY(source.shape, source.dtype),
+        functools.partial(load_kernel, part * rows),
+        out_shape=(
+            VMEM_ARRAY((rows, source.shape[1]), source.dtype),
+            VMEM_ARRAY((8, LANES), jnp.float32),
+        ),
         in_specs=[IN_HBM, IN_VMEM],
-        out_specs=IN_VMEM,
+        out_specs=(IN_VMEM, IN_VMEM),
         scratch_shapes=[pltpu.SemaphoreType.DMA((4,))],
         compiler_params=pltpu.CompilerParams(vmem_limit_bytes=MIB),
         cost_estimate=pl.CostEstimate(
-            flops=0, bytes_accessed=2 * source.size * source.dtype.itemsize, transcendentals=0
+            flops=0,
+            bytes_accessed=2 * rows * source.shape[1] * source.dtype.itemsize,
+            transcendentals=0,
         ),
     )(in_hbm(source), in_vmem(after))
 
 
+def pass_on(kernel, ins, outs, *refs):
+    more = len(refs) - ins - outs
+    kernel(*refs[:ins], *refs[ins + more // 2 : ins + more // 2 + outs])
+
+
+def small_call(kernel, operands, shapes, carried, limit):
+    ins, outs = len(operands), len(shapes)
+    results = pl.pallas_call(
+        functools.partial(pass_on, kernel, ins, outs),
+        out_shape=tuple(shapes) + tuple(VMEM_ARRAY(c.shape, c.dtype) for c in carried),
+        in_specs=[IN_VMEM] * ins + [ANYWHERE] * len(carried),
+        out_specs=(IN_VMEM,) * outs + (ANYWHERE,) * len(carried),
+        input_output_aliases={ins + i: outs + i for i in range(len(carried))},
+        compiler_params=pltpu.CompilerParams(vmem_limit_bytes=limit),
+    )(*operands, *[in_vmem(c) for c in carried])
+    return results[:outs], tuple(results[outs:])
+
+
 def attend_kernel(
-    order, lengths, me, queries, cache, proj, value_up, kept, sent, proj_in, value_in, held, wide, sems
+    order, lengths_hbm, me, queries_hbm, cache, value_up, kept, sent, value_in, lengths, queries, held, wide, sems
 ):
     rows_dev, _, heads = queries.shape
     context = cache.shape[2]
     latent = wide.shape[-1]
     caches = [pltpu.make_async_copy(cache.at[r], held.at[r], sems.at[r]) for r in range(rows_dev)]
-    weights = [pltpu.make_async_copy(value_up, value_in, sems.at[rows_dev])]
-    weights += pieces(proj, proj_in, sems, rows_dev + 1)
-    for copy in caches + weights:
+    first = [
+        pltpu.make_async_copy(lengths_hbm, lengths, sems.at[rows_dev]),
+        pltpu.make_async_copy(queries_hbm, queries, sems.at[rows_dev + 1]),
+    ]
+    weights = pltpu.make_async_copy(value_up, value_in, sems.at[rows_dev + 2])
+    for copy in first + caches + [weights]:
         copy.start()
+    for copy in first:
+        copy.wait()
     for r in range(rows_dev):
         caches[r].wait()
         scores = score_scale * lax.dot_general(
@@ -111,11 +142,10 @@
     for p, s in enumerate(order):
         target = (kept, sent)[p // half]
         target[p % half] = wide[me[0] ^ s].astype(target.dtype)
-    for copy in weights:
-        copy.wait()
-
-
-def attend(queries, latent_cache, cache_lengths, out_proj, value_up, order, me):
+    weights.wait()
+
+
+def attend(queries, latent_cache, cache_lengths, value_up, order, me):
     rows_dev, heads, key_width = queries.shape
     context = latent_cache.shape[1]
     heads_dev, latent, _ = value_up.shape
@@ -127,23 +157,23 @@
         out_shape=(
             VMEM_ARRAY(shape, jnp.bfloat16),
             VMEM_ARRAY(spare, jnp.bfloat16),
-            VMEM_ARRAY(out_proj.shape, out_proj.dtype),
             VMEM_ARRAY(value_up.shape, value_up.dtype),
         ),
-        in_specs=[IN_SMEM, IN_SMEM, IN_VMEM, IN_HBM, IN_HBM, IN_HBM],
-        out_specs=(IN_VMEM,) * 4,
+        in_specs=[IN_HBM, IN_SMEM, IN_HBM, IN_HBM, IN_HBM],
+        out_specs=(IN_VMEM,) * 3,
         scratch_shapes=[
+            pltpu.SMEM((rows_dev,), jnp.int32),
+            pltpu.VMEM((rows_dev, key_width, heads), jnp.bfloat16),
             pltpu.VMEM((rows_dev, key_width, context), jnp.bfloat16),
             pltpu.VMEM(wide, jnp.float32),
-            pltpu.SemaphoreType.DMA((rows_dev + 5,)),
+            pltpu.SemaphoreType.DMA((rows_dev + 3,)),
         ],
         compiler_params=pltpu.CompilerParams(vmem_limit_bytes=24 * MIB),
     )(
-        cache_lengths,
+        in_hbm(cache_lengths),
         me[None],
-        queries.transpose(0, 2, 1),
+        in_hbm(queries.transpose(0, 2, 1)),
         in_hbm(latent_cache.transpose(0, 2, 1)),
-        in_hbm(out_proj),
         in_hbm(value_up),
     )
 
@@ -166,23 +196,26 @@
             target[j * run : (j + 1) * run] = sources[a][first : first + run]
 
 
-def deal(sources, ways, run):
+def deal(sources, ways, run, waits_for=()):
     plan = dealt([a.shape[0] for a in sources], ways, run)
     shape = (len(plan[0]) * run, *sources[0].shape[1:])
     return pl.pallas_call(
         functools.partial(deal_kernel, plan, run, len(sources)),
         out_shape=tuple(jax.ShapeDtypeStruct(shape, sources[0].dtype) for _ in plan),
-        in_specs=[IN_VMEM] * len(sources),
+        in_specs=[IN_VMEM] * (len(sources) + len(waits_for)),
         out_specs=(IN_VMEM,) * ways,
         compiler_params=pltpu.CompilerParams(vmem_limit_bytes=4 * MIB),
-    )(*sources)
-
-
-def project_kernel(
-    tile, count, *refs
-):
-    row_of, value_up, proj, hidden, tail = refs[count : count + 5]
-    kept, sent = refs[-2:]
+    )(*sources, *waits_for)
+
+
+def project_kernel(tile, count, *refs):
+    row_of, value_up, top, bottom, hidden, tail = refs[count : count + 6]
+    next_hbm, kept, sent, next_in, sems = refs[count + 6 :] if len(refs) > count + 8 else (
+        None, *refs[count + 6 :], None, None
+    )
+    copies = pieces(next_hbm, next_in, sems, 0) if sems is not None else []
+    for copy in copies:
+        copy.start()
     heads_dev = value_up.shape[0]
     half, wide = kept.shape
     rows_dev, width = hidden.shape
@@ -197,11 +230,15 @@
     select = (row_of[...] == source).astype(jnp.bfloat16)
     head_rows = jnp.dot(select, mixed, preferred_element_type=jnp.float32)
     head_rows = head_rows.astype(jnp.bfloat16)
+    cut = top.shape[0]
 
     @pl.loop(0, width // tile)
     def _(i):
         columns = pl.ds(pl.multiple_of(i * tile, tile), tile)
-        terms = jnp.dot(head_rows, proj[:, columns], preferred_element_type=jnp.float32)
+        terms = jnp.dot(head_rows[:, :cut], top[:, columns], preferred_element_type=jnp.float32)
+        terms += jnp.dot(
+            head_rows[:, cut:], bottom[:, columns], preferred_element_type=jnp.float32
+        )
         kept[:, columns] = terms[:half]
         kept[0:rows_dev, columns] += hidden[:, columns].astype(jnp.float32)
         sent[:, columns] = terms[half:].astype(sent.dtype)
@@ -209,29 +246,36 @@
     kept[:, width:] = jnp.zeros((half, wide - width), kept.dtype)
     kept[0:rows_dev, width:] = tail[...]
     sent[:, width:] = jnp.zeros((half, wide - width), sent.dtype)
-
-
-def project(by_head, row_of, value_up, out_proj, hidden, tail):
+    for copy in copies:
+        copy.wait()
+
+
+def project(by_head, row_of, value_up, top, bottom, hidden, tail, following):
     rows_in = row_of.shape[0]
     width = hidden.shape[1]
     shape = (rows_in // 2, width + LANES)
-    return pl.pallas_call(
+    results = pl.pallas_call(
         functools.partial(project_kernel, 512, len(by_head)),
         out_shape=(
             jax.ShapeDtypeStruct(shape, jnp.float32),
             jax.ShapeDtypeStruct(shape, jnp.bfloat16),
-        ),
-        in_specs=[IN_VMEM] * (len(by_head) + 5),
-        out_specs=(IN_VMEM, IN_VMEM),
+            *[VMEM_ARRAY(w.shape, w.dtype) for w in following],
+        ),
+        in_specs=[IN_VMEM] * (len(by_head) + 6) + [IN_HBM] * len(following),
+        out_specs=(IN_VMEM,) * (2 + len(following)),
+        scratch_shapes=[pltpu.SemaphoreType.DMA((4,))] * len(following),
         compiler_params=pltpu.CompilerParams(vmem_limit_bytes=8 * MIB),
     )(
         *by_head,
         row_of,
         in_vmem(value_up),
-        in_vmem(out_proj),
+        in_vmem(top),
+        in_vmem(bottom),
         hidden,
         tail,
-    )
+        *[in_hbm(w) for w in following],
+    )
+    return results[:2], tuple(results[2:])
 
 
 def halve_kernel(kept, got, next_kept, sent):
@@ -250,20 +294,10 @@
     sent[...] = jnp.where((row & shift) == 0, later, earlier).astype(sent.dtype)
 
 
-def combine(kernel, kept, got, out_rows):
+def combine(kernel, kept, got, out_rows, carried=()):
     shape = (out_rows, kept.shape[1])
-    return pl.pallas_call(
-        kernel,
-        out_shape=(
-            jax.ShapeDtypeStruct(shape, jnp.float32),
-            jax.ShapeDtypeStruct(shape, jnp.bfloat16),
-        ),
-        in_specs=[IN_VMEM] * 2,
-        out_specs=(IN_VMEM, IN_VMEM),
-        compiler_params=pltpu.CompilerParams(
-            vmem_limit_bytes=2 * MIB + 24 * kept.size
-        ),
-    )(kept, got)
+    shapes = (jax.ShapeDtypeStruct(shape, jnp.float32), jax.ShapeDtypeStruct(shape, jnp.bfloat16))
+    return small_call(kernel, (kept, got), shapes, carried, 2 * MIB + 24 * kept.size)
 
 
 def norm_kernel(kept, got, gain, residual, moe_in):
@@ -276,19 +310,12 @@
     moe_in[:, width:] = total[:, width:].astype(moe_in.dtype)
 
 
-def norm(kept, got, gain, rows_dev):
-    return pl.pallas_call(
-        norm_kernel,
-        out_shape=(
-            jax.ShapeDtypeStruct((rows_dev, gain.shape[1]), jnp.float32),
-            jax.ShapeDtypeStruct(kept.shape, jnp.bfloat16),
-        ),
-        in_specs=[IN_VMEM] * 3,
-        out_specs=(IN_VMEM, IN_VMEM),
-        compiler_params=pltpu.CompilerParams(
-            vmem_limit_bytes=2 * MIB + 24 * kept.size
-        ),
-    )(kept, got, gain)
+def norm(kept, got, gain, rows_dev, carried):
+    shapes = (
+        jax.ShapeDtypeStruct((rows_dev, gain.shape[1]), jnp.float32),
+        jax.ShapeDtypeStruct(kept.shape, jnp.bfloat16),
+    )
+    return small_call(norm_kernel, (kept, got, gain), shapes, carried, 2 * MIB + 24 * kept.size)
 
 
 def stack_kernel(first, second, out):
@@ -297,15 +324,12 @@
     out[rows:] = second[...]
 
 
-def stack(first, second):
-    shape = (2 * first.shape[0], first.shape[1])
-    return pl.pallas_call(
-        stack_kernel,
-        out_shape=jax.ShapeDtypeStruct(shape, first.dtype),
-        in_specs=[IN_VMEM] * 2,
-        out_specs=IN_VMEM,
-        compiler_params=pltpu.CompilerParams(vmem_limit_bytes=2 * MIB + 8 * first.size),
-    )(first, second)
+def stack(first, second, carried):
+    shape = jax.ShapeDtypeStruct((2 * first.shape[0], first.shape[1]), first.dtype)
+    (out,), carried = small_call(
+        stack_kernel, (first, second), (shape,), carried, 2 * MIB + 8 * first.size
+    )
+    return out, carried
 
 
 def strips(source, target, sems):
@@ -320,7 +344,7 @@
 
 
 def expert_kernel(
-    expert, first, second, gate, up, down, kept, sent, moe_in, gates, units, up_in, down_in, up_sems, down_sems
+    me, first, second, gate, up, down, kept, sent, moe_in, gates, units, up_in, down_in, up_sems, down_sems
 ):
     width, inner = gate.shape
     half = kept.shape[0]
@@ -333,7 +357,8 @@
     strip = inner // len(ups)
     tail = moe_in[:, width:].astype(jnp.float32)
     column = lax.broadcasted_iota(jnp.int32, tail.shape, 1)
-    mine = (column == expert[0]) | (column == expert[0] + EXPERTS)
+    expert = lax.rem(me[0], EXPERTS)
+    mine = (column == expert) | (column == expert + EXPERTS)
     weight = jnp.sum(jnp.where(mine, tail, 0.0), axis=1, keepdims=True)
 
     @pl.loop(0, len(ups))
@@ -363,7 +388,7 @@
         sent[:, columns] = terms[half:].astype(sent.dtype)
 
 
-def run_expert(expert, first, second, gate, up, down):
+def run_expert(me, first, second, gate, up, down):
     rows = 2 * first.shape[0]
     width, inner = gate.shape
     shape = (rows // 2, width)
@@ -387,7 +412,7 @@
         compiler_params=pltpu.CompilerParams(
             vmem_limit_bytes=4 * MIB + 4 * width * inner + 64 * rows * inner
         ),
-    )(expert, first, second, in_vmem(gate), in_hbm(up), in_hbm(down))
+    )(me, first, second, in_vmem(gate), in_hbm(up), in_hbm(down))
 
 
 def on_device(
@@ -424,52 +449,54 @@
     order = relative_order(bits)
     gate, up, down = gate_proj[0], up_proj[0], down_proj[0]
     if heads_dev % 8 == 0:
-        kept, sent, out_proj, value_up = attend(
-            queries, latent_cache, cache_lengths, out_proj, value_up, order, me
-        )
+        kept, sent, value_up = attend(queries, latent_cache, cache_lengths, value_up, order, me)
         run = ep_size >> 2
         got = exchange(sent, 0)
         kept, sent = deal((kept, got), 2, run)
         got = exchange(sent, 1)
-        parts = deal((kept, got), run, 1)
+        top, token = load(out_proj, sent, 0, 2)
+        parts = deal((kept, got), run, 1, (token,))
+        bottom, _ = load(out_proj, parts[0], 1, 2)
         masks = order[:run]
         by_head = [parts[0]] + [trade(part, mask) for part, mask in zip(parts[1:], masks[1:])]
         held = [mask | x << 1 | core for mask in masks for x in range(2) for core in range(2)]
         row_of = jnp.array([held.index(s) * rows_dev + r for s in order for r in range(rows_dev)])
     else:
-        out, _, out_proj, value_up = attend(
-            queries, latent_cache, cache_lengths, out_proj, value_up, (), me
-        )
+        out, _, value_up = attend(queries, latent_cache, cache_lengths, value_up, (), me)
+        top, _ = load(out_proj, value_up, 0, 2)
+        bottom, _ = load(out_proj, value_up, 1, 2)
         out = out.reshape(rows_dev, ep_size, heads_dev, latent).transpose(1, 0, 2, 3)
         by_head = [lax.all_to_all(out, "ep", split_axis=0, concat_axis=0, tiled=True)]
         by_head = [by_head[0].reshape(rows_in * heads_dev, latent)]
         row_of = (jnp.array(order) ^ me)[:, None] * rows_dev + jnp.arange(rows_dev)[None, :]
         row_of = row_of.reshape(-1)
     row_of = row_of.astype(jnp.int32)
-    kept, sent = project(by_head, row_of[:, None], value_up, out_proj, hidden, tail)
+    following = (gate,) if split_ways == 1 else ()
+    (kept, sent), carried = project(
+        by_head, row_of[:, None], value_up, top, bottom, hidden, tail, following
+    )
 
     rows = rows_in // 2
     for bit in range(scatter_bits - 1):
         rows //= 2
-        kept, sent = combine(halve_kernel, kept, exchange(sent, bit), rows)
+        (kept, sent), carried = combine(
+            halve_kernel, kept, exchange(sent, bit), rows, carried
+        )
     got = exchange(sent, scatter_bits - 1)
     for bit in range(scatter_bits, bits):
-        shift = rows_dev << (bits - 1 - bit)
-        kept, sent = combine(functools.partial(swap_kernel, shift), kept, got, rows)
+        swap = functools.partial(swap_kernel, rows_dev << (bits - 1 - bit))
+        (kept, sent), carried = combine(swap, kept, got, rows, carried)
         got = exchange(sent, bit)
-    residual, moe_in = norm(kept, got, norm_gain[None, :], rows_dev)
+    (residual, moe_in), carried = norm(kept, got, norm_gain[None, :], rows_dev, carried)
     for bit in reversed(range(1, scatter_bits)):
-        got = exchange(moe_in, bit)
-        moe_in = stack(moe_in, got)
+        moe_in, carried = stack(moe_in, exchange(moe_in, bit), carried)
+    other = exchange(moe_in, 0)
+
     if split_ways == 1:
-        gate = load(gate, moe_in)
-    other = exchange(moe_in, 0)
-
-    expert = me % EXPERTS
-    if split_ways == 1:
-        kept, sent = run_expert(expert[None], moe_in, other, gate, up, down)
+        kept, sent = run_expert(me[None], moe_in, other, carried[0], up, down)
     else:
         moe_in = jnp.concatenate((moe_in, other), axis=0)
+        expert = me % EXPERTS
         tail_in = moe_in[:, width:].astype(jnp.float32)
         column = lax.broadcasted_iota(jnp.int32, tail_in.shape, 1)
         mine = (column == expert) | (column == expert + EXPERTS)
@@ -493,7 +520,7 @@
     rows = rows_in // 2
     for bit in range(bits - 1):
         rows //= 2
-        kept, sent = combine(halve_kernel, kept, exchange(sent, bit), rows)
+        (kept, sent), _ = combine(halve_kernel, kept, exchange(sent, bit), rows)
     routed = kept + exchange(sent, bits - 1).astype(jnp.float32)
     return (residual + routed).astype(jnp.bfloat16)
 

time: 89.7 us -> 82.3 us (0.918)
  waiting for transfers between devices: 43.4 us -> 36.6 us
  local copies, waits for them, and re-layouts: 1.66 us -> 0.01 us
    ppermute x15, waiting for transfers between devices: 43.4 us -> 36.6 us  [trade(): lax.ppermute(value, 'ep', [(i, i ^ mask) for i in range(lax.axis_size('ep...]
    pallas_call x1, Pallas kernels: 7.51 us -> 4.98 us  [attend(): pl.pallas_call(functools.partial(attend_kernel, order), out_shape=(VMEM_A...]
    pallas_call x9 -> x10, Pallas kernels: 5.74 us -> 7.44 us  [the longest x2 6.97 us: load(): pl.pallas_call(functools.partial(load_kernel, part * rows), out_shape=(VM...]
    unnamed x14 -> x6, local copies, waits for them, and re-layouts: 1.66 us -> 0.01 us
    pallas_call x1, Pallas kernels: 4.64 us -> 5.54 us  [project(): pl.pallas_call(functools.partial(project_kernel, 512, len(by_head)), out_...]
  transfers between devices with their start and end apart: 15 -> 15, of which waited for: 14 -> 13; matrix products, arithmetic and copies ran while one was open for 0% -> 1% of each run, Pallas kernels for 6% -> 8%
where the time goes in v2:
time: 82.3 us; the launch traced here: 82.1 us
  waiting for transfers between devices  36.6 us (44%)
  Pallas kernels  29 us (35%)
  starting transfers between devices  14.8 us (18%)
  other arithmetic  1.51 us (2%)
    ppermute x15, waiting for transfers between devices, trade(): lax.ppermute(value, 'ep', [(i, i ^ mask) for i in range(lax.axis_size('ep...  36.6 us
    ppermute x15, starting transfers between devices, trade(): lax.ppermute(value, 'ep', [(i, i ^ mask) for i in range(lax.axis_size('ep...  14.8 us
    pallas_call x1, Pallas kernels, run_expert(): pl.pallas_call(expert_kernel, out_shape=(jax.ShapeDtypeStruct(shape, jnp....  11 us
    pallas_call x2, Pallas kernels, load(): pl.pallas_call(functools.partial(load_kernel, part * rows), out_shape=(VM...  6.97 us
    pallas_call x1, Pallas kernels, project(): pl.pallas_call(functools.partial(project_kernel, 512, len(by_head)), out_...  5.54 us
    pallas_call x1, Pallas kernels, attend(): pl.pallas_call(functools.partial(attend_kernel, order), out_shape=(VMEM_A...  4.98 us
  transfers between devices with their start and end apart: 15, of which 13 were waited for; matrix products, arithmetic and copies ran while one was open for 1% of the time, Pallas kernels for 8%

profile of v2, /device:TPU:0, one launch (start us, length us, event | category | flops | bytes accessed | tf_op | source)
XLA Modules:
  0.0 82.1 jit_solution(15118671543302435234)
XLA Ops:
  0.0 5.0 %shard_map.127 = (bf16[8,16,512]{2,1,0:T(8,128)(2,1)S(1)}, bf16[8,16,512]{2,1,0:T(8,128)(2,1)S(1)}, bf16[8,512,128]{2,1,0:T(8,128)(2,1)S(1)}) custom-call(s32[2]{0:T(128)} %lengths_hbm.1, s32[1]{0:T(128)} %bitcast.me, bf16[2,576,128]{2,1,0:T(8,128)(2,1)} %bitcast.12, bf16[2,576,2048]{2,1,0:T(8,128)(2,1)} %bitcast.11, bf16[8,512,128]{2,1,0:T(8,128)(2,1)} %value_up.1), custom_call_target="tpu_custom_call" | custom-call | tf_op jit(solution)/shard_map/pallas_call | solution.py:155
  5.0 0.5 collective-permute-start
  5.5 0.8 select_reduce_fusion
  6.3 0.2 collective-permute-done.refs_1_
  6.5 2.9 %collective-permute-start.1 = (bf16[8,16,512]{2,1,0:T(8,128)(2,1)S(1)}, bf16[8,16,512]{2,1,0:T(8,128)(2,1)S(1)}, u32[]{:S(2)}, u32[]{:S(2)}) collective-permute-start(bf16[8,16,512]{2,1,0:T(8,128)(2,1)S(1)} %get-tuple-element.45.after), channel_id=1, source_target_pairs={{0,2},{1,3},{2,0},{3,1},{4,6},{5,7},{6,4},{7,5},{8,10},{9,11},{10,... | collective-permute-start | bytes 393224 | tf_op jit(solution)/shard_map/ppermute | solution.py:22
  9.4 0.0 copy-start.1
  9.4 0.0 copy-start.2
  9.4 3.2 %shard_map.129 = (bf16[512,7168]{1,0:T(8,128)(2,1)S(1)}, f32[8,128]{1,0:T(8,128)S(1)}) custom-call(bf16[1024,7168]{1,0:T(8,128)(2,1)} %source.3, bf16[8,16,512]{2,1,0:T(8,128)(2,1)S(1)} %get-tuple-element.45.after), custom_call_target="tpu_custom_call" | custom-call | bytes 14680064 | tf_op jit(solution)/shard_map/pallas_call | solution.py:68
  12.6 0.6 collective-permute-done.1.refs_1_
  13.3 2.9 %collective-permute-start.2 = (bf16[4,16,512]{2,1,0:T(8,128)(2,1)S(1)}, bf16[4,16,512]{2,1,0:T(8,128)(2,1)S(1)}, u32[]{:S(2)}, u32[]{:S(2)}) collective-permute-start(bf16[4,16,512]{2,1,0:T(8,128)(2,1)S(1)} %get-tuple-element.48), channel_id=1, source_target_pairs={{0,8},{1,9},{2,10},{3,11},{4,12},{5,13},{6,14},{7,15},{8,0},{9,1},... | collective-permute-start | bytes 196616 | tf_op jit(solution)/shard_map/ppermute | solution.py:22
  16.2 1.6 %collective-permute-start.3 = (bf16[4,16,512]{2,1,0:T(8,128)(2,1)S(1)}, bf16[4,16,512]{2,1,0:T(8,128)(2,1)S(1)}, u32[]{:S(2)}, u32[]{:S(2)}) collective-permute-start(bf16[4,16,512]{2,1,0:T(8,128)(2,1)S(1)} %get-tuple-element.49), channel_id=1, source_target_pairs={{0,4},{1,5},{2,6},{3,7},{4,0},{5,1},{6,2},{7,3},{8,12},{9,13},{10,... | collective-permute-start | bytes 196616 | tf_op jit(solution)/shard_map/ppermute | solution.py:22
  17.7 0.0 collective-permute-start.4
  17.7 0.1 select_maximum_fusion.refs_9_
  17.8 3.8 %shard_map.131 = (bf16[512,7168]{1,0:T(8,128)(2,1)S(1)}, f32[8,128]{1,0:T(8,128)}) custom-call(bf16[1024,7168]{1,0:T(8,128)(2,1)} %source.3, bf16[4,16,512]{2,1,0:T(8,128)(2,1)S(1)} %get-tuple-element.47.after.refs_0_), custom_call_target="tpu_custom_call" | custom-call | bytes 14680064 | tf_op jit(solution)/shard_map/pallas_call | solution.py:68
  21.6 0.0 collective-permute-done.2.refs_1_
  21.6 0.0 collective-permute-done.3.refs_2_
  21.6 2.2 %collective-permute-done.4.refs_3_ = bf16[4,16,512]{2,1,0:T(8,128)(2,1)S(1)} collective-permute-done((bf16[4,16,512]{2,1,0:T(8,128)(2,1)S(1)}, bf16[4,16,512]{2,1,0:T(8,128)(2,1)S(1)}, u32[]{:S(2)}, u32[]{:S(2)}) %collective-permute-start.4) | collective-permute-done | bytes 65568 | tf_op jit(solution)/shard_map/ppermute | solution.py:22
  23.8 0.0 copy-done.1
  23.8 0.0 copy-done.2
  23.8 5.5 %shard_map.132 = (f32[16,7296]{1,0:T(8,128)S(1)}, bf16[16,7296]{1,0:T(8,128)(2,1)S(1)}, bf16[7168,1024]{1,0:T(8,128)(2,1)S(1)}) custom-call(bf16[4,16,512]{2,1,0:T(8,128)(2,1)S(1)} %get-tuple-element.47.after.refs_0_, bf16[4,16,512]{2,1,0:T(8,128)(2,1)S(1)} %collective-permute-done.2.refs_1_, bf16[4,16,512]{2,1,0:T(8,128)(2,1)S(1)} %collective-permute-done.3.refs_2_, ...), custom_call_target="tpu_custom_call" | custom-call | tf_op jit(solution)/shard_map/pallas_call | solution.py:257
  29.4 0.1 collective-permute-start.5
  29.4 1.5 %collective-permute-done.5.refs_1_ = bf16[16,7296]{1,0:T(8,128)(2,1)S(1)} collective-permute-done((bf16[16,7296]{1,0:T(8,128)(2,1)S(1)}, bf16[16,7296]{1,0:T(8,128)(2,1)S(1)}, u32[]{:S(2)}, u32[]{:S(2)}) %collective-permute-start.5) | collective-permute-done | bytes 233504 | tf_op jit(solution)/shard_map/ppermute | solution.py:22
  30.9 0.1 shard_map.133
  31.0 1.6 %collective-permute-start.6 = (bf16[8,7296]{1,0:T(8,128)(2,1)S(1)}, bf16[8,7296]{1,0:T(8,128)(2,1)S(1)}, u32[]{:S(2)}, u32[]{:S(2)}) collective-permute-start(bf16[8,7296]{1,0:T(8,128)(2,1)S(1)} %get-tuple-element.58), channel_id=1, source_target_pairs={{0,2},{1,3},{2,0},{3,1},{4,6},{5,7},{6,4},{7,5},{8,10},{9,11},{10,... | collective-permute-start | bytes 350216 | tf_op jit(solution)/shard_map/ppermute | solution.py:22
  32.5 3.7 %collective-permute-done.6.refs_1_ = bf16[8,7296]{1,0:T(8,128)(2,1)S(1)} collective-permute-done((bf16[8,7296]{1,0:T(8,128)(2,1)S(1)}, bf16[8,7296]{1,0:T(8,128)(2,1)S(1)}, u32[]{:S(2)}, u32[]{:S(2)}) %collective-permute-start.6) | collective-permute-done | bytes 116768 | tf_op jit(solution)/shard_map/ppermute | solution.py:22
  36.3 0.0 copy-start
  36.3 0.1 collective-permute-start.7
  36.4 4.8 %collective-permute-done.7.refs_1_ = bf16[8,7296]{1,0:T(8,128)(2,1)S(1)} collective-permute-done((bf16[8,7296]{1,0:T(8,128)(2,1)S(1)}, bf16[8,7296]{1,0:T(8,128)(2,1)S(1)}, u32[]{:S(2)}, u32[]{:S(2)}) %collective-permute-start.7) | collective-permute-done | bytes 116768 | tf_op jit(solution)/shard_map/ppermute | solution.py:22
  41.2 0.1 shard_map.135
  41.3 0.9 %collective-permute-start.8 = (bf16[8,7296]{1,0:T(8,128)(2,1)S(1)}, bf16[8,7296]{1,0:T(8,128)(2,1)S(1)}, u32[]{:S(2)}, u32[]{:S(2)}) collective-permute-start(bf16[8,7296]{1,0:T(8,128)(2,1)S(1)} %get-tuple-element.64), channel_id=1, source_target_pairs={{0,8},{1,9},{2,10},{3,11},{4,12},{5,13},{6,14},{7,15},{8,0},{9,1},... | collective-permute-start | bytes 350216 | tf_op jit(solution)/shard_map/ppermute | solution.py:22
  42.1 5.6 %collective-permute-done.8.refs_1_ = bf16[8,7296]{1,0:T(8,128)(2,1)S(1)} collective-permute-done((bf16[8,7296]{1,0:T(8,128)(2,1)S(1)}, bf16[8,7296]{1,0:T(8,128)(2,1)S(1)}, u32[]{:S(2)}, u32[]{:S(2)}) %collective-permute-start.8) | collective-permute-done | bytes 116768 | tf_op jit(solution)/shard_map/ppermute | solution.py:22
  47.7 0.0 copy-done
  47.7 0.2 shard_map.136
  47.9 1.6 %collective-permute-start.9 = (bf16[8,7296]{1,0:T(8,128)(2,1)S(1)}, bf16[8,7296]{1,0:T(8,128)(2,1)S(1)}, u32[]{:S(2)}, u32[]{:S(2)}) collective-permute-start(bf16[8,7296]{1,0:T(8,128)(2,1)S(1)} %get-tuple-element.67.refs_0_), channel_id=1, source_target_pairs={{0,2},{1,3},{2,0},{3,1},{4,6},{5,7},{6,4},{7,5},{8,10},{9,11},{10,... | collective-permute-start | bytes 350216 | tf_op jit(solution)/shard_map/ppermute | solution.py:22
  49.5 3.3 %collective-permute-done.9.refs_1_ = bf16[8,7296]{1,0:T(8,128)(2,1)S(1)} collective-permute-done((bf16[8,7296]{1,0:T(8,128)(2,1)S(1)}, bf16[8,7296]{1,0:T(8,128)(2,1)S(1)}, u32[]{:S(2)}, u32[]{:S(2)}) %collective-permute-start.9) | collective-permute-done | bytes 116768 | tf_op jit(solution)/shard_map/ppermute | solution.py:22
  52.8 0.1 collective-permute-start.10
  52.9 1.5 %collective-permute-done.10.second = bf16[16,7296]{1,0:T(8,128)(2,1)S(1)} collective-permute-done((bf16[16,7296]{1,0:T(8,128)(2,1)S(1)}, bf16[16,7296]{1,0:T(8,128)(2,1)S(1)}, u32[]{:S(2)}, u32[]{:S(2)}) %collective-permute-start.10) | collective-permute-done | bytes 233504 | tf_op jit(solution)/shard_map/ppermute | solution.py:22
  54.4 11.0 %shard_map.138 = (f32[16,7168]{1,0:T(8,128)S(1)}, bf16[16,7168]{1,0:T(8,128)(2,1)S(1)}) custom-call(s32[1]{0:T(128)} %bitcast.me, bf16[16,7296]{1,0:T(8,128)(2,1)S(1)} %get-tuple-element.69.first, bf16[16,7296]{1,0:T(8,128)(2,1)S(1)} %collective-permute-done.10.second, bf16[7168,1024]{1,0:T(8,128)(2,1)S(1)} %get-tuple-element.70.gate, ...), custom_call_target="tpu_custom_call" | custom-call | tf_op jit(solution)/shard_map/pallas_call | solution.py:395
  65.4 0.2 collective-permute-start.11
  65.6 1.4 %collective-permute-done.11.refs_1_ = bf16[16,7168]{1,0:T(8,128)(2,1)S(1)} collective-permute-done((bf16[16,7168]{1,0:T(8,128)(2,1)S(1)}, bf16[16,7168]{1,0:T(8,128)(2,1)S(1)}, u32[]{:S(2)}, u32[]{:S(2)}) %collective-permute-start.11) | collective-permute-done | bytes 229408 | tf_op jit(solution)/shard_map/ppermute | solution.py:22
  67.0 1.6 %collective-permute-start.12 = (bf16[8,7168]{1,0:T(8,128)(2,1)S(1)}, bf16[8,7168]{1,0:T(8,128)(2,1)S(1)}, u32[]{:S(2)}, u32[]{:S(2)}) collective-permute-start(bf16[8,7168]{1,0:T(8,128)(2,1)S(1)} %get-tuple-element.74), channel_id=1, source_target_pairs={{0,2},{1,3},{2,0},{3,1},{4,6},{5,7},{6,4},{7,5},{8,10},{9,11},{10,... | collective-permute-start | bytes 344072 | tf_op jit(solution)/shard_map/ppermute | solution.py:22
  68.6 3.7 %collective-permute-done.12.refs_1_ = bf16[8,7168]{1,0:T(8,128)(2,1)S(1)} collective-permute-done((bf16[8,7168]{1,0:T(8,128)(2,1)S(1)}, bf16[8,7168]{1,0:T(8,128)(2,1)S(1)}, u32[]{:S(2)}, u32[]{:S(2)}) %collective-permute-start.12) | collective-permute-done | bytes 114720 | tf_op jit(solution)/shard_map/ppermute | solution.py:22
  72.3 0.1 collective-permute-start.13
  72.4 4.2 %collective-permute-done.13.refs_1_ = bf16[4,7168]{1,0:T(4,128)(2,1)S(1)} collective-permute-done((bf16[4,7168]{1,0:T(4,128)(2,1)S(1)}, bf16[4,7168]{1,0:T(4,128)(2,1)S(1)}, u32[]{:S(2)}, u32[]{:S(2)}) %collective-permute-start.13) | collective-permute-done | bytes 57376 | tf_op jit(solution)/shard_map/ppermute | solution.py:22
  76.6 0.8 %collective-permute-start.14 = (bf16[2,7168]{1,0:T(2,128)(2,1)S(1)}, bf16[2,7168]{1,0:T(2,128)(2,1)S(1)}, u32[]{:S(2)}, u32[]{:S(2)}) collective-permute-start(bf16[2,7168]{1,0:T(2,128)(2,1)S(1)} %get-tuple-element.78), channel_id=1, source_target_pairs={{0,8},{1,9},{2,10},{3,11},{4,12},{5,13},{6,14},{7,15},{8,0},{9,1},... | collective-permute-start | bytes 86024 | tf_op jit(solution)/shard_map/ppermute | solution.py:22
  77.5 4.0 %collective-permute-done.14 = bf16[2,7168]{1,0:T(2,128)(2,1)S(1)} collective-permute-done((bf16[2,7168]{1,0:T(2,128)(2,1)S(1)}, bf16[2,7168]{1,0:T(2,128)(2,1)S(1)}, u32[]{:S(2)}, u32[]{:S(2)}) %collective-permute-start.14) | collective-permute-done | bytes 28704 | tf_op jit(solution)/shard_map/ppermute | solution.py:22
  81.4 0.7 add_convert_fusion
  (8 shorter events, 0.2 us)
Async XLA Ops:
  5.0 1.5 %collective-permute-start = (bf16[8,16,512]{2,1,0:T(8,128)(2,1)S(1)}, bf16[8,16,512]{2,1,0:T(8,128)(2,1)S(1)}, u32[]{:S(2)}, u32[]{:S(2)}) collective-permute-start(bf16[8,16,512]{2,1,0:T(8,128)(2,1)S(1)} %get-tuple-element.43), channel_id=1, source_target_pairs={{0,1},{1,0},{2,3},{3,2},{4,5},{5,4},{6,7},{7,6},{8,9},{9,8},{10,11... | collective-permute-start | bytes 393224 | tf_op jit(solution)/shard_map/ppermute | solution.py:22
  6.5 6.7 %collective-permute-start.1 = (bf16[8,16,512]{2,1,0:T(8,128)(2,1)S(1)}, bf16[8,16,512]{2,1,0:T(8,128)(2,1)S(1)}, u32[]{:S(2)}, u32[]{:S(2)}) collective-permute-start(bf16[8,16,512]{2,1,0:T(8,128)(2,1)S(1)} %get-tuple-element.45.after), channel_id=1, source_target_pairs={{0,2},{1,3},{2,0},{3,1},{4,6},{5,7},{6,4},{7,5},{8,10},{9,11},{10,... | collective-permute-start | bytes 393224 | tf_op jit(solution)/shard_map/ppermute | solution.py:22
  9.4 14.4 %copy-start.1 = (bf16[2,7168]{1,0:T(2,128)(2,1)S(1)}, bf16[2,7168]{1,0:T(2,128)(2,1)}, u32[]{:S(2)}) copy-start(bf16[2,7168]{1,0:T(2,128)(2,1)} %refs_8_.1) | copy-start | bytes 86020
  9.4 14.4 %copy-start.2 = (s32[32,1]{1,0:T(8,128)S(1)}, s32[32,1]{1,0:T(8,128)}, u32[]{:S(2)}) copy-start(s32[32,1]{1,0:T(8,128)} %constant.23.refs_4_) | copy-start | bytes 388
  13.3 8.4 %collective-permute-start.2 = (bf16[4,16,512]{2,1,0:T(8,128)(2,1)S(1)}, bf16[4,16,512]{2,1,0:T(8,128)(2,1)S(1)}, u32[]{:S(2)}, u32[]{:S(2)}) collective-permute-start(bf16[4,16,512]{2,1,0:T(8,128)(2,1)S(1)} %get-tuple-element.48), channel_id=1, source_target_pairs={{0,8},{1,9},{2,10},{3,11},{4,12},{5,13},{6,14},{7,15},{8,0},{9,1},... | collective-permute-start | bytes 196616 | tf_op jit(solution)/shard_map/ppermute | solution.py:22
  16.2 5.5 %collective-permute-start.3 = (bf16[4,16,512]{2,1,0:T(8,128)(2,1)S(1)}, bf16[4,16,512]{2,1,0:T(8,128)(2,1)S(1)}, u32[]{:S(2)}, u32[]{:S(2)}) collective-permute-start(bf16[4,16,512]{2,1,0:T(8,128)(2,1)S(1)} %get-tuple-element.49), channel_id=1, source_target_pairs={{0,4},{1,5},{2,6},{3,7},{4,0},{5,1},{6,2},{7,3},{8,12},{9,13},{10,... | collective-permute-start | bytes 196616 | tf_op jit(solution)/shard_map/ppermute | solution.py:22
  17.7 6.1 %collective-permute-start.4 = (bf16[4,16,512]{2,1,0:T(8,128)(2,1)S(1)}, bf16[4,16,512]{2,1,0:T(8,128)(2,1)S(1)}, u32[]{:S(2)}, u32[]{:S(2)}) collective-permute-start(bf16[4,16,512]{2,1,0:T(8,128)(2,1)S(1)} %get-tuple-element.50), channel_id=1, source_target_pairs={{0,12},{1,13},{2,14},{3,15},{4,8},{5,9},{6,10},{7,11},{8,4},{9,5},... | collective-permute-start | bytes 196616 | tf_op jit(solution)/shard_map/ppermute | solution.py:22
  29.4 1.6 %collective-permute-start.5 = (bf16[16,7296]{1,0:T(8,128)(2,1)S(1)}, bf16[16,7296]{1,0:T(8,128)(2,1)S(1)}, u32[]{:S(2)}, u32[]{:S(2)}) collective-permute-start(bf16[16,7296]{1,0:T(8,128)(2,1)S(1)} %get-tuple-element.55), channel_id=1, source_target_pairs={{0,1},{1,0},{2,3},{3,2},{4,5},{5,4},{6,7},{7,6},{8,9},{9,8},{10,11... | collective-permute-start | bytes 700424 | tf_op jit(solution)/shard_map/ppermute | solution.py:22
  31.0 5.3 %collective-permute-start.6 = (bf16[8,7296]{1,0:T(8,128)(2,1)S(1)}, bf16[8,7296]{1,0:T(8,128)(2,1)S(1)}, u32[]{:S(2)}, u32[]{:S(2)}) collective-permute-start(bf16[8,7296]{1,0:T(8,128)(2,1)S(1)} %get-tuple-element.58), channel_id=1, source_target_pairs={{0,2},{1,3},{2,0},{3,1},{4,6},{5,7},{6,4},{7,5},{8,10},{9,11},{10,... | collective-permute-start | bytes 350216 | tf_op jit(solution)/shard_map/ppermute | solution.py:22
  36.3 11.5 %copy-start = (f32[7168]{0:T(1024)S(1)}, f32[7168]{0:T(1024)}, u32[]{:S(2)}) copy-start(f32[7168]{0:T(1024)} %param.19) | copy-start | bytes 86020
  36.3 4.9 %collective-permute-start.7 = (bf16[8,7296]{1,0:T(8,128)(2,1)S(1)}, bf16[8,7296]{1,0:T(8,128)(2,1)S(1)}, u32[]{:S(2)}, u32[]{:S(2)}) collective-permute-start(bf16[8,7296]{1,0:T(8,128)(2,1)S(1)} %get-tuple-element.61), channel_id=1, source_target_pairs={{0,4},{1,5},{2,6},{3,7},{4,0},{5,1},{6,2},{7,3},{8,12},{9,13},{10,... | collective-permute-start | bytes 350216 | tf_op jit(solution)/shard_map/ppermute | solution.py:22
  41.3 6.5 %collective-permute-start.8 = (bf16[8,7296]{1,0:T(8,128)(2,1)S(1)}, bf16[8,7296]{1,0:T(8,128)(2,1)S(1)}, u32[]{:S(2)}, u32[]{:S(2)}) collective-permute-start(bf16[8,7296]{1,0:T(8,128)(2,1)S(1)} %get-tuple-element.64), channel_id=1, source_target_pairs={{0,8},{1,9},{2,10},{3,11},{4,12},{5,13},{6,14},{7,15},{8,0},{9,1},... | collective-permute-start | bytes 350216 | tf_op jit(solution)/shard_map/ppermute | solution.py:22
  47.9 4.9 %collective-permute-start.9 = (bf16[8,7296]{1,0:T(8,128)(2,1)S(1)}, bf16[8,7296]{1,0:T(8,128)(2,1)S(1)}, u32[]{:S(2)}, u32[]{:S(2)}) collective-permute-start(bf16[8,7296]{1,0:T(8,128)(2,1)S(1)} %get-tuple-element.67.refs_0_), channel_id=1, source_target_pairs={{0,2},{1,3},{2,0},{3,1},{4,6},{5,7},{6,4},{7,5},{8,10},{9,11},{10,... | collective-permute-start | bytes 350216 | tf_op jit(solution)/shard_map/ppermute | solution.py:22
  52.8 1.6 %collective-permute-start.10 = (bf16[16,7296]{1,0:T(8,128)(2,1)S(1)}, bf16[16,7296]{1,0:T(8,128)(2,1)S(1)}, u32[]{:S(2)}, u32[]{:S(2)}) collective-permute-start(bf16[16,7296]{1,0:T(8,128)(2,1)S(1)} %get-tuple-element.69.first), channel_id=1, source_target_pairs={{0,1},{1,0},{2,3},{3,2},{4,5},{5,4},{6,7},{7,6},{8,9},{9,8},{10,11... | collective-permute-start | bytes 700424 | tf_op jit(solution)/shard_map/ppermute | solution.py:22
  65.4 1.6 %collective-permute-start.11 = (bf16[16,7168]{1,0:T(8,128)(2,1)S(1)}, bf16[16,7168]{1,0:T(8,128)(2,1)S(1)}, u32[]{:S(2)}, u32[]{:S(2)}) collective-permute-start(bf16[16,7168]{1,0:T(8,128)(2,1)S(1)} %get-tuple-element.72), channel_id=1, source_target_pairs={{0,1},{1,0},{2,3},{3,2},{4,5},{5,4},{6,7},{7,6},{8,9},{9,8},{10,11... | collective-permute-start | bytes 688136 | tf_op jit(solution)/shard_map/ppermute | solution.py:22
  67.0 5.3 %collective-permute-start.12 = (bf16[8,7168]{1,0:T(8,128)(2,1)S(1)}, bf16[8,7168]{1,0:T(8,128)(2,1)S(1)}, u32[]{:S(2)}, u32[]{:S(2)}) collective-permute-start(bf16[8,7168]{1,0:T(8,128)(2,1)S(1)} %get-tuple-element.74), channel_id=1, source_target_pairs={{0,2},{1,3},{2,0},{3,1},{4,6},{5,7},{6,4},{7,5},{8,10},{9,11},{10,... | collective-permute-start | bytes 344072 | tf_op jit(solution)/shard_map/ppermute | solution.py:22
  72.3 4.2 %collective-permute-start.13 = (bf16[4,7168]{1,0:T(4,128)(2,1)S(1)}, bf16[4,7168]{1,0:T(4,128)(2,1)S(1)}, u32[]{:S(2)}, u32[]{:S(2)}) collective-permute-start(bf16[4,7168]{1,0:T(4,128)(2,1)S(1)} %get-tuple-element.76), channel_id=1, source_target_pairs={{0,4},{1,5},{2,6},{3,7},{4,0},{5,1},{6,2},{7,3},{8,12},{9,13},{10,... | collective-permute-start | bytes 172040 | tf_op jit(solution)/shard_map/ppermute | solution.py:22
  76.6 4.8 %collective-permute-start.14 = (bf16[2,7168]{1,0:T(2,128)(2,1)S(1)}, bf16[2,7168]{1,0:T(2,128)(2,1)S(1)}, u32[]{:S(2)}, u32[]{:S(2)}) collective-permute-start(bf16[2,7168]{1,0:T(2,128)(2,1)S(1)} %get-tuple-element.78), channel_id=1, source_target_pairs={{0,8},{1,9},{2,10},{3,11},{4,12},{5,13},{6,14},{7,15},{8,0},{9,1},... | collective-permute-start | bytes 86024 | tf_op jit(solution)/shard_map/ppermute | solution.py:22

commit v3 on v2

--- a/solution.py
+++ b/solution.py
@@ -30,7 +30,6 @@
 MIB = 1 << 20
 IN_VMEM = pl.BlockSpec(memory_space=pltpu.VMEM)
 IN_SMEM = pl.BlockSpec(memory_space=pltpu.SMEM)
-ANYWHERE = pl.BlockSpec(memory_space=pl.ANY)
 IN_HBM = pl.BlockSpec(memory_space=pltpu.HBM)
 VMEM_ARRAY = pltpu.VMEM
 
@@ -63,7 +62,7 @@
         copy.wait()
 
 
-def load(source, after, part=0, parts=1):
+def load(source, after, limit, part, parts=2):
     rows = source.shape[0] // parts
     return pl.pallas_call(
         functools.partial(load_kernel, part * rows),
@@ -74,7 +73,7 @@
         in_specs=[IN_HBM, IN_VMEM],
         out_specs=(IN_VMEM, IN_VMEM),
         scratch_shapes=[pltpu.SemaphoreType.DMA((4,))],
-        compiler_params=pltpu.CompilerParams(vmem_limit_bytes=MIB),
+        compiler_params=pltpu.CompilerParams(vmem_limit_bytes=limit),
         cost_estimate=pl.CostEstimate(
             flops=0,
             bytes_accessed=2 * rows * source.shape[1] * source.dtype.itemsize,
@@ -83,22 +82,23 @@
     )(in_hbm(source), in_vmem(after))
 
 
-def pass_on(kernel, ins, outs, *refs):
-    more = len(refs) - ins - outs
-    kernel(*refs[:ins], *refs[ins + more // 2 : ins + more // 2 + outs])
-
-
-def small_call(kernel, operands, shapes, carried, limit):
+def grant(rows, columns):
+    return 4 * MIB + 16 * rows * columns
+
+
+def only(kernel, ins, outs, *refs):
+    kernel(*refs[:ins], *refs[len(refs) - outs :])
+
+
+def small_call(kernel, operands, shapes, waits_for, limit):
     ins, outs = len(operands), len(shapes)
-    results = pl.pallas_call(
-        functools.partial(pass_on, kernel, ins, outs),
-        out_shape=tuple(shapes) + tuple(VMEM_ARRAY(c.shape, c.dtype) for c in carried),
-        in_specs=[IN_VMEM] * ins + [ANYWHERE] * len(carried),
-        out_specs=(IN_VMEM,) * outs + (ANYWHERE,) * len(carried),
-        input_output_aliases={ins + i: outs + i for i in range(len(carried))},
+    return pl.pallas_call(
+        functools.partial(only, kernel, ins, outs),
+        out_shape=tuple(shapes),
+        in_specs=[IN_VMEM] * (ins + len(waits_for)),
+        out_specs=(IN_VMEM,) * outs,
         compiler_params=pltpu.CompilerParams(vmem_limit_bytes=limit),
-    )(*operands, *[in_vmem(c) for c in carried])
-    return results[:outs], tuple(results[outs:])
+    )(*operands, *waits_for)
 
 
 def attend_kernel(
@@ -196,7 +196,7 @@
             target[j * run : (j + 1) * run] = sources[a][first : first + run]
 
 
-def deal(sources, ways, run, waits_for=()):
+def deal(sources, ways, run, limit, waits_for=()):
     plan = dealt([a.shape[0] for a in sources], ways, run)
     shape = (len(plan[0]) * run, *sources[0].shape[1:])
     return pl.pallas_call(
@@ -204,7 +204,7 @@
         out_shape=tuple(jax.ShapeDtypeStruct(shape, sources[0].dtype) for _ in plan),
         in_specs=[IN_VMEM] * (len(sources) + len(waits_for)),
         out_specs=(IN_VMEM,) * ways,
-        compiler_params=pltpu.CompilerParams(vmem_limit_bytes=4 * MIB),
+        compiler_params=pltpu.CompilerParams(vmem_limit_bytes=limit),
     )(*sources, *waits_for)
 
 
@@ -213,7 +213,9 @@
     next_hbm, kept, sent, next_in, sems = refs[count + 6 :] if len(refs) > count + 8 else (
         None, *refs[count + 6 :], None, None
     )
-    copies = pieces(next_hbm, next_in, sems, 0) if sems is not None else []
+    copies = []
+    if sems is not None:
+        copies = pieces(next_hbm.at[pl.ds(0, next_in.shape[0])], next_in, sems, 0)
     for copy in copies:
         copy.start()
     heads_dev = value_up.shape[0]
@@ -250,21 +252,21 @@
         copy.wait()
 
 
-def project(by_head, row_of, value_up, top, bottom, hidden, tail, following):
+def project(by_head, row_of, value_up, top, bottom, hidden, tail, following, limit):
     rows_in = row_of.shape[0]
     width = hidden.shape[1]
     shape = (rows_in // 2, width + LANES)
     results = pl.pallas_call(
-        functools.partial(project_kernel, 512, len(by_head)),
+        functools.partial(project_kernel, width // 2, len(by_head)),
         out_shape=(
             jax.ShapeDtypeStruct(shape, jnp.float32),
             jax.ShapeDtypeStruct(shape, jnp.bfloat16),
-            *[VMEM_ARRAY(w.shape, w.dtype) for w in following],
+            *[VMEM_ARRAY((w.shape[0] // 2, w.shape[1]), w.dtype) for w in following],
         ),
         in_specs=[IN_VMEM] * (len(by_head) + 6) + [IN_HBM] * len(following),
         out_specs=(IN_VMEM,) * (2 + len(following)),
         scratch_shapes=[pltpu.SemaphoreType.DMA((4,))] * len(following),
-        compiler_params=pltpu.CompilerParams(vmem_limit_bytes=8 * MIB),
+        compiler_params=pltpu.CompilerParams(vmem_limit_bytes=limit),
     )(
         *by_head,
         row_of,
@@ -294,10 +296,10 @@
     sent[...] = jnp.where((row & shift) == 0, later, earlier).astype(sent.dtype)
 
 
-def combine(kernel, kept, got, out_rows, carried=()):
+def combine(kernel, kept, got, out_rows, limit, waits_for=()):
     shape = (out_rows, kept.shape[1])
     shapes = (jax.ShapeDtypeStruct(shape, jnp.float32), jax.ShapeDtypeStruct(shape, jnp.bfloat16))
-    return small_call(kernel, (kept, got), shapes, carried, 2 * MIB + 24 * kept.size)
+    return small_call(kernel, (kept, got), shapes, waits_for, limit)
 
 
 def norm_kernel(kept, got, gain, residual, moe_in):
@@ -310,12 +312,12 @@
     moe_in[:, width:] = total[:, width:].astype(moe_in.dtype)
 
 
-def norm(kept, got, gain, rows_dev, carried):
+def norm(kept, got, gain, rows_dev, limit, waits_for):
     shapes = (
         jax.ShapeDtypeStruct((rows_dev, gain.shape[1]), jnp.float32),
         jax.ShapeDtypeStruct(kept.shape, jnp.bfloat16),
     )
-    return small_call(norm_kernel, (kept, got, gain), shapes, carried, 2 * MIB + 24 * kept.size)
+    return small_call(norm_kernel, (kept, got, gain), shapes, waits_for, limit)
 
 
 def stack_kernel(first, second, out):
@@ -324,12 +326,9 @@
     out[rows:] = second[...]
 
 
-def stack(first, second, carried):
+def stack(first, second, limit):
     shape = jax.ShapeDtypeStruct((2 * first.shape[0], first.shape[1]), first.dtype)
-    (out,), carried = small_call(
-        stack_kernel, (first, second), (shape,), carried, 2 * MIB + 8 * first.size
-    )
-    return out, carried
+    return small_call(stack_kernel, (first, second), (shape,), (), limit)[0]
 
 
 def strips(source, target, sems):
@@ -344,43 +343,37 @@
 
 
 def expert_kernel(
-    me, first, second, gate, up, down, kept, sent, moe_in, gates, units, up_in, down_in, up_sems, down_sems
+    me, first, second, gate_top, gate_bottom, up_top, up_bottom, down, kept, sent, moe_in, units, down_in, sems
 ):
-    width, inner = gate.shape
+    cut, inner = gate_top.shape
+    width = 2 * cut
     half = kept.shape[0]
-    ups, downs = strips(up, up_in, up_sems), strips(down, down_in, down_sems)
-    for copy in ups:
+    downs = strips(down, down_in, sems)
+    for copy in downs:
         copy.start()
     moe_in[:half] = first[...]
     moe_in[half:] = second[...]
-    rows = moe_in[:, :width]
-    strip = inner // len(ups)
     tail = moe_in[:, width:].astype(jnp.float32)
     column = lax.broadcasted_iota(jnp.int32, tail.shape, 1)
     expert = lax.rem(me[0], EXPERTS)
     mine = (column == expert) | (column == expert + EXPERTS)
     weight = jnp.sum(jnp.where(mine, tail, 0.0), axis=1, keepdims=True)
 
-    @pl.loop(0, len(ups))
-    def _(i):
-        columns = pl.ds(pl.multiple_of(i * strip, strip), strip)
-        gate_act = jnp.dot(rows, gate[:, columns], preferred_element_type=jnp.float32)
-        gates[:, columns] = jax.nn.silu(gate_act)
-
-    later = iter(downs)
-    for i, copy in enumerate(ups):
+    def product(top, bottom, columns):
+        return jnp.dot(
+            moe_in[:, :cut], top[:, columns], preferred_element_type=jnp.float32
+        ) + jnp.dot(moe_in[:, cut:width], bottom[:, columns], preferred_element_type=jnp.float32)
+
+    strip = inner // 2
+    for i in range(2):
+        columns = slice(i * strip, (i + 1) * strip)
+        gate_act = product(gate_top, gate_bottom, columns)
+        up_act = product(up_top, up_bottom, columns)
+        units[:, columns] = (jax.nn.silu(gate_act) * up_act).astype(units.dtype)
+    for copy in downs:
         copy.wait()
-        next(later).start()
-        columns = slice(i * strip, (i + 1) * strip)
-        up_act = jnp.dot(rows, up_in[:, columns], preferred_element_type=jnp.float32)
-        units[:, columns] = (gates[:, columns] * up_act).astype(units.dtype)
-    strip = width // len(downs)
-    for i, copy in enumerate(downs):
-        copy.wait()
-        for ahead in later:
-            ahead.start()
-            break
-        columns = slice(i * strip, (i + 1) * strip)
+    for i in range(2):
+        columns = slice(i * cut, (i + 1) * cut)
         terms = weight * jnp.dot(
             units[...], down_in[:, columns], preferred_element_type=jnp.float32
         )
@@ -388,9 +381,9 @@
         sent[:, columns] = terms[half:].astype(sent.dtype)
 
 
-def run_expert(me, first, second, gate, up, down):
+def run_expert(me, first, second, gate, up, down, limit):
     rows = 2 * first.shape[0]
-    width, inner = gate.shape
+    inner, width = down.shape
     shape = (rows // 2, width)
     return pl.pallas_call(
         expert_kernel,
@@ -398,21 +391,16 @@
             jax.ShapeDtypeStruct(shape, jnp.float32),
             jax.ShapeDtypeStruct(shape, jnp.bfloat16),
         ),
-        in_specs=[IN_SMEM] + [IN_VMEM] * 3 + [IN_HBM] * 2,
+        in_specs=[IN_SMEM] + [IN_VMEM] * 6 + [IN_HBM],
         out_specs=(IN_VMEM, IN_VMEM),
         scratch_shapes=[
             pltpu.VMEM((rows, first.shape[1]), jnp.bfloat16),
-            pltpu.VMEM((rows, inner), jnp.float32),
             pltpu.VMEM((rows, inner), jnp.bfloat16),
-            pltpu.VMEM(up.shape, up.dtype),
             pltpu.VMEM(down.shape, down.dtype),
             pltpu.SemaphoreType.DMA((4,)),
-            pltpu.SemaphoreType.DMA((7,)),
         ],
-        compiler_params=pltpu.CompilerParams(
-            vmem_limit_bytes=4 * MIB + 4 * width * inner + 64 * rows * inner
-        ),
-    )(me, first, second, in_vmem(gate), in_hbm(up), in_hbm(down))
+        compiler_params=pltpu.CompilerParams(vmem_limit_bytes=limit + 2 * down.size),
+    )(me, first, second, *[in_vmem(w) for w in gate + up], in_hbm(down))
 
 
 def on_device(
@@ -447,24 +435,25 @@
     tail = jnp.pad(tail, ((0, 0), (0, LANES - tail.shape[1])))
 
     order = relative_order(bits)
+    limit = grant(rows_in, width)
     gate, up, down = gate_proj[0], up_proj[0], down_proj[0]
     if heads_dev % 8 == 0:
         kept, sent, value_up = attend(queries, latent_cache, cache_lengths, value_up, order, me)
         run = ep_size >> 2
         got = exchange(sent, 0)
-        kept, sent = deal((kept, got), 2, run)
+        kept, sent = deal((kept, got), 2, run, limit)
         got = exchange(sent, 1)
-        top, token = load(out_proj, sent, 0, 2)
-        parts = deal((kept, got), run, 1, (token,))
-        bottom, _ = load(out_proj, parts[0], 1, 2)
+        top, token = load(out_proj, sent, limit, 0)
+        parts = deal((kept, got), run, 1, limit, (token,))
+        bottom, _ = load(out_proj, parts[0], limit, 1)
         masks = order[:run]
         by_head = [parts[0]] + [trade(part, mask) for part, mask in zip(parts[1:], masks[1:])]
         held = [mask | x << 1 | core for mask in masks for x in range(2) for core in range(2)]
         row_of = jnp.array([held.index(s) * rows_dev + r for s in order for r in range(rows_dev)])
     else:
         out, _, value_up = attend(queries, latent_cache, cache_lengths, value_up, (), me)
-        top, _ = load(out_proj, value_up, 0, 2)
-        bottom, _ = load(out_proj, value_up, 1, 2)
+        top, _ = load(out_proj, value_up, limit, 0)
+        bottom, _ = load(out_proj, value_up, limit, 1)
         out = out.reshape(rows_dev, ep_size, heads_dev, latent).transpose(1, 0, 2, 3)
         by_head = [lax.all_to_all(out, "ep", split_axis=0, concat_axis=0, tiled=True)]
         by_head = [by_head[0].reshape(rows_in * heads_dev, latent)]
@@ -472,28 +461,38 @@
         row_of = row_of.reshape(-1)
     row_of = row_of.astype(jnp.int32)
     following = (gate,) if split_ways == 1 else ()
-    (kept, sent), carried = project(
-        by_head, row_of[:, None], value_up, top, bottom, hidden, tail, following
+    (kept, sent), halves = project(
+        by_head, row_of[:, None], value_up, top, bottom, hidden, tail, following, limit
     )
+    halves, later = list(halves), [(gate, 1), (up, 0), (up, 1)] if split_ways == 1 else []
+
+    def beside(value):
+        if not later:
+            return ()
+        source, part = later.pop(0)
+        half, token = load(source, value, limit, part)
+        halves.append(half)
+        return (token,)
+
 
     rows = rows_in // 2
     for bit in range(scatter_bits - 1):
         rows //= 2
-        (kept, sent), carried = combine(
-            halve_kernel, kept, exchange(sent, bit), rows, carried
-        )
+        kept, sent = combine(halve_kernel, kept, exchange(sent, bit), rows, limit)
     got = exchange(sent, scatter_bits - 1)
     for bit in range(scatter_bits, bits):
         swap = functools.partial(swap_kernel, rows_dev << (bits - 1 - bit))
-        (kept, sent), carried = combine(swap, kept, got, rows, carried)
+        kept, sent = combine(swap, kept, got, rows, limit, beside(sent))
         got = exchange(sent, bit)
-    (residual, moe_in), carried = norm(kept, got, norm_gain[None, :], rows_dev, carried)
+    residual, moe_in = norm(kept, got, norm_gain[None, :], rows_dev, limit, beside(sent))
     for bit in reversed(range(1, scatter_bits)):
-        moe_in, carried = stack(moe_in, exchange(moe_in, bit), carried)
+        moe_in = stack(moe_in, exchange(moe_in, bit), limit)
     other = exchange(moe_in, 0)
 
     if split_ways == 1:
-        kept, sent = run_expert(me[None], moe_in, other, carried[0], up, down)
+        while later:
+            beside(moe_in)
+        kept, sent = run_expert(me[None], moe_in, other, halves[:2], halves[2:], down, limit)
     else:
         moe_in = jnp.concatenate((moe_in, other), axis=0)
         expert = me % EXPERTS
@@ -520,7 +519,7 @@
     rows = rows_in // 2
     for bit in range(bits - 1):
         rows //= 2
-        (kept, sent), _ = combine(halve_kernel, kept, exchange(sent, bit), rows)
+        kept, sent = combine(halve_kernel, kept, exchange(sent, bit), rows, limit)
     routed = kept + exchange(sent, bits - 1).astype(jnp.float32)
     return (residual + routed).astype(jnp.bfloat16)
 

time: 82.3 us -> 82.6 us (level)
  Pallas kernels: 29 us -> 38.5 us
  waiting for transfers between devices: 36.6 us -> 27.8 us
    pallas_call x2 -> x5, Pallas kernels: 6.97 us -> 16.5 us  [load(): pl.pallas_call(functools.partial(load_kernel, part * rows), out_shape=(VM...]
    ppermute x15, waiting for transfers between devices: 36.6 us -> 27.8 us  [trade(): lax.ppermute(value, 'ep', [(i, i ^ mask) for i in range(lax.axis_size('ep...]
    pallas_call x9, Pallas kernels: 6.01 us -> 3.94 us  [the longest x1 3.45 us: project(): pl.pallas_call(functools.partial(project_kernel, width // 2, len(by_head)...]
    pallas_call x1, Pallas kernels: 11 us -> 13 us  [run_expert(): pl.pallas_call(expert_kernel, out_shape=(jax.ShapeDtypeStruct(shape, jnp....]
  transfers between devices with their start and end apart: 15 -> 15, of which waited for: 13 -> 13; matrix products, arithmetic and copies ran while one was open for 1% -> 1% of each run, Pallas kernels for 8% -> 20%
where the time goes in v3:
time: 82.6 us; the launch traced here: 82.4 us
  Pallas kernels  38.5 us (47%)
  waiting for transfers between devices  27.8 us (34%)
  starting transfers between devices  14.4 us (17%)
  other arithmetic  1.51 us (2%)
    ppermute x15, waiting for transfers between devices, trade(): lax.ppermute(value, 'ep', [(i, i ^ mask) for i in range(lax.axis_size('ep...  27.8 us
    pallas_call x5, Pallas kernels, load(): pl.pallas_call(functools.partial(load_kernel, part * rows), out_shape=(VM...  16.5 us
    ppermute x15, starting transfers between devices, trade(): lax.ppermute(value, 'ep', [(i, i ^ mask) for i in range(lax.axis_size('ep...  14.4 us
    pallas_call x1, Pallas kernels, run_expert(): pl.pallas_call(expert_kernel, out_shape=(jax.ShapeDtypeStruct(shape, jnp....  13 us
    pallas_call x1, Pallas kernels, attend(): pl.pallas_call(functools.partial(attend_kernel, order), out_shape=(VMEM_A...  4.98 us
    pallas_call x1, Pallas kernels, project(): pl.pallas_call(functools.partial(project_kernel, width // 2, len(by_head)...  3.45 us
  transfers between devices with their start and end apart: 15, of which 13 were waited for; matrix products, arithmetic and copies ran while one was open for 1% of the time, Pallas kernels for 20%

profile of v3, /device:TPU:0, one launch (start us, length us, event | category | flops | bytes accessed | tf_op | source)
XLA Modules:
  0.0 82.4 jit_solution(8675253262364857932)
XLA Ops:
  0.0 5.0 %shard_map.127 = (bf16[8,16,512]{2,1,0:T(8,128)(2,1)S(1)}, bf16[8,16,512]{2,1,0:T(8,128)(2,1)S(1)}, bf16[8,512,128]{2,1,0:T(8,128)(2,1)S(1)}) custom-call(s32[2]{0:T(128)} %lengths_hbm.1, s32[1]{0:T(128)} %bitcast.me, bf16[2,576,128]{2,1,0:T(8,128)(2,1)} %bitcast.14, bf16[2,576,2048]{2,1,0:T(8,128)(2,1)} %bitcast.13, bf16[8,512,128]{2,1,0:T(8,128)(2,1)} %value_up.1), custom_call_target="tpu_custom_call" | custom-call | tf_op jit(solution)/shard_map/pallas_call | solution.py:155
  5.0 0.5 collective-permute-start
  5.5 0.8 select_reduce_fusion
  6.3 0.2 collective-permute-done.refs_1_
  6.5 2.9 %collective-permute-start.1 = (bf16[8,16,512]{2,1,0:T(8,128)(2,1)S(1)}, bf16[8,16,512]{2,1,0:T(8,128)(2,1)S(1)}, u32[]{:S(2)}, u32[]{:S(2)}) collective-permute-start(bf16[8,16,512]{2,1,0:T(8,128)(2,1)S(1)} %get-tuple-element.45.after), channel_id=1, source_target_pairs={{0,2},{1,3},{2,0},{3,1},{4,6},{5,7},{6,4},{7,5},{8,10},{9,11},{10,... | collective-permute-start | bytes 393224 | tf_op jit(solution)/shard_map/ppermute | solution.py:22
  9.4 3.2 %shard_map.129 = (bf16[512,7168]{1,0:T(8,128)(2,1)S(1)}, f32[8,128]{1,0:T(8,128)S(1)}) custom-call(bf16[1024,7168]{1,0:T(8,128)(2,1)} %source.3, bf16[8,16,512]{2,1,0:T(8,128)(2,1)S(1)} %get-tuple-element.45.after), custom_call_target="tpu_custom_call" | custom-call | bytes 14680064 | tf_op jit(solution)/shard_map/pallas_call | solution.py:67
  12.6 0.6 collective-permute-done.1.refs_1_
  13.3 2.9 %collective-permute-start.2 = (bf16[4,16,512]{2,1,0:T(8,128)(2,1)S(1)}, bf16[4,16,512]{2,1,0:T(8,128)(2,1)S(1)}, u32[]{:S(2)}, u32[]{:S(2)}) collective-permute-start(bf16[4,16,512]{2,1,0:T(8,128)(2,1)S(1)} %get-tuple-element.48), channel_id=1, source_target_pairs={{0,8},{1,9},{2,10},{3,11},{4,12},{5,13},{6,14},{7,15},{8,0},{9,1},... | collective-permute-start | bytes 196616 | tf_op jit(solution)/shard_map/ppermute | solution.py:22
  16.2 1.6 %collective-permute-start.3 = (bf16[4,16,512]{2,1,0:T(8,128)(2,1)S(1)}, bf16[4,16,512]{2,1,0:T(8,128)(2,1)S(1)}, u32[]{:S(2)}, u32[]{:S(2)}) collective-permute-start(bf16[4,16,512]{2,1,0:T(8,128)(2,1)S(1)} %get-tuple-element.49), channel_id=1, source_target_pairs={{0,4},{1,5},{2,6},{3,7},{4,0},{5,1},{6,2},{7,3},{8,12},{9,13},{10,... | collective-permute-start | bytes 196616 | tf_op jit(solution)/shard_map/ppermute | solution.py:22
  17.7 0.0 collective-permute-start.4
  17.7 0.1 select_maximum_fusion.refs_9_
  17.8 0.0 copy-start
  17.8 0.0 copy-start.2
  17.8 3.8 %shard_map.131 = (bf16[512,7168]{1,0:T(8,128)(2,1)S(1)}, f32[8,128]{1,0:T(8,128)}) custom-call(bf16[1024,7168]{1,0:T(8,128)(2,1)} %source.3, bf16[4,16,512]{2,1,0:T(8,128)(2,1)S(1)} %get-tuple-element.47.after.refs_0_), custom_call_target="tpu_custom_call" | custom-call | bytes 14680064 | tf_op jit(solution)/shard_map/pallas_call | solution.py:67
  21.6 0.0 collective-permute-done.2.refs_1_
  21.6 0.0 collective-permute-done.3.refs_2_
  21.6 2.2 %collective-permute-done.4.refs_3_ = bf16[4,16,512]{2,1,0:T(8,128)(2,1)S(1)} collective-permute-done((bf16[4,16,512]{2,1,0:T(8,128)(2,1)S(1)}, bf16[4,16,512]{2,1,0:T(8,128)(2,1)S(1)}, u32[]{:S(2)}, u32[]{:S(2)}) %collective-permute-start.4) | collective-permute-done | bytes 65568 | tf_op jit(solution)/shard_map/ppermute | solution.py:22
  23.8 0.0 copy-done
  23.8 0.0 copy-done.2
  23.8 3.4 %shard_map.132 = (f32[16,7296]{1,0:T(8,128)S(1)}, bf16[16,7296]{1,0:T(8,128)(2,1)S(1)}, bf16[3584,1024]{1,0:T(8,128)(2,1)S(1)}) custom-call(bf16[4,16,512]{2,1,0:T(8,128)(2,1)S(1)} %get-tuple-element.47.after.refs_0_, bf16[4,16,512]{2,1,0:T(8,128)(2,1)S(1)} %collective-permute-done.2.refs_1_, bf16[4,16,512]{2,1,0:T(8,128)(2,1)S(1)} %collective-permute-done.3.refs_2_, ...), custom_call_target="tpu_custom_call" | custom-call | tf_op jit(solution)/shard_map/pallas_call | solution.py:259
  27.3 0.1 collective-permute-start.5
  27.4 1.5 %collective-permute-done.5.refs_1_ = bf16[16,7296]{1,0:T(8,128)(2,1)S(1)} collective-permute-done((bf16[16,7296]{1,0:T(8,128)(2,1)S(1)}, bf16[16,7296]{1,0:T(8,128)(2,1)S(1)}, u32[]{:S(2)}, u32[]{:S(2)}) %collective-permute-start.5) | collective-permute-done | bytes 233504 | tf_op jit(solution)/shard_map/ppermute | solution.py:22
  28.8 0.1 shard_map.133
  28.9 1.6 %collective-permute-start.6 = (bf16[8,7296]{1,0:T(8,128)(2,1)S(1)}, bf16[8,7296]{1,0:T(8,128)(2,1)S(1)}, u32[]{:S(2)}, u32[]{:S(2)}) collective-permute-start(bf16[8,7296]{1,0:T(8,128)(2,1)S(1)} %get-tuple-element.57.after), channel_id=1, source_target_pairs={{0,2},{1,3},{2,0},{3,1},{4,6},{5,7},{6,4},{7,5},{8,10},{9,11},{10,... | collective-permute-start | bytes 350216 | tf_op jit(solution)/shard_map/ppermute | solution.py:22
  30.5 3.2 %shard_map.134 = (bf16[3584,1024]{1,0:T(8,128)(2,1)S(1)}, f32[8,128]{1,0:T(8,128)S(1)}) custom-call(bf16[7168,1024]{1,0:T(8,128)(2,1)} %bitcast.9, bf16[8,7296]{1,0:T(8,128)(2,1)S(1)} %get-tuple-element.57.after), custom_call_target="tpu_custom_call" | custom-call | bytes 14680064 | tf_op jit(solution)/shard_map/pallas_call | solution.py:67
  33.7 0.5 collective-permute-done.6.refs_1_
  34.2 0.1 collective-permute-start.7
  34.3 3.2 %shard_map.136 = (bf16[3584,1024]{1,0:T(8,128)(2,1)S(1)}, f32[8,128]{1,0:T(8,128)S(1)}) custom-call(bf16[7168,1024]{1,0:T(8,128)(2,1)} %bitcast.10, bf16[8,7296]{1,0:T(8,128)(2,1)S(1)} %get-tuple-element.60.after), custom_call_target="tpu_custom_call" | custom-call | bytes 14680064 | tf_op jit(solution)/shard_map/pallas_call | solution.py:67
  37.5 1.6 %collective-permute-done.7.refs_1_ = bf16[8,7296]{1,0:T(8,128)(2,1)S(1)} collective-permute-done((bf16[8,7296]{1,0:T(8,128)(2,1)S(1)}, bf16[8,7296]{1,0:T(8,128)(2,1)S(1)}, u32[]{:S(2)}, u32[]{:S(2)}) %collective-permute-start.7) | collective-permute-done | bytes 116768 | tf_op jit(solution)/shard_map/ppermute | solution.py:22
  39.1 0.1 shard_map.137
  39.2 0.0 copy-start.1
  39.2 0.9 %collective-permute-start.8 = (bf16[8,7296]{1,0:T(8,128)(2,1)S(1)}, bf16[8,7296]{1,0:T(8,128)(2,1)S(1)}, u32[]{:S(2)}, u32[]{:S(2)}) collective-permute-start(bf16[8,7296]{1,0:T(8,128)(2,1)S(1)} %get-tuple-element.63.after), channel_id=1, source_target_pairs={{0,8},{1,9},{2,10},{3,11},{4,12},{5,13},{6,14},{7,15},{8,0},{9,1},... | collective-permute-start | bytes 350216 | tf_op jit(solution)/shard_map/ppermute | solution.py:22
  40.0 3.2 %shard_map.138 = (bf16[3584,1024]{1,0:T(8,128)(2,1)S(1)}, f32[8,128]{1,0:T(8,128)S(1)}) custom-call(bf16[7168,1024]{1,0:T(8,128)(2,1)} %bitcast.11, bf16[8,7296]{1,0:T(8,128)(2,1)S(1)} %get-tuple-element.63.after), custom_call_target="tpu_custom_call" | custom-call | bytes 14680064 | tf_op jit(solution)/shard_map/pallas_call | solution.py:67
  43.2 2.8 %collective-permute-done.8.refs_1_ = bf16[8,7296]{1,0:T(8,128)(2,1)S(1)} collective-permute-done((bf16[8,7296]{1,0:T(8,128)(2,1)S(1)}, bf16[8,7296]{1,0:T(8,128)(2,1)S(1)}, u32[]{:S(2)}, u32[]{:S(2)}) %collective-permute-start.8) | collective-permute-done | bytes 116768 | tf_op jit(solution)/shard_map/ppermute | solution.py:22
  46.1 0.0 copy-done.1
  46.1 0.2 shard_map.139
  46.3 1.6 %collective-permute-start.9 = (bf16[8,7296]{1,0:T(8,128)(2,1)S(1)}, bf16[8,7296]{1,0:T(8,128)(2,1)S(1)}, u32[]{:S(2)}, u32[]{:S(2)}) collective-permute-start(bf16[8,7296]{1,0:T(8,128)(2,1)S(1)} %get-tuple-element.66.refs_0_), channel_id=1, source_target_pairs={{0,2},{1,3},{2,0},{3,1},{4,6},{5,7},{6,4},{7,5},{8,10},{9,11},{10,... | collective-permute-start | bytes 350216 | tf_op jit(solution)/shard_map/ppermute | solution.py:22
  47.8 3.3 %collective-permute-done.9.refs_1_ = bf16[8,7296]{1,0:T(8,128)(2,1)S(1)} collective-permute-done((bf16[8,7296]{1,0:T(8,128)(2,1)S(1)}, bf16[8,7296]{1,0:T(8,128)(2,1)S(1)}, u32[]{:S(2)}, u32[]{:S(2)}) %collective-permute-start.9) | collective-permute-done | bytes 116768 | tf_op jit(solution)/shard_map/ppermute | solution.py:22
  51.2 0.1 collective-permute-start.10
  51.2 1.5 %collective-permute-done.10.second = bf16[16,7296]{1,0:T(8,128)(2,1)S(1)} collective-permute-done((bf16[16,7296]{1,0:T(8,128)(2,1)S(1)}, bf16[16,7296]{1,0:T(8,128)(2,1)S(1)}, u32[]{:S(2)}, u32[]{:S(2)}) %collective-permute-start.10) | collective-permute-done | bytes 233504 | tf_op jit(solution)/shard_map/ppermute | solution.py:22
  52.7 13.0 %shard_map.141 = (f32[16,7168]{1,0:T(8,128)S(1)}, bf16[16,7168]{1,0:T(8,128)(2,1)S(1)}) custom-call(s32[1]{0:T(128)} %bitcast.me, bf16[16,7296]{1,0:T(8,128)(2,1)S(1)} %shard_map.140.first, bf16[16,7296]{1,0:T(8,128)(2,1)S(1)} %collective-permute-done.10.second, bf16[3584,1024]{1,0:T(8,128)(2,1)S(1)} %get-tuple-element.67.gate_top, ...), custom_call_target="tpu_custom_call" | custom-call | tf_op jit(solution)/shard_map/pallas_call | solution.py:388
  65.7 0.2 collective-permute-start.11
  65.9 1.4 %collective-permute-done.11.refs_1_ = bf16[16,7168]{1,0:T(8,128)(2,1)S(1)} collective-permute-done((bf16[16,7168]{1,0:T(8,128)(2,1)S(1)}, bf16[16,7168]{1,0:T(8,128)(2,1)S(1)}, u32[]{:S(2)}, u32[]{:S(2)}) %collective-permute-start.11) | collective-permute-done | bytes 229408 | tf_op jit(solution)/shard_map/ppermute | solution.py:22
  67.3 1.6 %collective-permute-start.12 = (bf16[8,7168]{1,0:T(8,128)(2,1)S(1)}, bf16[8,7168]{1,0:T(8,128)(2,1)S(1)}, u32[]{:S(2)}, u32[]{:S(2)}) collective-permute-start(bf16[8,7168]{1,0:T(8,128)(2,1)S(1)} %get-tuple-element.74), channel_id=1, source_target_pairs={{0,2},{1,3},{2,0},{3,1},{4,6},{5,7},{6,4},{7,5},{8,10},{9,11},{10,... | collective-permute-start | bytes 344072 | tf_op jit(solution)/shard_map/ppermute | solution.py:22
  68.9 3.7 %collective-permute-done.12.refs_1_ = bf16[8,7168]{1,0:T(8,128)(2,1)S(1)} collective-permute-done((bf16[8,7168]{1,0:T(8,128)(2,1)S(1)}, bf16[8,7168]{1,0:T(8,128)(2,1)S(1)}, u32[]{:S(2)}, u32[]{:S(2)}) %collective-permute-start.12) | collective-permute-done | bytes 114720 | tf_op jit(solution)/shard_map/ppermute | solution.py:22
  72.6 0.1 collective-permute-start.13
  72.7 4.2 %collective-permute-done.13.refs_1_ = bf16[4,7168]{1,0:T(4,128)(2,1)S(1)} collective-permute-done((bf16[4,7168]{1,0:T(4,128)(2,1)S(1)}, bf16[4,7168]{1,0:T(4,128)(2,1)S(1)}, u32[]{:S(2)}, u32[]{:S(2)}) %collective-permute-start.13) | collective-permute-done | bytes 57376 | tf_op jit(solution)/shard_map/ppermute | solution.py:22
  76.9 0.4 collective-permute-start.14
  77.3 4.4 %collective-permute-done.14 = bf16[2,7168]{1,0:T(2,128)(2,1)S(1)} collective-permute-done((bf16[2,7168]{1,0:T(2,128)(2,1)S(1)}, bf16[2,7168]{1,0:T(2,128)(2,1)S(1)}, u32[]{:S(2)}, u32[]{:S(2)}) %collective-permute-start.14) | collective-permute-done | bytes 28704 | tf_op jit(solution)/shard_map/ppermute | solution.py:22
  81.7 0.7 add_convert_fusion
  (8 shorter events, 0.2 us)
Async XLA Ops:
  5.0 1.5 %collective-permute-start = (bf16[8,16,512]{2,1,0:T(8,128)(2,1)S(1)}, bf16[8,16,512]{2,1,0:T(8,128)(2,1)S(1)}, u32[]{:S(2)}, u32[]{:S(2)}) collective-permute-start(bf16[8,16,512]{2,1,0:T(8,128)(2,1)S(1)} %get-tuple-element.43), channel_id=1, source_target_pairs={{0,1},{1,0},{2,3},{3,2},{4,5},{5,4},{6,7},{7,6},{8,9},{9,8},{10,11... | collective-permute-start | bytes 393224 | tf_op jit(solution)/shard_map/ppermute | solution.py:22
  6.5 6.7 %collective-permute-start.1 = (bf16[8,16,512]{2,1,0:T(8,128)(2,1)S(1)}, bf16[8,16,512]{2,1,0:T(8,128)(2,1)S(1)}, u32[]{:S(2)}, u32[]{:S(2)}) collective-permute-start(bf16[8,16,512]{2,1,0:T(8,128)(2,1)S(1)} %get-tuple-element.45.after), channel_id=1, source_target_pairs={{0,2},{1,3},{2,0},{3,1},{4,6},{5,7},{6,4},{7,5},{8,10},{9,11},{10,... | collective-permute-start | bytes 393224 | tf_op jit(solution)/shard_map/ppermute | solution.py:22
  13.3 8.4 %collective-permute-start.2 = (bf16[4,16,512]{2,1,0:T(8,128)(2,1)S(1)}, bf16[4,16,512]{2,1,0:T(8,128)(2,1)S(1)}, u32[]{:S(2)}, u32[]{:S(2)}) collective-permute-start(bf16[4,16,512]{2,1,0:T(8,128)(2,1)S(1)} %get-tuple-element.48), channel_id=1, source_target_pairs={{0,8},{1,9},{2,10},{3,11},{4,12},{5,13},{6,14},{7,15},{8,0},{9,1},... | collective-permute-start | bytes 196616 | tf_op jit(solution)/shard_map/ppermute | solution.py:22
  16.2 5.5 %collective-permute-start.3 = (bf16[4,16,512]{2,1,0:T(8,128)(2,1)S(1)}, bf16[4,16,512]{2,1,0:T(8,128)(2,1)S(1)}, u32[]{:S(2)}, u32[]{:S(2)}) collective-permute-start(bf16[4,16,512]{2,1,0:T(8,128)(2,1)S(1)} %get-tuple-element.49), channel_id=1, source_target_pairs={{0,4},{1,5},{2,6},{3,7},{4,0},{5,1},{6,2},{7,3},{8,12},{9,13},{10,... | collective-permute-start | bytes 196616 | tf_op jit(solution)/shard_map/ppermute | solution.py:22
  17.7 6.1 %collective-permute-start.4 = (bf16[4,16,512]{2,1,0:T(8,128)(2,1)S(1)}, bf16[4,16,512]{2,1,0:T(8,128)(2,1)S(1)}, u32[]{:S(2)}, u32[]{:S(2)}) collective-permute-start(bf16[4,16,512]{2,1,0:T(8,128)(2,1)S(1)} %get-tuple-element.50), channel_id=1, source_target_pairs={{0,12},{1,13},{2,14},{3,15},{4,8},{5,9},{6,10},{7,11},{8,4},{9,5},... | collective-permute-start | bytes 196616 | tf_op jit(solution)/shard_map/ppermute | solution.py:22
  17.8 6.0 %copy-start = (bf16[2,7168]{1,0:T(2,128)(2,1)S(1)}, bf16[2,7168]{1,0:T(2,128)(2,1)}, u32[]{:S(2)}) copy-start(bf16[2,7168]{1,0:T(2,128)(2,1)} %refs_8_.1) | copy-start | bytes 86020
  17.8 6.0 %copy-start.2 = (s32[32,1]{1,0:T(8,128)S(1)}, s32[32,1]{1,0:T(8,128)}, u32[]{:S(2)}) copy-start(s32[32,1]{1,0:T(8,128)} %constant.23.refs_4_) | copy-start | bytes 388
  27.3 1.6 %collective-permute-start.5 = (bf16[16,7296]{1,0:T(8,128)(2,1)S(1)}, bf16[16,7296]{1,0:T(8,128)(2,1)S(1)}, u32[]{:S(2)}, u32[]{:S(2)}) collective-permute-start(bf16[16,7296]{1,0:T(8,128)(2,1)S(1)} %get-tuple-element.55), channel_id=1, source_target_pairs={{0,1},{1,0},{2,3},{3,2},{4,5},{5,4},{6,7},{7,6},{8,9},{9,8},{10,11... | collective-permute-start | bytes 700424 | tf_op jit(solution)/shard_map/ppermute | solution.py:22
  28.9 5.3 %collective-permute-start.6 = (bf16[8,7296]{1,0:T(8,128)(2,1)S(1)}, bf16[8,7296]{1,0:T(8,128)(2,1)S(1)}, u32[]{:S(2)}, u32[]{:S(2)}) collective-permute-start(bf16[8,7296]{1,0:T(8,128)(2,1)S(1)} %get-tuple-element.57.after), channel_id=1, source_target_pairs={{0,2},{1,3},{2,0},{3,1},{4,6},{5,7},{6,4},{7,5},{8,10},{9,11},{10,... | collective-permute-start | bytes 350216 | tf_op jit(solution)/shard_map/ppermute | solution.py:22
  34.2 4.9 %collective-permute-start.7 = (bf16[8,7296]{1,0:T(8,128)(2,1)S(1)}, bf16[8,7296]{1,0:T(8,128)(2,1)S(1)}, u32[]{:S(2)}, u32[]{:S(2)}) collective-permute-start(bf16[8,7296]{1,0:T(8,128)(2,1)S(1)} %get-tuple-element.60.after), channel_id=1, source_target_pairs={{0,4},{1,5},{2,6},{3,7},{4,0},{5,1},{6,2},{7,3},{8,12},{9,13},{10,... | collective-permute-start | bytes 350216 | tf_op jit(solution)/shard_map/ppermute | solution.py:22
  39.2 6.9 %copy-start.1 = (f32[7168]{0:T(1024)S(1)}, f32[7168]{0:T(1024)}, u32[]{:S(2)}) copy-start(f32[7168]{0:T(1024)} %param.19) | copy-start | bytes 86020
  39.2 6.9 %collective-permute-start.8 = (bf16[8,7296]{1,0:T(8,128)(2,1)S(1)}, bf16[8,7296]{1,0:T(8,128)(2,1)S(1)}, u32[]{:S(2)}, u32[]{:S(2)}) collective-permute-start(bf16[8,7296]{1,0:T(8,128)(2,1)S(1)} %get-tuple-element.63.after), channel_id=1, source_target_pairs={{0,8},{1,9},{2,10},{3,11},{4,12},{5,13},{6,14},{7,15},{8,0},{9,1},... | collective-permute-start | bytes 350216 | tf_op jit(solution)/shard_map/ppermute | solution.py:22
  46.3 4.9 %collective-permute-start.9 = (bf16[8,7296]{1,0:T(8,128)(2,1)S(1)}, bf16[8,7296]{1,0:T(8,128)(2,1)S(1)}, u32[]{:S(2)}, u32[]{:S(2)}) collective-permute-start(bf16[8,7296]{1,0:T(8,128)(2,1)S(1)} %get-tuple-element.66.refs_0_), channel_id=1, source_target_pairs={{0,2},{1,3},{2,0},{3,1},{4,6},{5,7},{6,4},{7,5},{8,10},{9,11},{10,... | collective-permute-start | bytes 350216 | tf_op jit(solution)/shard_map/ppermute | solution.py:22
  51.2 1.6 %collective-permute-start.10 = (bf16[16,7296]{1,0:T(8,128)(2,1)S(1)}, bf16[16,7296]{1,0:T(8,128)(2,1)S(1)}, u32[]{:S(2)}, u32[]{:S(2)}) collective-permute-start(bf16[16,7296]{1,0:T(8,128)(2,1)S(1)} %shard_map.140.first), channel_id=1, source_target_pairs={{0,1},{1,0},{2,3},{3,2},{4,5},{5,4},{6,7},{7,6},{8,9},{9,8},{10,11... | collective-permute-start | bytes 700424 | tf_op jit(solution)/shard_map/ppermute | solution.py:22
  65.7 1.6 %collective-permute-start.11 = (bf16[16,7168]{1,0:T(8,128)(2,1)S(1)}, bf16[16,7168]{1,0:T(8,128)(2,1)S(1)}, u32[]{:S(2)}, u32[]{:S(2)}) collective-permute-start(bf16[16,7168]{1,0:T(8,128)(2,1)S(1)} %get-tuple-element.72), channel_id=1, source_target_pairs={{0,1},{1,0},{2,3},{3,2},{4,5},{5,4},{6,7},{7,6},{8,9},{9,8},{10,11... | collective-permute-start | bytes 688136 | tf_op jit(solution)/shard_map/ppermute | solution.py:22
  67.3 5.3 %collective-permute-start.12 = (bf16[8,7168]{1,0:T(8,128)(2,1)S(1)}, bf16[8,7168]{1,0:T(8,128)(2,1)S(1)}, u32[]{:S(2)}, u32[]{:S(2)}) collective-permute-start(bf16[8,7168]{1,0:T(8,128)(2,1)S(1)} %get-tuple-element.74), channel_id=1, source_target_pairs={{0,2},{1,3},{2,0},{3,1},{4,6},{5,7},{6,4},{7,5},{8,10},{9,11},{10,... | collective-permute-start | bytes 344072 | tf_op jit(solution)/shard_map/ppermute | solution.py:22
  72.6 4.2 %collective-permute-start.13 = (bf16[4,7168]{1,0:T(4,128)(2,1)S(1)}, bf16[4,7168]{1,0:T(4,128)(2,1)S(1)}, u32[]{:S(2)}, u32[]{:S(2)}) collective-permute-start(bf16[4,7168]{1,0:T(4,128)(2,1)S(1)} %get-tuple-element.76), channel_id=1, source_target_pairs={{0,4},{1,5},{2,6},{3,7},{4,0},{5,1},{6,2},{7,3},{8,12},{9,13},{10,... | collective-permute-start | bytes 172040 | tf_op jit(solution)/shard_map/ppermute | solution.py:22
  76.9 4.8 %collective-permute-start.14 = (bf16[2,7168]{1,0:T(2,128)(2,1)S(1)}, bf16[2,7168]{1,0:T(2,128)(2,1)S(1)}, u32[]{:S(2)}, u32[]{:S(2)}) collective-permute-start(bf16[2,7168]{1,0:T(2,128)(2,1)S(1)} %get-tuple-element.78), channel_id=1, source_target_pairs={{0,8},{1,9},{2,10},{3,11},{4,12},{5,13},{6,14},{7,15},{8,0},{9,1},... | collective-permute-start | bytes 86024 | tf_op jit(solution)/shard_map/ppermute | solution.py:22

commit v4 on v3

--- a/solution.py
+++ b/solution.py
@@ -365,15 +365,19 @@
         ) + jnp.dot(moe_in[:, cut:width], bottom[:, columns], preferred_element_type=jnp.float32)
 
     strip = inner // 2
-    for i in range(2):
-        columns = slice(i * strip, (i + 1) * strip)
+
+    @pl.loop(0, 2)
+    def _(i):
+        columns = pl.ds(pl.multiple_of(i * strip, strip), strip)
         gate_act = product(gate_top, gate_bottom, columns)
         up_act = product(up_top, up_bottom, columns)
         units[:, columns] = (jax.nn.silu(gate_act) * up_act).astype(units.dtype)
     for copy in downs:
         copy.wait()
-    for i in range(2):
-        columns = slice(i * cut, (i + 1) * cut)
+
+    @pl.loop(0, 2)
+    def _(i):
+        columns = pl.ds(pl.multiple_of(i * cut, cut), cut)
         terms = weight * jnp.dot(
             units[...], down_in[:, columns], preferred_element_type=jnp.float32
         )

time: 82.6 us -> 77.9 us (0.943)
  Pallas kernels: 38.5 us -> 33.8 us
    pallas_call x1, Pallas kernels: 13 us -> 8.32 us  [run_expert(): pl.pallas_call(expert_kernel, out_shape=(jax.ShapeDtypeStruct(shape, jnp....]
  transfers between devices with their start and end apart: 15 -> 15, of which waited for: 13 -> 13; matrix products, arithmetic and copies ran while one was open for 1% -> 1% of each run, Pallas kernels for 20% -> 21%
where the time goes in v4:
time: 77.9 us; the launch traced here: 77.7 us
  Pallas kernels  33.8 us (43%)
  waiting for transfers between devices  27.8 us (36%)
  starting transfers between devices  14.4 us (18%)
  other arithmetic  1.51 us (2%)
    ppermute x15, waiting for transfers between devices, trade(): lax.ppermute(value, 'ep', [(i, i ^ mask) for i in range(lax.axis_size('ep...  27.8 us
    pallas_call x5, Pallas kernels, load(): pl.pallas_call(functools.partial(load_kernel, part * rows), out_shape=(VM...  16.5 us
    ppermute x15, starting transfers between devices, trade(): lax.ppermute(value, 'ep', [(i, i ^ mask) for i in range(lax.axis_size('ep...  14.4 us
    pallas_call x1, Pallas kernels, run_expert(): pl.pallas_call(expert_kernel, out_shape=(jax.ShapeDtypeStruct(shape, jnp....  8.32 us
    pallas_call x1, Pallas kernels, attend(): pl.pallas_call(functools.partial(attend_kernel, order), out_shape=(VMEM_A...  4.98 us
    pallas_call x1, Pallas kernels, project(): pl.pallas_call(functools.partial(project_kernel, width // 2, len(by_head)...  3.45 us
  transfers between devices with their start and end apart: 15, of which 13 were waited for; matrix products, arithmetic and copies ran while one was open for 1% of the time, Pallas kernels for 21%

profile of v4, /device:TPU:0, one launch (start us, length us, event | category | flops | bytes accessed | tf_op | source)
XLA Modules:
  0.0 77.7 jit_solution(4210961995244977806)
XLA Ops:
  0.0 5.0 %shard_map.127 = (bf16[8,16,512]{2,1,0:T(8,128)(2,1)S(1)}, bf16[8,16,512]{2,1,0:T(8,128)(2,1)S(1)}, bf16[8,512,128]{2,1,0:T(8,128)(2,1)S(1)}) custom-call(s32[2]{0:T(128)} %lengths_hbm.1, s32[1]{0:T(128)} %bitcast.me, bf16[2,576,128]{2,1,0:T(8,128)(2,1)} %bitcast.14, bf16[2,576,2048]{2,1,0:T(8,128)(2,1)} %bitcast.13, bf16[8,512,128]{2,1,0:T(8,128)(2,1)} %value_up.1), custom_call_target="tpu_custom_call" | custom-call | tf_op jit(solution)/shard_map/pallas_call | solution.py:155
  5.0 0.5 collective-permute-start
  5.5 0.8 %select_reduce_fusion = f32[2,16]{1,0:T(2,128)S(1)} fusion(f32[2,8]{1,0:T(2,128)} %param.21, s32[2,8]{1,0:T(2,128)} %param.20), kind=kLoop, calls=%fused_computation.1 | loop fusion | flops 736 | bytes 256 | tf_op jit(solution)/shard_map/reduce_sum | solution.py:435
  6.3 0.2 collective-permute-done.refs_1_
  6.5 2.9 %collective-permute-start.1 = (bf16[8,16,512]{2,1,0:T(8,128)(2,1)S(1)}, bf16[8,16,512]{2,1,0:T(8,128)(2,1)S(1)}, u32[]{:S(2)}, u32[]{:S(2)}) collective-permute-start(bf16[8,16,512]{2,1,0:T(8,128)(2,1)S(1)} %get-tuple-element.45.after), channel_id=1, source_target_pairs={{0,2},{1,3},{2,0},{3,1},{4,6},{5,7},{6,4},{7,5},{8,10},{9,11},{10,... | collective-permute-start | bytes 393224 | tf_op jit(solution)/shard_map/ppermute | solution.py:22
  9.4 3.2 %shard_map.129 = (bf16[512,7168]{1,0:T(8,128)(2,1)S(1)}, f32[8,128]{1,0:T(8,128)S(1)}) custom-call(bf16[1024,7168]{1,0:T(8,128)(2,1)} %source.3, bf16[8,16,512]{2,1,0:T(8,128)(2,1)S(1)} %get-tuple-element.45.after), custom_call_target="tpu_custom_call" | custom-call | bytes 14680064 | tf_op jit(solution)/shard_map/pallas_call | solution.py:67
  12.6 0.6 collective-permute-done.1.refs_1_
  13.3 2.9 %collective-permute-start.2 = (bf16[4,16,512]{2,1,0:T(8,128)(2,1)S(1)}, bf16[4,16,512]{2,1,0:T(8,128)(2,1)S(1)}, u32[]{:S(2)}, u32[]{:S(2)}) collective-permute-start(bf16[4,16,512]{2,1,0:T(8,128)(2,1)S(1)} %get-tuple-element.48), channel_id=1, source_target_pairs={{0,8},{1,9},{2,10},{3,11},{4,12},{5,13},{6,14},{7,15},{8,0},{9,1},... | collective-permute-start | bytes 196616 | tf_op jit(solution)/shard_map/ppermute | solution.py:22
  16.2 1.6 %collective-permute-start.3 = (bf16[4,16,512]{2,1,0:T(8,128)(2,1)S(1)}, bf16[4,16,512]{2,1,0:T(8,128)(2,1)S(1)}, u32[]{:S(2)}, u32[]{:S(2)}) collective-permute-start(bf16[4,16,512]{2,1,0:T(8,128)(2,1)S(1)} %get-tuple-element.49), channel_id=1, source_target_pairs={{0,4},{1,5},{2,6},{3,7},{4,0},{5,1},{6,2},{7,3},{8,12},{9,13},{10,... | collective-permute-start | bytes 196616 | tf_op jit(solution)/shard_map/ppermute | solution.py:22
  17.7 0.0 collective-permute-start.4
  17.7 0.1 select_maximum_fusion.refs_9_
  17.8 0.0 copy-start
  17.8 0.0 copy-start.2
  17.8 3.8 %shard_map.131 = (bf16[512,7168]{1,0:T(8,128)(2,1)S(1)}, f32[8,128]{1,0:T(8,128)}) custom-call(bf16[1024,7168]{1,0:T(8,128)(2,1)} %source.3, bf16[4,16,512]{2,1,0:T(8,128)(2,1)S(1)} %get-tuple-element.47.after.refs_0_), custom_call_target="tpu_custom_call" | custom-call | bytes 14680064 | tf_op jit(solution)/shard_map/pallas_call | solution.py:67
  21.6 0.0 collective-permute-done.2.refs_1_
  21.6 0.0 collective-permute-done.3.refs_2_
  21.6 2.2 %collective-permute-done.4.refs_3_ = bf16[4,16,512]{2,1,0:T(8,128)(2,1)S(1)} collective-permute-done((bf16[4,16,512]{2,1,0:T(8,128)(2,1)S(1)}, bf16[4,16,512]{2,1,0:T(8,128)(2,1)S(1)}, u32[]{:S(2)}, u32[]{:S(2)}) %collective-permute-start.4) | collective-permute-done | bytes 65568 | tf_op jit(solution)/shard_map/ppermute | solution.py:22
  23.8 0.0 copy-done
  23.8 0.0 copy-done.2
  23.8 3.4 %shard_map.132 = (f32[16,7296]{1,0:T(8,128)S(1)}, bf16[16,7296]{1,0:T(8,128)(2,1)S(1)}, bf16[3584,1024]{1,0:T(8,128)(2,1)S(1)}) custom-call(bf16[4,16,512]{2,1,0:T(8,128)(2,1)S(1)} %get-tuple-element.47.after.refs_0_, bf16[4,16,512]{2,1,0:T(8,128)(2,1)S(1)} %collective-permute-done.2.refs_1_, bf16[4,16,512]{2,1,0:T(8,128)(2,1)S(1)} %collective-permute-done.3.refs_2_, ...), custom_call_target="tpu_custom_call" | custom-call | tf_op jit(solution)/shard_map/pallas_call | solution.py:259
  27.3 0.1 collective-permute-start.5
  27.4 1.5 %collective-permute-done.5.refs_1_ = bf16[16,7296]{1,0:T(8,128)(2,1)S(1)} collective-permute-done((bf16[16,7296]{1,0:T(8,128)(2,1)S(1)}, bf16[16,7296]{1,0:T(8,128)(2,1)S(1)}, u32[]{:S(2)}, u32[]{:S(2)}) %collective-permute-start.5) | collective-permute-done | bytes 233504 | tf_op jit(solution)/shard_map/ppermute | solution.py:22
  28.8 0.1 shard_map.133
  28.9 1.6 %collective-permute-start.6 = (bf16[8,7296]{1,0:T(8,128)(2,1)S(1)}, bf16[8,7296]{1,0:T(8,128)(2,1)S(1)}, u32[]{:S(2)}, u32[]{:S(2)}) collective-permute-start(bf16[8,7296]{1,0:T(8,128)(2,1)S(1)} %get-tuple-element.57.after), channel_id=1, source_target_pairs={{0,2},{1,3},{2,0},{3,1},{4,6},{5,7},{6,4},{7,5},{8,10},{9,11},{10,... | collective-permute-start | bytes 350216 | tf_op jit(solution)/shard_map/ppermute | solution.py:22
  30.5 3.2 %shard_map.134 = (bf16[3584,1024]{1,0:T(8,128)(2,1)S(1)}, f32[8,128]{1,0:T(8,128)S(1)}) custom-call(bf16[7168,1024]{1,0:T(8,128)(2,1)} %bitcast.9, bf16[8,7296]{1,0:T(8,128)(2,1)S(1)} %get-tuple-element.57.after), custom_call_target="tpu_custom_call" | custom-call | bytes 14680064 | tf_op jit(solution)/shard_map/pallas_call | solution.py:67
  33.7 0.5 collective-permute-done.6.refs_1_
  34.2 0.1 collective-permute-start.7
  34.3 3.2 %shard_map.136 = (bf16[3584,1024]{1,0:T(8,128)(2,1)S(1)}, f32[8,128]{1,0:T(8,128)S(1)}) custom-call(bf16[7168,1024]{1,0:T(8,128)(2,1)} %bitcast.10, bf16[8,7296]{1,0:T(8,128)(2,1)S(1)} %get-tuple-element.60.after), custom_call_target="tpu_custom_call" | custom-call | bytes 14680064 | tf_op jit(solution)/shard_map/pallas_call | solution.py:67
  37.5 1.6 %collective-permute-done.7.refs_1_ = bf16[8,7296]{1,0:T(8,128)(2,1)S(1)} collective-permute-done((bf16[8,7296]{1,0:T(8,128)(2,1)S(1)}, bf16[8,7296]{1,0:T(8,128)(2,1)S(1)}, u32[]{:S(2)}, u32[]{:S(2)}) %collective-permute-start.7) | collective-permute-done | bytes 116768 | tf_op jit(solution)/shard_map/ppermute | solution.py:22
  39.1 0.1 shard_map.137
  39.2 0.0 copy-start.1
  39.2 0.9 %collective-permute-start.8 = (bf16[8,7296]{1,0:T(8,128)(2,1)S(1)}, bf16[8,7296]{1,0:T(8,128)(2,1)S(1)}, u32[]{:S(2)}, u32[]{:S(2)}) collective-permute-start(bf16[8,7296]{1,0:T(8,128)(2,1)S(1)} %get-tuple-element.63.after), channel_id=1, source_target_pairs={{0,8},{1,9},{2,10},{3,11},{4,12},{5,13},{6,14},{7,15},{8,0},{9,1},... | collective-permute-start | bytes 350216 | tf_op jit(solution)/shard_map/ppermute | solution.py:22
  40.0 3.2 %shard_map.138 = (bf16[3584,1024]{1,0:T(8,128)(2,1)S(1)}, f32[8,128]{1,0:T(8,128)S(1)}) custom-call(bf16[7168,1024]{1,0:T(8,128)(2,1)} %bitcast.11, bf16[8,7296]{1,0:T(8,128)(2,1)S(1)} %get-tuple-element.63.after), custom_call_target="tpu_custom_call" | custom-call | bytes 14680064 | tf_op jit(solution)/shard_map/pallas_call | solution.py:67
  43.2 2.8 %collective-permute-done.8.refs_1_ = bf16[8,7296]{1,0:T(8,128)(2,1)S(1)} collective-permute-done((bf16[8,7296]{1,0:T(8,128)(2,1)S(1)}, bf16[8,7296]{1,0:T(8,128)(2,1)S(1)}, u32[]{:S(2)}, u32[]{:S(2)}) %collective-permute-start.8) | collective-permute-done | bytes 116768 | tf_op jit(solution)/shard_map/ppermute | solution.py:22
  46.1 0.0 copy-done.1
  46.1 0.2 shard_map.139
  46.3 1.6 %collective-permute-start.9 = (bf16[8,7296]{1,0:T(8,128)(2,1)S(1)}, bf16[8,7296]{1,0:T(8,128)(2,1)S(1)}, u32[]{:S(2)}, u32[]{:S(2)}) collective-permute-start(bf16[8,7296]{1,0:T(8,128)(2,1)S(1)} %get-tuple-element.66.refs_0_), channel_id=1, source_target_pairs={{0,2},{1,3},{2,0},{3,1},{4,6},{5,7},{6,4},{7,5},{8,10},{9,11},{10,... | collective-permute-start | bytes 350216 | tf_op jit(solution)/shard_map/ppermute | solution.py:22
  47.8 3.3 %collective-permute-done.9.refs_1_ = bf16[8,7296]{1,0:T(8,128)(2,1)S(1)} collective-permute-done((bf16[8,7296]{1,0:T(8,128)(2,1)S(1)}, bf16[8,7296]{1,0:T(8,128)(2,1)S(1)}, u32[]{:S(2)}, u32[]{:S(2)}) %collective-permute-start.9) | collective-permute-done | bytes 116768 | tf_op jit(solution)/shard_map/ppermute | solution.py:22
  51.2 0.1 collective-permute-start.10
  51.2 1.5 %collective-permute-done.10.second = bf16[16,7296]{1,0:T(8,128)(2,1)S(1)} collective-permute-done((bf16[16,7296]{1,0:T(8,128)(2,1)S(1)}, bf16[16,7296]{1,0:T(8,128)(2,1)S(1)}, u32[]{:S(2)}, u32[]{:S(2)}) %collective-permute-start.10) | collective-permute-done | bytes 233504 | tf_op jit(solution)/shard_map/ppermute | solution.py:22
  52.7 8.3 %shard_map.141 = (f32[16,7168]{1,0:T(8,128)S(1)}, bf16[16,7168]{1,0:T(8,128)(2,1)S(1)}) custom-call(s32[1]{0:T(128)} %bitcast.me, bf16[16,7296]{1,0:T(8,128)(2,1)S(1)} %shard_map.140.first, bf16[16,7296]{1,0:T(8,128)(2,1)S(1)} %collective-permute-done.10.second, bf16[3584,1024]{1,0:T(8,128)(2,1)S(1)} %get-tuple-element.67.gate_top, ...), custom_call_target="tpu_custom_call" | custom-call | tf_op jit(solution)/shard_map/pallas_call | solution.py:392
  61.1 0.2 collective-permute-start.11
  61.3 1.4 %collective-permute-done.11.refs_1_ = bf16[16,7168]{1,0:T(8,128)(2,1)S(1)} collective-permute-done((bf16[16,7168]{1,0:T(8,128)(2,1)S(1)}, bf16[16,7168]{1,0:T(8,128)(2,1)S(1)}, u32[]{:S(2)}, u32[]{:S(2)}) %collective-permute-start.11) | collective-permute-done | bytes 229408 | tf_op jit(solution)/shard_map/ppermute | solution.py:22
  62.7 1.6 %collective-permute-start.12 = (bf16[8,7168]{1,0:T(8,128)(2,1)S(1)}, bf16[8,7168]{1,0:T(8,128)(2,1)S(1)}, u32[]{:S(2)}, u32[]{:S(2)}) collective-permute-start(bf16[8,7168]{1,0:T(8,128)(2,1)S(1)} %get-tuple-element.74), channel_id=1, source_target_pairs={{0,2},{1,3},{2,0},{3,1},{4,6},{5,7},{6,4},{7,5},{8,10},{9,11},{10,... | collective-permute-start | bytes 344072 | tf_op jit(solution)/shard_map/ppermute | solution.py:22
  64.2 3.7 %collective-permute-done.12.refs_1_ = bf16[8,7168]{1,0:T(8,128)(2,1)S(1)} collective-permute-done((bf16[8,7168]{1,0:T(8,128)(2,1)S(1)}, bf16[8,7168]{1,0:T(8,128)(2,1)S(1)}, u32[]{:S(2)}, u32[]{:S(2)}) %collective-permute-start.12) | collective-permute-done | bytes 114720 | tf_op jit(solution)/shard_map/ppermute | solution.py:22
  68.0 0.1 collective-permute-start.13
  68.0 4.2 %collective-permute-done.13.refs_1_ = bf16[4,7168]{1,0:T(4,128)(2,1)S(1)} collective-permute-done((bf16[4,7168]{1,0:T(4,128)(2,1)S(1)}, bf16[4,7168]{1,0:T(4,128)(2,1)S(1)}, u32[]{:S(2)}, u32[]{:S(2)}) %collective-permute-start.13) | collective-permute-done | bytes 57376 | tf_op jit(solution)/shard_map/ppermute | solution.py:22
  72.2 0.4 collective-permute-start.14
  72.7 4.4 %collective-permute-done.14 = bf16[2,7168]{1,0:T(2,128)(2,1)S(1)} collective-permute-done((bf16[2,7168]{1,0:T(2,128)(2,1)S(1)}, bf16[2,7168]{1,0:T(2,128)(2,1)S(1)}, u32[]{:S(2)}, u32[]{:S(2)}) %collective-permute-start.14) | collective-permute-done | bytes 28704 | tf_op jit(solution)/shard_map/ppermute | solution.py:22
  77.1 0.7 add_convert_fusion
  (8 shorter events, 0.2 us)
Async XLA Ops:
  5.0 1.5 %collective-permute-start = (bf16[8,16,512]{2,1,0:T(8,128)(2,1)S(1)}, bf16[8,16,512]{2,1,0:T(8,128)(2,1)S(1)}, u32[]{:S(2)}, u32[]{:S(2)}) collective-permute-start(bf16[8,16,512]{2,1,0:T(8,128)(2,1)S(1)} %get-tuple-element.43), channel_id=1, source_target_pairs={{0,1},{1,0},{2,3},{3,2},{4,5},{5,4},{6,7},{7,6},{8,9},{9,8},{10,11... | collective-permute-start | bytes 393224 | tf_op jit(solution)/shard_map/ppermute | solution.py:22
  6.5 6.7 %collective-permute-start.1 = (bf16[8,16,512]{2,1,0:T(8,128)(2,1)S(1)}, bf16[8,16,512]{2,1,0:T(8,128)(2,1)S(1)}, u32[]{:S(2)}, u32[]{:S(2)}) collective-permute-start(bf16[8,16,512]{2,1,0:T(8,128)(2,1)S(1)} %get-tuple-element.45.after), channel_id=1, source_target_pairs={{0,2},{1,3},{2,0},{3,1},{4,6},{5,7},{6,4},{7,5},{8,10},{9,11},{10,... | collective-permute-start | bytes 393224 | tf_op jit(solution)/shard_map/ppermute | solution.py:22
  13.3 8.4 %collective-permute-start.2 = (bf16[4,16,512]{2,1,0:T(8,128)(2,1)S(1)}, bf16[4,16,512]{2,1,0:T(8,128)(2,1)S(1)}, u32[]{:S(2)}, u32[]{:S(2)}) collective-permute-start(bf16[4,16,512]{2,1,0:T(8,128)(2,1)S(1)} %get-tuple-element.48), channel_id=1, source_target_pairs={{0,8},{1,9},{2,10},{3,11},{4,12},{5,13},{6,14},{7,15},{8,0},{9,1},... | collective-permute-start | bytes 196616 | tf_op jit(solution)/shard_map/ppermute | solution.py:22
  16.2 5.5 %collective-permute-start.3 = (bf16[4,16,512]{2,1,0:T(8,128)(2,1)S(1)}, bf16[4,16,512]{2,1,0:T(8,128)(2,1)S(1)}, u32[]{:S(2)}, u32[]{:S(2)}) collective-permute-start(bf16[4,16,512]{2,1,0:T(8,128)(2,1)S(1)} %get-tuple-element.49), channel_id=1, source_target_pairs={{0,4},{1,5},{2,6},{3,7},{4,0},{5,1},{6,2},{7,3},{8,12},{9,13},{10,... | collective-permute-start | bytes 196616 | tf_op jit(solution)/shard_map/ppermute | solution.py:22
  17.7 6.1 %collective-permute-start.4 = (bf16[4,16,512]{2,1,0:T(8,128)(2,1)S(1)}, bf16[4,16,512]{2,1,0:T(8,128)(2,1)S(1)}, u32[]{:S(2)}, u32[]{:S(2)}) collective-permute-start(bf16[4,16,512]{2,1,0:T(8,128)(2,1)S(1)} %get-tuple-element.50), channel_id=1, source_target_pairs={{0,12},{1,13},{2,14},{3,15},{4,8},{5,9},{6,10},{7,11},{8,4},{9,5},... | collective-permute-start | bytes 196616 | tf_op jit(solution)/shard_map/ppermute | solution.py:22
  17.8 6.0 %copy-start = (bf16[2,7168]{1,0:T(2,128)(2,1)S(1)}, bf16[2,7168]{1,0:T(2,128)(2,1)}, u32[]{:S(2)}) copy-start(bf16[2,7168]{1,0:T(2,128)(2,1)} %refs_8_.1) | copy-start | bytes 86020
  17.8 6.0 %copy-start.2 = (s32[32,1]{1,0:T(8,128)S(1)}, s32[32,1]{1,0:T(8,128)}, u32[]{:S(2)}) copy-start(s32[32,1]{1,0:T(8,128)} %constant.23.refs_4_) | copy-start | bytes 388
  27.3 1.6 %collective-permute-start.5 = (bf16[16,7296]{1,0:T(8,128)(2,1)S(1)}, bf16[16,7296]{1,0:T(8,128)(2,1)S(1)}, u32[]{:S(2)}, u32[]{:S(2)}) collective-permute-start(bf16[16,7296]{1,0:T(8,128)(2,1)S(1)} %get-tuple-element.55), channel_id=1, source_target_pairs={{0,1},{1,0},{2,3},{3,2},{4,5},{5,4},{6,7},{7,6},{8,9},{9,8},{10,11... | collective-permute-start | bytes 700424 | tf_op jit(solution)/shard_map/ppermute | solution.py:22
  28.9 5.3 %collective-permute-start.6 = (bf16[8,7296]{1,0:T(8,128)(2,1)S(1)}, bf16[8,7296]{1,0:T(8,128)(2,1)S(1)}, u32[]{:S(2)}, u32[]{:S(2)}) collective-permute-start(bf16[8,7296]{1,0:T(8,128)(2,1)S(1)} %get-tuple-element.57.after), channel_id=1, source_target_pairs={{0,2},{1,3},{2,0},{3,1},{4,6},{5,7},{6,4},{7,5},{8,10},{9,11},{10,... | collective-permute-start | bytes 350216 | tf_op jit(solution)/shard_map/ppermute | solution.py:22
  34.2 4.9 %collective-permute-start.7 = (bf16[8,7296]{1,0:T(8,128)(2,1)S(1)}, bf16[8,7296]{1,0:T(8,128)(2,1)S(1)}, u32[]{:S(2)}, u32[]{:S(2)}) collective-permute-start(bf16[8,7296]{1,0:T(8,128)(2,1)S(1)} %get-tuple-element.60.after), channel_id=1, source_target_pairs={{0,4},{1,5},{2,6},{3,7},{4,0},{5,1},{6,2},{7,3},{8,12},{9,13},{10,... | collective-permute-start | bytes 350216 | tf_op jit(solution)/shard_map/ppermute | solution.py:22
  39.2 6.9 %copy-start.1 = (f32[7168]{0:T(1024)S(1)}, f32[7168]{0:T(1024)}, u32[]{:S(2)}) copy-start(f32[7168]{0:T(1024)} %param.19) | copy-start | bytes 86020
  39.2 6.9 %collective-permute-start.8 = (bf16[8,7296]{1,0:T(8,128)(2,1)S(1)}, bf16[8,7296]{1,0:T(8,128)(2,1)S(1)}, u32[]{:S(2)}, u32[]{:S(2)}) collective-permute-start(bf16[8,7296]{1,0:T(8,128)(2,1)S(1)} %get-tuple-element.63.after), channel_id=1, source_target_pairs={{0,8},{1,9},{2,10},{3,11},{4,12},{5,13},{6,14},{7,15},{8,0},{9,1},... | collective-permute-start | bytes 350216 | tf_op jit(solution)/shard_map/ppermute | solution.py:22
  46.3 4.9 %collective-permute-start.9 = (bf16[8,7296]{1,0:T(8,128)(2,1)S(1)}, bf16[8,7296]{1,0:T(8,128)(2,1)S(1)}, u32[]{:S(2)}, u32[]{:S(2)}) collective-permute-start(bf16[8,7296]{1,0:T(8,128)(2,1)S(1)} %get-tuple-element.66.refs_0_), channel_id=1, source_target_pairs={{0,2},{1,3},{2,0},{3,1},{4,6},{5,7},{6,4},{7,5},{8,10},{9,11},{10,... | collective-permute-start | bytes 350216 | tf_op jit(solution)/shard_map/ppermute | solution.py:22
  51.2 1.6 %collective-permute-start.10 = (bf16[16,7296]{1,0:T(8,128)(2,1)S(1)}, bf16[16,7296]{1,0:T(8,128)(2,1)S(1)}, u32[]{:S(2)}, u32[]{:S(2)}) collective-permute-start(bf16[16,7296]{1,0:T(8,128)(2,1)S(1)} %shard_map.140.first), channel_id=1, source_target_pairs={{0,1},{1,0},{2,3},{3,2},{4,5},{5,4},{6,7},{7,6},{8,9},{9,8},{10,11... | collective-permute-start | bytes 700424 | tf_op jit(solution)/shard_map/ppermute | solution.py:22
  61.1 1.6 %collective-permute-start.11 = (bf16[16,7168]{1,0:T(8,128)(2,1)S(1)}, bf16[16,7168]{1,0:T(8,128)(2,1)S(1)}, u32[]{:S(2)}, u32[]{:S(2)}) collective-permute-start(bf16[16,7168]{1,0:T(8,128)(2,1)S(1)} %get-tuple-element.72), channel_id=1, source_target_pairs={{0,1},{1,0},{2,3},{3,2},{4,5},{5,4},{6,7},{7,6},{8,9},{9,8},{10,11... | collective-permute-start | bytes 688136 | tf_op jit(solution)/shard_map/ppermute | solution.py:22
  62.7 5.3 %collective-permute-start.12 = (bf16[8,7168]{1,0:T(8,128)(2,1)S(1)}, bf16[8,7168]{1,0:T(8,128)(2,1)S(1)}, u32[]{:S(2)}, u32[]{:S(2)}) collective-permute-start(bf16[8,7168]{1,0:T(8,128)(2,1)S(1)} %get-tuple-element.74), channel_id=1, source_target_pairs={{0,2},{1,3},{2,0},{3,1},{4,6},{5,7},{6,4},{7,5},{8,10},{9,11},{10,... | collective-permute-start | bytes 344072 | tf_op jit(solution)/shard_map/ppermute | solution.py:22
  68.0 4.2 %collective-permute-start.13 = (bf16[4,7168]{1,0:T(4,128)(2,1)S(1)}, bf16[4,7168]{1,0:T(4,128)(2,1)S(1)}, u32[]{:S(2)}, u32[]{:S(2)}) collective-permute-start(bf16[4,7168]{1,0:T(4,128)(2,1)S(1)} %get-tuple-element.76), channel_id=1, source_target_pairs={{0,4},{1,5},{2,6},{3,7},{4,0},{5,1},{6,2},{7,3},{8,12},{9,13},{10,... | collective-permute-start | bytes 172040 | tf_op jit(solution)/shard_map/ppermute | solution.py:22
  72.2 4.8 %collective-permute-start.14 = (bf16[2,7168]{1,0:T(2,128)(2,1)S(1)}, bf16[2,7168]{1,0:T(2,128)(2,1)S(1)}, u32[]{:S(2)}, u32[]{:S(2)}) collective-permute-start(bf16[2,7168]{1,0:T(2,128)(2,1)S(1)} %get-tuple-element.78), channel_id=1, source_target_pairs={{0,8},{1,9},{2,10},{3,11},{4,12},{5,13},{6,14},{7,15},{8,0},{9,1},... | collective-permute-start | bytes 86024 | tf_op jit(solution)/shard_map/ppermute | solution.py:22

commit v5 on v4

--- a/solution.py
+++ b/solution.py
@@ -29,7 +29,6 @@
 LANES = 128
 MIB = 1 << 20
 IN_VMEM = pl.BlockSpec(memory_space=pltpu.VMEM)
-IN_SMEM = pl.BlockSpec(memory_space=pltpu.SMEM)
 IN_HBM = pl.BlockSpec(memory_space=pltpu.HBM)
 VMEM_ARRAY = pltpu.VMEM
 
@@ -102,7 +101,7 @@
 
 
 def attend_kernel(
-    order, lengths_hbm, me, queries_hbm, cache, value_up, kept, sent, value_in, lengths, queries, held, wide, sems
+    order, lengths_hbm, queries_hbm, cache, value_up, kept, sent, value_in, lengths, queries, held, wide, sems
 ):
     rows_dev, _, heads = queries.shape
     context = cache.shape[2]
@@ -139,13 +138,14 @@
         else:
             kept[r] = got.astype(kept.dtype)
     half = len(order) // 2
+    me = lax.axis_index("ep")
     for p, s in enumerate(order):
         target = (kept, sent)[p // half]
-        target[p % half] = wide[me[0] ^ s].astype(target.dtype)
+        target[p % half] = wide[me ^ s].astype(target.dtype)
     weights.wait()
 
 
-def attend(queries, latent_cache, cache_lengths, value_up, order, me):
+def attend(queries, latent_cache, cache_lengths, value_up, order):
     rows_dev, heads, key_width = queries.shape
     context = latent_cache.shape[1]
     heads_dev, latent, _ = value_up.shape
@@ -159,7 +159,7 @@
             VMEM_ARRAY(spare, jnp.bfloat16),
             VMEM_ARRAY(value_up.shape, value_up.dtype),
         ),
-        in_specs=[IN_HBM, IN_SMEM, IN_HBM, IN_HBM, IN_HBM],
+        in_specs=[IN_HBM] * 4,
         out_specs=(IN_VMEM,) * 3,
         scratch_shapes=[
             pltpu.SMEM((rows_dev,), jnp.int32),
@@ -171,7 +171,6 @@
         compiler_params=pltpu.CompilerParams(vmem_limit_bytes=24 * MIB),
     )(
         in_hbm(cache_lengths),
-        me[None],
         in_hbm(queries.transpose(0, 2, 1)),
         in_hbm(latent_cache.transpose(0, 2, 1)),
         in_hbm(value_up),
@@ -343,7 +342,7 @@
 
 
 def expert_kernel(
-    me, first, second, gate_top, gate_bottom, up_top, up_bottom, down, kept, sent, moe_in, units, down_in, sems
+    first, second, gate_top, gate_bottom, up_top, up_bottom, down, kept, sent, moe_in, units, down_in, sems
 ):
     cut, inner = gate_top.shape
     width = 2 * cut
@@ -355,7 +354,7 @@
     moe_in[half:] = second[...]
     tail = moe_in[:, width:].astype(jnp.float32)
     column = lax.broadcasted_iota(jnp.int32, tail.shape, 1)
-    expert = lax.rem(me[0], EXPERTS)
+    expert = lax.rem(lax.axis_index("ep"), EXPERTS)
     mine = (column == expert) | (column == expert + EXPERTS)
     weight = jnp.sum(jnp.where(mine, tail, 0.0), axis=1, keepdims=True)
 
@@ -385,7 +384,7 @@
         sent[:, columns] = terms[half:].astype(sent.dtype)
 
 
-def run_expert(me, first, second, gate, up, down, limit):
+def run_expert(first, second, gate, up, down, limit):
     rows = 2 * first.shape[0]
     inner, width = down.shape
     shape = (rows // 2, width)
@@ -395,7 +394,7 @@
             jax.ShapeDtypeStruct(shape, jnp.float32),
             jax.ShapeDtypeStruct(shape, jnp.bfloat16),
         ),
-        in_specs=[IN_SMEM] + [IN_VMEM] * 6 + [IN_HBM],
+        in_specs=[IN_VMEM] * 6 + [IN_HBM],
         out_specs=(IN_VMEM, IN_VMEM),
         scratch_shapes=[
             pltpu.VMEM((rows, first.shape[1]), jnp.bfloat16),
@@ -404,7 +403,7 @@
             pltpu.SemaphoreType.DMA((4,)),
         ],
         compiler_params=pltpu.CompilerParams(vmem_limit_bytes=limit + 2 * down.size),
-    )(me, first, second, *[in_vmem(w) for w in gate + up], in_hbm(down))
+    )(first, second, *[in_vmem(w) for w in gate + up], in_hbm(down))
 
 
 def on_device(
@@ -442,7 +441,7 @@
     limit = grant(rows_in, width)
     gate, up, down = gate_proj[0], up_proj[0], down_proj[0]
     if heads_dev % 8 == 0:
-        kept, sent, value_up = attend(queries, latent_cache, cache_lengths, value_up, order, me)
+        kept, sent, value_up = attend(queries, latent_cache, cache_lengths, value_up, order)
         run = ep_size >> 2
         got = exchange(sent, 0)
         kept, sent = deal((kept, got), 2, run, limit)
@@ -455,7 +454,7 @@
         held = [mask | x << 1 | core for mask in masks for x in range(2) for core in range(2)]
         row_of = jnp.array([held.index(s) * rows_dev + r for s in order for r in range(rows_dev)])
     else:
-        out, _, value_up = attend(queries, latent_cache, cache_lengths, value_up, (), me)
+        out, _, value_up = attend(queries, latent_cache, cache_lengths, value_up, ())
         top, _ = load(out_proj, value_up, limit, 0)
         bottom, _ = load(out_proj, value_up, limit, 1)
         out = out.reshape(rows_dev, ep_size, heads_dev, latent).transpose(1, 0, 2, 3)
@@ -496,7 +495,7 @@
     if split_ways == 1:
         while later:
             beside(moe_in)
-        kept, sent = run_expert(me[None], moe_in, other, halves[:2], halves[2:], down, limit)
+        kept, sent = run_expert(moe_in, other, halves[:2], halves[2:], down, limit)
     else:
         moe_in = jnp.concatenate((moe_in, other), axis=0)
         expert = me % EXPERTS

time: 77.9 us -> 77.9 us (level)
  no operation moved by 1% of the time
where the time goes in v5:
time: 77.9 us; the launch traced here: 77.7 us
  Pallas kernels  33.8 us (43%)
  waiting for transfers between devices  27.9 us (36%)
  starting transfers between devices  14.4 us (18%)
  other arithmetic  1.51 us (2%)
    ppermute x15, waiting for transfers between devices, trade(): lax.ppermute(value, 'ep', [(i, i ^ mask) for i in range(lax.axis_size('ep...  27.9 us
    pallas_call x5, Pallas kernels, load(): pl.pallas_call(functools.partial(load_kernel, part * rows), out_shape=(VM...  16.5 us
    ppermute x15, starting transfers between devices, trade(): lax.ppermute(value, 'ep', [(i, i ^ mask) for i in range(lax.axis_size('ep...  14.4 us
    pallas_call x1, Pallas kernels, run_expert(): pl.pallas_call(expert_kernel, out_shape=(jax.ShapeDtypeStruct(shape, jnp....  8.3 us
    pallas_call x1, Pallas kernels, attend(): pl.pallas_call(functools.partial(attend_kernel, order), out_shape=(VMEM_A...  4.98 us
    pallas_call x1, Pallas kernels, project(): pl.pallas_call(functools.partial(project_kernel, width // 2, len(by_head)...  3.45 us
  transfers between devices with their start and end apart: 15, of which 13 were waited for; matrix products, arithmetic and copies ran while one was open for 1% of the time, Pallas kernels for 21%

profile of v5, /device:TPU:0, one launch (start us, length us, event | category | flops | bytes accessed | tf_op | source)
XLA Modules:
  0.0 77.7 jit_solution(4545414913745969484)
XLA Ops:
  0.0 5.0 %shard_map.127 = (bf16[8,16,512]{2,1,0:T(8,128)(2,1)S(1)}, bf16[8,16,512]{2,1,0:T(8,128)(2,1)S(1)}, bf16[8,512,128]{2,1,0:T(8,128)(2,1)S(1)}) custom-call(s32[2]{0:T(128)} %lengths_hbm.1, bf16[2,576,128]{2,1,0:T(8,128)(2,1)} %bitcast.13, bf16[2,576,2048]{2,1,0:T(8,128)(2,1)} %bitcast.12, bf16[8,512,128]{2,1,0:T(8,128)(2,1)} %value_up.1), custom_call_target="tpu_custom_call" | custom-call | tf_op jit(solution)/shard_map/pallas_call | solution.py:155
  5.0 0.5 collective-permute-start
  5.5 0.8 %select_reduce_fusion = f32[2,16]{1,0:T(2,128)S(1)} fusion(f32[2,8]{1,0:T(2,128)} %param.21, s32[2,8]{1,0:T(2,128)} %param.20), kind=kLoop, calls=%fused_computation.1 | loop fusion | flops 736 | bytes 256 | tf_op jit(solution)/shard_map/reduce_sum | solution.py:434
  6.3 0.2 collective-permute-done.refs_1_
  6.5 2.9 %collective-permute-start.1 = (bf16[8,16,512]{2,1,0:T(8,128)(2,1)S(1)}, bf16[8,16,512]{2,1,0:T(8,128)(2,1)S(1)}, u32[]{:S(2)}, u32[]{:S(2)}) collective-permute-start(bf16[8,16,512]{2,1,0:T(8,128)(2,1)S(1)} %get-tuple-element.45.after), channel_id=1, source_target_pairs={{0,2},{1,3},{2,0},{3,1},{4,6},{5,7},{6,4},{7,5},{8,10},{9,11},{10,... | collective-permute-start | bytes 393224 | tf_op jit(solution)/shard_map/ppermute | solution.py:22
  9.4 3.2 %shard_map.129 = (bf16[512,7168]{1,0:T(8,128)(2,1)S(1)}, f32[8,128]{1,0:T(8,128)S(1)}) custom-call(bf16[1024,7168]{1,0:T(8,128)(2,1)} %source.3, bf16[8,16,512]{2,1,0:T(8,128)(2,1)S(1)} %get-tuple-element.45.after), custom_call_target="tpu_custom_call" | custom-call | bytes 14680064 | tf_op jit(solution)/shard_map/pallas_call | solution.py:66
  12.6 0.6 collective-permute-done.1.refs_1_
  13.3 2.9 %collective-permute-start.2 = (bf16[4,16,512]{2,1,0:T(8,128)(2,1)S(1)}, bf16[4,16,512]{2,1,0:T(8,128)(2,1)S(1)}, u32[]{:S(2)}, u32[]{:S(2)}) collective-permute-start(bf16[4,16,512]{2,1,0:T(8,128)(2,1)S(1)} %get-tuple-element.48), channel_id=1, source_target_pairs={{0,8},{1,9},{2,10},{3,11},{4,12},{5,13},{6,14},{7,15},{8,0},{9,1},... | collective-permute-start | bytes 196616 | tf_op jit(solution)/shard_map/ppermute | solution.py:22
  16.2 1.6 %collective-permute-start.3 = (bf16[4,16,512]{2,1,0:T(8,128)(2,1)S(1)}, bf16[4,16,512]{2,1,0:T(8,128)(2,1)S(1)}, u32[]{:S(2)}, u32[]{:S(2)}) collective-permute-start(bf16[4,16,512]{2,1,0:T(8,128)(2,1)S(1)} %get-tuple-element.49), channel_id=1, source_target_pairs={{0,4},{1,5},{2,6},{3,7},{4,0},{5,1},{6,2},{7,3},{8,12},{9,13},{10,... | collective-permute-start | bytes 196616 | tf_op jit(solution)/shard_map/ppermute | solution.py:22
  17.7 0.0 collective-permute-start.4
  17.7 0.1 select_maximum_fusion.refs_9_
  17.8 0.0 copy-start
  17.8 0.0 copy-start.2
  17.8 3.8 %shard_map.131 = (bf16[512,7168]{1,0:T(8,128)(2,1)S(1)}, f32[8,128]{1,0:T(8,128)}) custom-call(bf16[1024,7168]{1,0:T(8,128)(2,1)} %source.3, bf16[4,16,512]{2,1,0:T(8,128)(2,1)S(1)} %get-tuple-element.47.after.refs_0_), custom_call_target="tpu_custom_call" | custom-call | bytes 14680064 | tf_op jit(solution)/shard_map/pallas_call | solution.py:66
  21.6 0.0 collective-permute-done.2.refs_1_
  21.6 0.0 collective-permute-done.3.refs_2_
  21.6 2.2 %collective-permute-done.4.refs_3_ = bf16[4,16,512]{2,1,0:T(8,128)(2,1)S(1)} collective-permute-done((bf16[4,16,512]{2,1,0:T(8,128)(2,1)S(1)}, bf16[4,16,512]{2,1,0:T(8,128)(2,1)S(1)}, u32[]{:S(2)}, u32[]{:S(2)}) %collective-permute-start.4) | collective-permute-done | bytes 65568 | tf_op jit(solution)/shard_map/ppermute | solution.py:22
  23.8 0.0 copy-done
  23.8 0.0 copy-done.2
  23.8 3.4 %shard_map.132 = (f32[16,7296]{1,0:T(8,128)S(1)}, bf16[16,7296]{1,0:T(8,128)(2,1)S(1)}, bf16[3584,1024]{1,0:T(8,128)(2,1)S(1)}) custom-call(bf16[4,16,512]{2,1,0:T(8,128)(2,1)S(1)} %get-tuple-element.47.after.refs_0_, bf16[4,16,512]{2,1,0:T(8,128)(2,1)S(1)} %collective-permute-done.2.refs_1_, bf16[4,16,512]{2,1,0:T(8,128)(2,1)S(1)} %collective-permute-done.3.refs_2_, ...), custom_call_target="tpu_custom_call" | custom-call | tf_op jit(solution)/shard_map/pallas_call | solution.py:258
  27.3 0.1 collective-permute-start.5
  27.3 1.5 %collective-permute-done.5.refs_1_ = bf16[16,7296]{1,0:T(8,128)(2,1)S(1)} collective-permute-done((bf16[16,7296]{1,0:T(8,128)(2,1)S(1)}, bf16[16,7296]{1,0:T(8,128)(2,1)S(1)}, u32[]{:S(2)}, u32[]{:S(2)}) %collective-permute-start.5) | collective-permute-done | bytes 233504 | tf_op jit(solution)/shard_map/ppermute | solution.py:22
  28.8 0.1 shard_map.133
  28.9 1.6 %collective-permute-start.6 = (bf16[8,7296]{1,0:T(8,128)(2,1)S(1)}, bf16[8,7296]{1,0:T(8,128)(2,1)S(1)}, u32[]{:S(2)}, u32[]{:S(2)}) collective-permute-start(bf16[8,7296]{1,0:T(8,128)(2,1)S(1)} %get-tuple-element.57.after), channel_id=1, source_target_pairs={{0,2},{1,3},{2,0},{3,1},{4,6},{5,7},{6,4},{7,5},{8,10},{9,11},{10,... | collective-permute-start | bytes 350216 | tf_op jit(solution)/shard_map/ppermute | solution.py:22
  30.5 3.2 %shard_map.134 = (bf16[3584,1024]{1,0:T(8,128)(2,1)S(1)}, f32[8,128]{1,0:T(8,128)S(1)}) custom-call(bf16[7168,1024]{1,0:T(8,128)(2,1)} %bitcast.8, bf16[8,7296]{1,0:T(8,128)(2,1)S(1)} %get-tuple-element.57.after), custom_call_target="tpu_custom_call" | custom-call | bytes 14680064 | tf_op jit(solution)/shard_map/pallas_call | solution.py:66
  33.7 0.5 collective-permute-done.6.refs_1_
  34.2 0.1 collective-permute-start.7
  34.3 3.2 %shard_map.136 = (bf16[3584,1024]{1,0:T(8,128)(2,1)S(1)}, f32[8,128]{1,0:T(8,128)S(1)}) custom-call(bf16[7168,1024]{1,0:T(8,128)(2,1)} %bitcast.9, bf16[8,7296]{1,0:T(8,128)(2,1)S(1)} %get-tuple-element.60.after), custom_call_target="tpu_custom_call" | custom-call | bytes 14680064 | tf_op jit(solution)/shard_map/pallas_call | solution.py:66
  37.5 1.6 %collective-permute-done.7.refs_1_ = bf16[8,7296]{1,0:T(8,128)(2,1)S(1)} collective-permute-done((bf16[8,7296]{1,0:T(8,128)(2,1)S(1)}, bf16[8,7296]{1,0:T(8,128)(2,1)S(1)}, u32[]{:S(2)}, u32[]{:S(2)}) %collective-permute-start.7) | collective-permute-done | bytes 116768 | tf_op jit(solution)/shard_map/ppermute | solution.py:22
  39.1 0.1 shard_map.137
  39.2 0.0 copy-start.1
  39.2 0.9 %collective-permute-start.8 = (bf16[8,7296]{1,0:T(8,128)(2,1)S(1)}, bf16[8,7296]{1,0:T(8,128)(2,1)S(1)}, u32[]{:S(2)}, u32[]{:S(2)}) collective-permute-start(bf16[8,7296]{1,0:T(8,128)(2,1)S(1)} %get-tuple-element.63.after), channel_id=1, source_target_pairs={{0,8},{1,9},{2,10},{3,11},{4,12},{5,13},{6,14},{7,15},{8,0},{9,1},... | collective-permute-start | bytes 350216 | tf_op jit(solution)/shard_map/ppermute | solution.py:22
  40.0 3.2 %shard_map.138 = (bf16[3584,1024]{1,0:T(8,128)(2,1)S(1)}, f32[8,128]{1,0:T(8,128)S(1)}) custom-call(bf16[7168,1024]{1,0:T(8,128)(2,1)} %bitcast.10, bf16[8,7296]{1,0:T(8,128)(2,1)S(1)} %get-tuple-element.63.after), custom_call_target="tpu_custom_call" | custom-call | bytes 14680064 | tf_op jit(solution)/shard_map/pallas_call | solution.py:66
  43.2 2.8 %collective-permute-done.8.refs_1_ = bf16[8,7296]{1,0:T(8,128)(2,1)S(1)} collective-permute-done((bf16[8,7296]{1,0:T(8,128)(2,1)S(1)}, bf16[8,7296]{1,0:T(8,128)(2,1)S(1)}, u32[]{:S(2)}, u32[]{:S(2)}) %collective-permute-start.8) | collective-permute-done | bytes 116768 | tf_op jit(solution)/shard_map/ppermute | solution.py:22
  46.1 0.0 copy-done.1
  46.1 0.2 shard_map.139
  46.3 1.6 %collective-permute-start.9 = (bf16[8,7296]{1,0:T(8,128)(2,1)S(1)}, bf16[8,7296]{1,0:T(8,128)(2,1)S(1)}, u32[]{:S(2)}, u32[]{:S(2)}) collective-permute-start(bf16[8,7296]{1,0:T(8,128)(2,1)S(1)} %get-tuple-element.66.refs_0_), channel_id=1, source_target_pairs={{0,2},{1,3},{2,0},{3,1},{4,6},{5,7},{6,4},{7,5},{8,10},{9,11},{10,... | collective-permute-start | bytes 350216 | tf_op jit(solution)/shard_map/ppermute | solution.py:22
  47.8 3.3 %collective-permute-done.9.refs_1_ = bf16[8,7296]{1,0:T(8,128)(2,1)S(1)} collective-permute-done((bf16[8,7296]{1,0:T(8,128)(2,1)S(1)}, bf16[8,7296]{1,0:T(8,128)(2,1)S(1)}, u32[]{:S(2)}, u32[]{:S(2)}) %collective-permute-start.9) | collective-permute-done | bytes 116768 | tf_op jit(solution)/shard_map/ppermute | solution.py:22
  51.2 0.1 collective-permute-start.10
  51.2 1.5 %collective-permute-done.10.second = bf16[16,7296]{1,0:T(8,128)(2,1)S(1)} collective-permute-done((bf16[16,7296]{1,0:T(8,128)(2,1)S(1)}, bf16[16,7296]{1,0:T(8,128)(2,1)S(1)}, u32[]{:S(2)}, u32[]{:S(2)}) %collective-permute-start.10) | collective-permute-done | bytes 233504 | tf_op jit(solution)/shard_map/ppermute | solution.py:22
  52.7 8.3 %shard_map.141 = (f32[16,7168]{1,0:T(8,128)S(1)}, bf16[16,7168]{1,0:T(8,128)(2,1)S(1)}) custom-call(bf16[16,7296]{1,0:T(8,128)(2,1)S(1)} %shard_map.140.first, bf16[16,7296]{1,0:T(8,128)(2,1)S(1)} %collective-permute-done.10.second, bf16[3584,1024]{1,0:T(8,128)(2,1)S(1)} %get-tuple-element.67.gate_top, bf16[3584,1024]{1,0:T(8,128)(2,1)S(1)} %get-tuple-element.68.gate_bottom, ...), custom_call_target="tpu_custom_call" | custom-call | tf_op jit(solution)/shard_map/pallas_call | solution.py:391
  61.0 0.2 collective-permute-start.11
  61.2 1.4 %collective-permute-done.11.refs_1_ = bf16[16,7168]{1,0:T(8,128)(2,1)S(1)} collective-permute-done((bf16[16,7168]{1,0:T(8,128)(2,1)S(1)}, bf16[16,7168]{1,0:T(8,128)(2,1)S(1)}, u32[]{:S(2)}, u32[]{:S(2)}) %collective-permute-start.11) | collective-permute-done | bytes 229408 | tf_op jit(solution)/shard_map/ppermute | solution.py:22
  62.6 0.1 shard_map.142
  62.7 1.6 %collective-permute-start.12 = (bf16[8,7168]{1,0:T(8,128)(2,1)S(1)}, bf16[8,7168]{1,0:T(8,128)(2,1)S(1)}, u32[]{:S(2)}, u32[]{:S(2)}) collective-permute-start(bf16[8,7168]{1,0:T(8,128)(2,1)S(1)} %get-tuple-element.74), channel_id=1, source_target_pairs={{0,2},{1,3},{2,0},{3,1},{4,6},{5,7},{6,4},{7,5},{8,10},{9,11},{10,... | collective-permute-start | bytes 344072 | tf_op jit(solution)/shard_map/ppermute | solution.py:22
  64.2 3.7 %collective-permute-done.12.refs_1_ = bf16[8,7168]{1,0:T(8,128)(2,1)S(1)} collective-permute-done((bf16[8,7168]{1,0:T(8,128)(2,1)S(1)}, bf16[8,7168]{1,0:T(8,128)(2,1)S(1)}, u32[]{:S(2)}, u32[]{:S(2)}) %collective-permute-start.12) | collective-permute-done | bytes 114720 | tf_op jit(solution)/shard_map/ppermute | solution.py:22
  67.9 0.1 collective-permute-start.13
  68.0 4.2 %collective-permute-done.13.refs_1_ = bf16[4,7168]{1,0:T(4,128)(2,1)S(1)} collective-permute-done((bf16[4,7168]{1,0:T(4,128)(2,1)S(1)}, bf16[4,7168]{1,0:T(4,128)(2,1)S(1)}, u32[]{:S(2)}, u32[]{:S(2)}) %collective-permute-start.13) | collective-permute-done | bytes 57376 | tf_op jit(solution)/shard_map/ppermute | solution.py:22
  72.2 0.4 collective-permute-start.14
  72.7 4.4 %collective-permute-done.14 = bf16[2,7168]{1,0:T(2,128)(2,1)S(1)} collective-permute-done((bf16[2,7168]{1,0:T(2,128)(2,1)S(1)}, bf16[2,7168]{1,0:T(2,128)(2,1)S(1)}, u32[]{:S(2)}, u32[]{:S(2)}) %collective-permute-start.14) | collective-permute-done | bytes 28704 | tf_op jit(solution)/shard_map/ppermute | solution.py:22
  77.1 0.7 add_convert_fusion
  (7 shorter events, 0.2 us)
Async XLA Ops:
  5.0 1.5 %collective-permute-start = (bf16[8,16,512]{2,1,0:T(8,128)(2,1)S(1)}, bf16[8,16,512]{2,1,0:T(8,128)(2,1)S(1)}, u32[]{:S(2)}, u32[]{:S(2)}) collective-permute-start(bf16[8,16,512]{2,1,0:T(8,128)(2,1)S(1)} %get-tuple-element.43), channel_id=1, source_target_pairs={{0,1},{1,0},{2,3},{3,2},{4,5},{5,4},{6,7},{7,6},{8,9},{9,8},{10,11... | collective-permute-start | bytes 393224 | tf_op jit(solution)/shard_map/ppermute | solution.py:22
  6.5 6.7 %collective-permute-start.1 = (bf16[8,16,512]{2,1,0:T(8,128)(2,1)S(1)}, bf16[8,16,512]{2,1,0:T(8,128)(2,1)S(1)}, u32[]{:S(2)}, u32[]{:S(2)}) collective-permute-start(bf16[8,16,512]{2,1,0:T(8,128)(2,1)S(1)} %get-tuple-element.45.after), channel_id=1, source_target_pairs={{0,2},{1,3},{2,0},{3,1},{4,6},{5,7},{6,4},{7,5},{8,10},{9,11},{10,... | collective-permute-start | bytes 393224 | tf_op jit(solution)/shard_map/ppermute | solution.py:22
  13.3 8.4 %collective-permute-start.2 = (bf16[4,16,512]{2,1,0:T(8,128)(2,1)S(1)}, bf16[4,16,512]{2,1,0:T(8,128)(2,1)S(1)}, u32[]{:S(2)}, u32[]{:S(2)}) collective-permute-start(bf16[4,16,512]{2,1,0:T(8,128)(2,1)S(1)} %get-tuple-element.48), channel_id=1, source_target_pairs={{0,8},{1,9},{2,10},{3,11},{4,12},{5,13},{6,14},{7,15},{8,0},{9,1},... | collective-permute-start | bytes 196616 | tf_op jit(solution)/shard_map/ppermute | solution.py:22
  16.2 5.5 %collective-permute-start.3 = (bf16[4,16,512]{2,1,0:T(8,128)(2,1)S(1)}, bf16[4,16,512]{2,1,0:T(8,128)(2,1)S(1)}, u32[]{:S(2)}, u32[]{:S(2)}) collective-permute-start(bf16[4,16,512]{2,1,0:T(8,128)(2,1)S(1)} %get-tuple-element.49), channel_id=1, source_target_pairs={{0,4},{1,5},{2,6},{3,7},{4,0},{5,1},{6,2},{7,3},{8,12},{9,13},{10,... | collective-permute-start | bytes 196616 | tf_op jit(solution)/shard_map/ppermute | solution.py:22
  17.7 6.1 %collective-permute-start.4 = (bf16[4,16,512]{2,1,0:T(8,128)(2,1)S(1)}, bf16[4,16,512]{2,1,0:T(8,128)(2,1)S(1)}, u32[]{:S(2)}, u32[]{:S(2)}) collective-permute-start(bf16[4,16,512]{2,1,0:T(8,128)(2,1)S(1)} %get-tuple-element.50), channel_id=1, source_target_pairs={{0,12},{1,13},{2,14},{3,15},{4,8},{5,9},{6,10},{7,11},{8,4},{9,5},... | collective-permute-start | bytes 196616 | tf_op jit(solution)/shard_map/ppermute | solution.py:22
  17.8 6.0 %copy-start = (bf16[2,7168]{1,0:T(2,128)(2,1)S(1)}, bf16[2,7168]{1,0:T(2,128)(2,1)}, u32[]{:S(2)}) copy-start(bf16[2,7168]{1,0:T(2,128)(2,1)} %refs_8_.1) | copy-start | bytes 86020
  17.8 6.0 %copy-start.2 = (s32[32,1]{1,0:T(8,128)S(1)}, s32[32,1]{1,0:T(8,128)}, u32[]{:S(2)}) copy-start(s32[32,1]{1,0:T(8,128)} %constant.19.refs_4_) | copy-start | bytes 388
  27.3 1.6 %collective-permute-start.5 = (bf16[16,7296]{1,0:T(8,128)(2,1)S(1)}, bf16[16,7296]{1,0:T(8,128)(2,1)S(1)}, u32[]{:S(2)}, u32[]{:S(2)}) collective-permute-start(bf16[16,7296]{1,0:T(8,128)(2,1)S(1)} %get-tuple-element.55), channel_id=1, source_target_pairs={{0,1},{1,0},{2,3},{3,2},{4,5},{5,4},{6,7},{7,6},{8,9},{9,8},{10,11... | collective-permute-start | bytes 700424 | tf_op jit(solution)/shard_map/ppermute | solution.py:22
  28.9 5.3 %collective-permute-start.6 = (bf16[8,7296]{1,0:T(8,128)(2,1)S(1)}, bf16[8,7296]{1,0:T(8,128)(2,1)S(1)}, u32[]{:S(2)}, u32[]{:S(2)}) collective-permute-start(bf16[8,7296]{1,0:T(8,128)(2,1)S(1)} %get-tuple-element.57.after), channel_id=1, source_target_pairs={{0,2},{1,3},{2,0},{3,1},{4,6},{5,7},{6,4},{7,5},{8,10},{9,11},{10,... | collective-permute-start | bytes 350216 | tf_op jit(solution)/shard_map/ppermute | solution.py:22
  34.2 4.9 %collective-permute-start.7 = (bf16[8,7296]{1,0:T(8,128)(2,1)S(1)}, bf16[8,7296]{1,0:T(8,128)(2,1)S(1)}, u32[]{:S(2)}, u32[]{:S(2)}) collective-permute-start(bf16[8,7296]{1,0:T(8,128)(2,1)S(1)} %get-tuple-element.60.after), channel_id=1, source_target_pairs={{0,4},{1,5},{2,6},{3,7},{4,0},{5,1},{6,2},{7,3},{8,12},{9,13},{10,... | collective-permute-start | bytes 350216 | tf_op jit(solution)/shard_map/ppermute | solution.py:22
  39.2 6.9 %copy-start.1 = (f32[7168]{0:T(1024)S(1)}, f32[7168]{0:T(1024)}, u32[]{:S(2)}) copy-start(f32[7168]{0:T(1024)} %param.19) | copy-start | bytes 86020
  39.2 6.9 %collective-permute-start.8 = (bf16[8,7296]{1,0:T(8,128)(2,1)S(1)}, bf16[8,7296]{1,0:T(8,128)(2,1)S(1)}, u32[]{:S(2)}, u32[]{:S(2)}) collective-permute-start(bf16[8,7296]{1,0:T(8,128)(2,1)S(1)} %get-tuple-element.63.after), channel_id=1, source_target_pairs={{0,8},{1,9},{2,10},{3,11},{4,12},{5,13},{6,14},{7,15},{8,0},{9,1},... | collective-permute-start | bytes 350216 | tf_op jit(solution)/shard_map/ppermute | solution.py:22
  46.3 4.9 %collective-permute-start.9 = (bf16[8,7296]{1,0:T(8,128)(2,1)S(1)}, bf16[8,7296]{1,0:T(8,128)(2,1)S(1)}, u32[]{:S(2)}, u32[]{:S(2)}) collective-permute-start(bf16[8,7296]{1,0:T(8,128)(2,1)S(1)} %get-tuple-element.66.refs_0_), channel_id=1, source_target_pairs={{0,2},{1,3},{2,0},{3,1},{4,6},{5,7},{6,4},{7,5},{8,10},{9,11},{10,... | collective-permute-start | bytes 350216 | tf_op jit(solution)/shard_map/ppermute | solution.py:22
  51.2 1.6 %collective-permute-start.10 = (bf16[16,7296]{1,0:T(8,128)(2,1)S(1)}, bf16[16,7296]{1,0:T(8,128)(2,1)S(1)}, u32[]{:S(2)}, u32[]{:S(2)}) collective-permute-start(bf16[16,7296]{1,0:T(8,128)(2,1)S(1)} %shard_map.140.first), channel_id=1, source_target_pairs={{0,1},{1,0},{2,3},{3,2},{4,5},{5,4},{6,7},{7,6},{8,9},{9,8},{10,11... | collective-permute-start | bytes 700424 | tf_op jit(solution)/shard_map/ppermute | solution.py:22
  61.0 1.6 %collective-permute-start.11 = (bf16[16,7168]{1,0:T(8,128)(2,1)S(1)}, bf16[16,7168]{1,0:T(8,128)(2,1)S(1)}, u32[]{:S(2)}, u32[]{:S(2)}) collective-permute-start(bf16[16,7168]{1,0:T(8,128)(2,1)S(1)} %get-tuple-element.72), channel_id=1, source_target_pairs={{0,1},{1,0},{2,3},{3,2},{4,5},{5,4},{6,7},{7,6},{8,9},{9,8},{10,11... | collective-permute-start | bytes 688136 | tf_op jit(solution)/shard_map/ppermute | solution.py:22
  62.7 5.3 %collective-permute-start.12 = (bf16[8,7168]{1,0:T(8,128)(2,1)S(1)}, bf16[8,7168]{1,0:T(8,128)(2,1)S(1)}, u32[]{:S(2)}, u32[]{:S(2)}) collective-permute-start(bf16[8,7168]{1,0:T(8,128)(2,1)S(1)} %get-tuple-element.74), channel_id=1, source_target_pairs={{0,2},{1,3},{2,0},{3,1},{4,6},{5,7},{6,4},{7,5},{8,10},{9,11},{10,... | collective-permute-start | bytes 344072 | tf_op jit(solution)/shard_map/ppermute | solution.py:22
  67.9 4.2 %collective-permute-start.13 = (bf16[4,7168]{1,0:T(4,128)(2,1)S(1)}, bf16[4,7168]{1,0:T(4,128)(2,1)S(1)}, u32[]{:S(2)}, u32[]{:S(2)}) collective-permute-start(bf16[4,7168]{1,0:T(4,128)(2,1)S(1)} %get-tuple-element.76), channel_id=1, source_target_pairs={{0,4},{1,5},{2,6},{3,7},{4,0},{5,1},{6,2},{7,3},{8,12},{9,13},{10,... | collective-permute-start | bytes 172040 | tf_op jit(solution)/shard_map/ppermute | solution.py:22
  72.2 4.8 %collective-permute-start.14 = (bf16[2,7168]{1,0:T(2,128)(2,1)S(1)}, bf16[2,7168]{1,0:T(2,128)(2,1)S(1)}, u32[]{:S(2)}, u32[]{:S(2)}) collective-permute-start(bf16[2,7168]{1,0:T(2,128)(2,1)S(1)} %get-tuple-element.78), channel_id=1, source_target_pairs={{0,8},{1,9},{2,10},{3,11},{4,12},{5,13},{6,14},{7,15},{8,0},{9,1},... | collective-permute-start | bytes 86024 | tf_op jit(solution)/shard_map/ppermute | solution.py:22

commit v6 on v4

--- a/solution.py
+++ b/solution.py
@@ -209,15 +209,7 @@
 
 
 def project_kernel(tile, count, *refs):
-    row_of, value_up, top, bottom, hidden, tail = refs[count : count + 6]
-    next_hbm, kept, sent, next_in, sems = refs[count + 6 :] if len(refs) > count + 8 else (
-        None, *refs[count + 6 :], None, None
-    )
-    copies = []
-    if sems is not None:
-        copies = pieces(next_hbm.at[pl.ds(0, next_in.shape[0])], next_in, sems, 0)
-    for copy in copies:
-        copy.start()
+    row_of, value_up, top, bottom, hidden, tail, kept, sent = refs[count:]
     heads_dev = value_up.shape[0]
     half, wide = kept.shape
     rows_dev, width = hidden.shape
@@ -248,24 +240,20 @@
     kept[:, width:] = jnp.zeros((half, wide - width), kept.dtype)
     kept[0:rows_dev, width:] = tail[...]
     sent[:, width:] = jnp.zeros((half, wide - width), sent.dtype)
-    for copy in copies:
-        copy.wait()
-
-
-def project(by_head, row_of, value_up, top, bottom, hidden, tail, following, limit):
+
+
+def project(by_head, row_of, value_up, top, bottom, hidden, tail, limit):
     rows_in = row_of.shape[0]
     width = hidden.shape[1]
     shape = (rows_in // 2, width + LANES)
-    results = pl.pallas_call(
+    return pl.pallas_call(
         functools.partial(project_kernel, width // 2, len(by_head)),
         out_shape=(
             jax.ShapeDtypeStruct(shape, jnp.float32),
             jax.ShapeDtypeStruct(shape, jnp.bfloat16),
-            *[VMEM_ARRAY((w.shape[0] // 2, w.shape[1]), w.dtype) for w in following],
         ),
-        in_specs=[IN_VMEM] * (len(by_head) + 6) + [IN_HBM] * len(following),
-        out_specs=(IN_VMEM,) * (2 + len(following)),
-        scratch_shapes=[pltpu.SemaphoreType.DMA((4,))] * len(following),
+        in_specs=[IN_VMEM] * (len(by_head) + 6),
+        out_specs=(IN_VMEM, IN_VMEM),
         compiler_params=pltpu.CompilerParams(vmem_limit_bytes=limit),
     )(
         *by_head,
@@ -275,9 +263,7 @@
         in_vmem(bottom),
         hidden,
         tail,
-        *[in_hbm(w) for w in following],
     )
-    return results[:2], tuple(results[2:])
 
 
 def halve_kernel(kept, got, next_kept, sent):
@@ -326,9 +312,9 @@
     out[rows:] = second[...]
 
 
-def stack(first, second, limit):
+def stack(first, second, limit, waits_for):
     shape = jax.ShapeDtypeStruct((2 * first.shape[0], first.shape[1]), first.dtype)
-    return small_call(stack_kernel, (first, second), (shape,), (), limit)[0]
+    return small_call(stack_kernel, (first, second), (shape,), waits_for, limit)[0]
 
 
 def strips(source, target, sems):
@@ -464,11 +450,12 @@
         row_of = (jnp.array(order) ^ me)[:, None] * rows_dev + jnp.arange(rows_dev)[None, :]
         row_of = row_of.reshape(-1)
     row_of = row_of.astype(jnp.int32)
-    following = (gate,) if split_ways == 1 else ()
-    (kept, sent), halves = project(
-        by_head, row_of[:, None], value_up, top, bottom, hidden, tail, following, limit
+    kept, sent = project(
+        by_head, row_of[:, None], value_up, top, bottom, hidden, tail, limit
     )
-    halves, later = list(halves), [(gate, 1), (up, 0), (up, 1)] if split_ways == 1 else []
+    halves, later = [], [(w, part) for w in (gate, up) for part in range(2)]
+    if split_ways > 1:
+        later = []
 
     def beside(value):
         if not later:
@@ -490,7 +477,8 @@
         got = exchange(sent, bit)
     residual, moe_in = norm(kept, got, norm_gain[None, :], rows_dev, limit, beside(sent))
     for bit in reversed(range(1, scatter_bits)):
-        moe_in = stack(moe_in, exchange(moe_in, bit), limit)
+        got = exchange(moe_in, bit)
+        moe_in = stack(moe_in, got, limit, beside(moe_in))
     other = exchange(moe_in, 0)
 
     if split_ways == 1:

time: 77.9 us -> 77.7 us (level)
  waiting for transfers between devices: 27.8 us -> 24.7 us
  Pallas kernels: 33.8 us -> 36.8 us
    pallas_call x5 -> x6, Pallas kernels: 16.5 us -> 19.7 us  [load(): pl.pallas_call(functools.partial(load_kernel, part * rows), out_shape=(VM...]
    ppermute x15, waiting for transfers between devices: 27.8 us -> 24.7 us  [trade(): lax.ppermute(value, 'ep', [(i, i ^ mask) for i in range(lax.axis_size('ep...]
  transfers between devices with their start and end apart: 15 -> 15, of which waited for: 13 -> 13; matrix products, arithmetic and copies ran while one was open for 1% -> 1% of each run, Pallas kernels for 21% -> 25%
where the time goes in v6:
time: 77.7 us; the launch traced here: 77.5 us
  Pallas kernels  36.8 us (47%)
  waiting for transfers between devices  24.7 us (32%)
  starting transfers between devices  14.3 us (18%)
  other arithmetic  1.51 us (2%)
    ppermute x15, waiting for transfers between devices, trade(): lax.ppermute(value, 'ep', [(i, i ^ mask) for i in range(lax.axis_size('ep...  24.7 us
    pallas_call x6, Pallas kernels, load(): pl.pallas_call(functools.partial(load_kernel, part * rows), out_shape=(VM...  19.7 us
    ppermute x15, starting transfers between devices, trade(): lax.ppermute(value, 'ep', [(i, i ^ mask) for i in range(lax.axis_size('ep...  14.3 us
    pallas_call x1, Pallas kernels, run_expert(): pl.pallas_call(expert_kernel, out_shape=(jax.ShapeDtypeStruct(shape, jnp....  8.33 us
    pallas_call x1, Pallas kernels, attend(): pl.pallas_call(functools.partial(attend_kernel, order), out_shape=(VMEM_A...  4.98 us
    pallas_call x1, Pallas kernels, project(): pl.pallas_call(functools.partial(project_kernel, width // 2, len(by_head)...  3.29 us
  transfers between devices with their start and end apart: 15, of which 13 were waited for; matrix products, arithmetic and copies ran while one was open for 1% of the time, Pallas kernels for 25%

profile of v6, /device:TPU:0, one launch (start us, length us, event | category | flops | bytes accessed | tf_op | source)
XLA Modules:
  0.0 77.5 jit_solution(3332514990105750524)
XLA Ops:
  0.0 5.0 %shard_map.127 = (bf16[8,16,512]{2,1,0:T(8,128)(2,1)S(1)}, bf16[8,16,512]{2,1,0:T(8,128)(2,1)S(1)}, bf16[8,512,128]{2,1,0:T(8,128)(2,1)S(1)}) custom-call(s32[2]{0:T(128)} %lengths_hbm.1, s32[1]{0:T(128)} %bitcast.me, bf16[2,576,128]{2,1,0:T(8,128)(2,1)} %bitcast.14, bf16[2,576,2048]{2,1,0:T(8,128)(2,1)} %bitcast.13, bf16[8,512,128]{2,1,0:T(8,128)(2,1)} %value_up.1), custom_call_target="tpu_custom_call" | custom-call | tf_op jit(solution)/shard_map/pallas_call | solution.py:155
  5.0 0.5 collective-permute-start
  5.5 0.8 %select_reduce_fusion = f32[2,16]{1,0:T(2,128)S(1)} fusion(f32[2,8]{1,0:T(2,128)} %param.21, s32[2,8]{1,0:T(2,128)} %param.20), kind=kLoop, calls=%fused_computation.1 | loop fusion | flops 736 | bytes 256 | tf_op jit(solution)/shard_map/reduce_sum | solution.py:421
  6.3 0.2 collective-permute-done.refs_1_
  6.5 2.9 %collective-permute-start.1 = (bf16[8,16,512]{2,1,0:T(8,128)(2,1)S(1)}, bf16[8,16,512]{2,1,0:T(8,128)(2,1)S(1)}, u32[]{:S(2)}, u32[]{:S(2)}) collective-permute-start(bf16[8,16,512]{2,1,0:T(8,128)(2,1)S(1)} %get-tuple-element.46.after), channel_id=1, source_target_pairs={{0,2},{1,3},{2,0},{3,1},{4,6},{5,7},{6,4},{7,5},{8,10},{9,11},{10,... | collective-permute-start | bytes 393224 | tf_op jit(solution)/shard_map/ppermute | solution.py:22
  9.4 3.2 %shard_map.129 = (bf16[512,7168]{1,0:T(8,128)(2,1)S(1)}, f32[8,128]{1,0:T(8,128)S(1)}) custom-call(bf16[1024,7168]{1,0:T(8,128)(2,1)} %source.3, bf16[8,16,512]{2,1,0:T(8,128)(2,1)S(1)} %get-tuple-element.46.after), custom_call_target="tpu_custom_call" | custom-call | bytes 14680064 | tf_op jit(solution)/shard_map/pallas_call | solution.py:67
  12.6 0.6 collective-permute-done.1.refs_1_
  13.3 2.9 %collective-permute-start.2 = (bf16[4,16,512]{2,1,0:T(8,128)(2,1)S(1)}, bf16[4,16,512]{2,1,0:T(8,128)(2,1)S(1)}, u32[]{:S(2)}, u32[]{:S(2)}) collective-permute-start(bf16[4,16,512]{2,1,0:T(8,128)(2,1)S(1)} %get-tuple-element.49), channel_id=1, source_target_pairs={{0,8},{1,9},{2,10},{3,11},{4,12},{5,13},{6,14},{7,15},{8,0},{9,1},... | collective-permute-start | bytes 196616 | tf_op jit(solution)/shard_map/ppermute | solution.py:22
  16.2 1.6 %collective-permute-start.3 = (bf16[4,16,512]{2,1,0:T(8,128)(2,1)S(1)}, bf16[4,16,512]{2,1,0:T(8,128)(2,1)S(1)}, u32[]{:S(2)}, u32[]{:S(2)}) collective-permute-start(bf16[4,16,512]{2,1,0:T(8,128)(2,1)S(1)} %get-tuple-element.50), channel_id=1, source_target_pairs={{0,4},{1,5},{2,6},{3,7},{4,0},{5,1},{6,2},{7,3},{8,12},{9,13},{10,... | collective-permute-start | bytes 196616 | tf_op jit(solution)/shard_map/ppermute | solution.py:22
  17.7 0.0 collective-permute-start.4
  17.7 0.1 select_maximum_fusion.refs_9_
  17.8 0.0 copy-start
  17.8 0.0 copy-start.2
  17.8 3.8 %shard_map.131 = (bf16[512,7168]{1,0:T(8,128)(2,1)S(1)}, f32[8,128]{1,0:T(8,128)}) custom-call(bf16[1024,7168]{1,0:T(8,128)(2,1)} %source.3, bf16[4,16,512]{2,1,0:T(8,128)(2,1)S(1)} %get-tuple-element.48.after.refs_0_), custom_call_target="tpu_custom_call" | custom-call | bytes 14680064 | tf_op jit(solution)/shard_map/pallas_call | solution.py:67
  21.6 0.0 collective-permute-done.2.refs_1_
  21.6 0.0 collective-permute-done.3.refs_2_
  21.6 2.2 %collective-permute-done.4.refs_3_ = bf16[4,16,512]{2,1,0:T(8,128)(2,1)S(1)} collective-permute-done((bf16[4,16,512]{2,1,0:T(8,128)(2,1)S(1)}, bf16[4,16,512]{2,1,0:T(8,128)(2,1)S(1)}, u32[]{:S(2)}, u32[]{:S(2)}) %collective-permute-start.4) | collective-permute-done | bytes 65568 | tf_op jit(solution)/shard_map/ppermute | solution.py:22
  23.8 0.0 copy-done
  23.8 0.0 copy-done.2
  23.8 3.3 %shard_map.132 = (f32[16,7296]{1,0:T(8,128)S(1)}, bf16[16,7296]{1,0:T(8,128)(2,1)S(1)}) custom-call(bf16[4,16,512]{2,1,0:T(8,128)(2,1)S(1)} %get-tuple-element.48.after.refs_0_, bf16[4,16,512]{2,1,0:T(8,128)(2,1)S(1)} %collective-permute-done.2.refs_1_, bf16[4,16,512]{2,1,0:T(8,128)(2,1)S(1)} %collective-permute-done.3.refs_2_, ...), custom_call_target="tpu_custom_call" | custom-call | tf_op jit(solution)/shard_map/pallas_call | solution.py:249
  27.1 0.0 collective-permute-start.5
  27.2 1.5 %collective-permute-done.5.refs_1_ = bf16[16,7296]{1,0:T(8,128)(2,1)S(1)} collective-permute-done((bf16[16,7296]{1,0:T(8,128)(2,1)S(1)}, bf16[16,7296]{1,0:T(8,128)(2,1)S(1)}, u32[]{:S(2)}, u32[]{:S(2)}) %collective-permute-start.5) | collective-permute-done | bytes 233504 | tf_op jit(solution)/shard_map/ppermute | solution.py:22
  28.6 0.1 shard_map.133
  28.7 1.6 %collective-permute-start.6 = (bf16[8,7296]{1,0:T(8,128)(2,1)S(1)}, bf16[8,7296]{1,0:T(8,128)(2,1)S(1)}, u32[]{:S(2)}, u32[]{:S(2)}) collective-permute-start(bf16[8,7296]{1,0:T(8,128)(2,1)S(1)} %get-tuple-element.58.after), channel_id=1, source_target_pairs={{0,2},{1,3},{2,0},{3,1},{4,6},{5,7},{6,4},{7,5},{8,10},{9,11},{10,... | collective-permute-start | bytes 350216 | tf_op jit(solution)/shard_map/ppermute | solution.py:22
  30.3 3.2 %shard_map.134 = (bf16[3584,1024]{1,0:T(8,128)(2,1)S(1)}, f32[8,128]{1,0:T(8,128)S(1)}) custom-call(bf16[7168,1024]{1,0:T(8,128)(2,1)} %bitcast.8, bf16[8,7296]{1,0:T(8,128)(2,1)S(1)} %get-tuple-element.58.after), custom_call_target="tpu_custom_call" | custom-call | bytes 14680064 | tf_op jit(solution)/shard_map/pallas_call | solution.py:67
  33.5 0.5 collective-permute-done.6.refs_1_
  34.0 0.1 collective-permute-start.7
  34.1 3.2 %shard_map.136 = (bf16[3584,1024]{1,0:T(8,128)(2,1)S(1)}, f32[8,128]{1,0:T(8,128)S(1)}) custom-call(bf16[7168,1024]{1,0:T(8,128)(2,1)} %bitcast.9, bf16[8,7296]{1,0:T(8,128)(2,1)S(1)} %get-tuple-element.61.after), custom_call_target="tpu_custom_call" | custom-call | bytes 14680064 | tf_op jit(solution)/shard_map/pallas_call | solution.py:67
  37.3 1.6 %collective-permute-done.7.refs_1_ = bf16[8,7296]{1,0:T(8,128)(2,1)S(1)} collective-permute-done((bf16[8,7296]{1,0:T(8,128)(2,1)S(1)}, bf16[8,7296]{1,0:T(8,128)(2,1)S(1)}, u32[]{:S(2)}, u32[]{:S(2)}) %collective-permute-start.7) | collective-permute-done | bytes 116768 | tf_op jit(solution)/shard_map/ppermute | solution.py:22
  38.9 0.1 shard_map.137
  39.0 0.9 %collective-permute-start.8 = (bf16[8,7296]{1,0:T(8,128)(2,1)S(1)}, bf16[8,7296]{1,0:T(8,128)(2,1)S(1)}, u32[]{:S(2)}, u32[]{:S(2)}) collective-permute-start(bf16[8,7296]{1,0:T(8,128)(2,1)S(1)} %get-tuple-element.64.after), channel_id=1, source_target_pairs={{0,8},{1,9},{2,10},{3,11},{4,12},{5,13},{6,14},{7,15},{8,0},{9,1},... | collective-permute-start | bytes 350216 | tf_op jit(solution)/shard_map/ppermute | solution.py:22
  39.8 0.0 copy-start.1
  39.8 3.2 %shard_map.138 = (bf16[3584,1024]{1,0:T(8,128)(2,1)S(1)}, f32[8,128]{1,0:T(8,128)S(1)}) custom-call(bf16[7168,1024]{1,0:T(8,128)(2,1)} %bitcast.10, bf16[8,7296]{1,0:T(8,128)(2,1)S(1)} %get-tuple-element.64.after), custom_call_target="tpu_custom_call" | custom-call | bytes 14680064 | tf_op jit(solution)/shard_map/pallas_call | solution.py:67
  43.0 2.8 %collective-permute-done.8.refs_1_ = bf16[8,7296]{1,0:T(8,128)(2,1)S(1)} collective-permute-done((bf16[8,7296]{1,0:T(8,128)(2,1)S(1)}, bf16[8,7296]{1,0:T(8,128)(2,1)S(1)}, u32[]{:S(2)}, u32[]{:S(2)}) %collective-permute-start.8) | collective-permute-done | bytes 116768 | tf_op jit(solution)/shard_map/ppermute | solution.py:22
  45.9 0.0 copy-done.1
  45.9 0.2 shard_map.139
  46.1 1.6 %collective-permute-start.9 = (bf16[8,7296]{1,0:T(8,128)(2,1)S(1)}, bf16[8,7296]{1,0:T(8,128)(2,1)S(1)}, u32[]{:S(2)}, u32[]{:S(2)}) collective-permute-start(bf16[8,7296]{1,0:T(8,128)(2,1)S(1)} %get-tuple-element.67.after.refs_0_), channel_id=1, source_target_pairs={{0,2},{1,3},{2,0},{3,1},{4,6},{5,7},{6,4},{7,5},{8,10},{9,11},{10,... | collective-permute-start | bytes 350216 | tf_op jit(solution)/shard_map/ppermute | solution.py:22
  47.6 3.2 %shard_map.140 = (bf16[3584,1024]{1,0:T(8,128)(2,1)S(1)}, f32[8,128]{1,0:T(8,128)S(1)}) custom-call(bf16[7168,1024]{1,0:T(8,128)(2,1)} %bitcast.11, bf16[8,7296]{1,0:T(8,128)(2,1)S(1)} %get-tuple-element.67.after.refs_0_), custom_call_target="tpu_custom_call" | custom-call | bytes 14680064 | tf_op jit(solution)/shard_map/pallas_call | solution.py:67
  50.8 0.1 collective-permute-done.9.refs_1_
  51.0 0.1 collective-permute-start.10
  51.0 1.5 %collective-permute-done.10.second = bf16[16,7296]{1,0:T(8,128)(2,1)S(1)} collective-permute-done((bf16[16,7296]{1,0:T(8,128)(2,1)S(1)}, bf16[16,7296]{1,0:T(8,128)(2,1)S(1)}, u32[]{:S(2)}, u32[]{:S(2)}) %collective-permute-start.10) | collective-permute-done | bytes 233504 | tf_op jit(solution)/shard_map/ppermute | solution.py:22
  52.5 8.3 %shard_map.142 = (f32[16,7168]{1,0:T(8,128)S(1)}, bf16[16,7168]{1,0:T(8,128)(2,1)S(1)}) custom-call(s32[1]{0:T(128)} %bitcast.me, bf16[16,7296]{1,0:T(8,128)(2,1)S(1)} %shard_map.141.first, bf16[16,7296]{1,0:T(8,128)(2,1)S(1)} %collective-permute-done.10.second, bf16[3584,1024]{1,0:T(8,128)(2,1)S(1)} %get-tuple-element.69.gate_top, ...), custom_call_target="tpu_custom_call" | custom-call | tf_op jit(solution)/shard_map/pallas_call | solution.py:378
  60.9 0.2 collective-permute-start.11
  61.1 1.4 %collective-permute-done.11.refs_1_ = bf16[16,7168]{1,0:T(8,128)(2,1)S(1)} collective-permute-done((bf16[16,7168]{1,0:T(8,128)(2,1)S(1)}, bf16[16,7168]{1,0:T(8,128)(2,1)S(1)}, u32[]{:S(2)}, u32[]{:S(2)}) %collective-permute-start.11) | collective-permute-done | bytes 229408 | tf_op jit(solution)/shard_map/ppermute | solution.py:22
  62.5 1.6 %collective-permute-start.12 = (bf16[8,7168]{1,0:T(8,128)(2,1)S(1)}, bf16[8,7168]{1,0:T(8,128)(2,1)S(1)}, u32[]{:S(2)}, u32[]{:S(2)}) collective-permute-start(bf16[8,7168]{1,0:T(8,128)(2,1)S(1)} %get-tuple-element.76), channel_id=1, source_target_pairs={{0,2},{1,3},{2,0},{3,1},{4,6},{5,7},{6,4},{7,5},{8,10},{9,11},{10,... | collective-permute-start | bytes 344072 | tf_op jit(solution)/shard_map/ppermute | solution.py:22
  64.0 3.7 %collective-permute-done.12.refs_1_ = bf16[8,7168]{1,0:T(8,128)(2,1)S(1)} collective-permute-done((bf16[8,7168]{1,0:T(8,128)(2,1)S(1)}, bf16[8,7168]{1,0:T(8,128)(2,1)S(1)}, u32[]{:S(2)}, u32[]{:S(2)}) %collective-permute-start.12) | collective-permute-done | bytes 114720 | tf_op jit(solution)/shard_map/ppermute | solution.py:22
  67.8 0.1 collective-permute-start.13
  67.8 4.2 %collective-permute-done.13.refs_1_ = bf16[4,7168]{1,0:T(4,128)(2,1)S(1)} collective-permute-done((bf16[4,7168]{1,0:T(4,128)(2,1)S(1)}, bf16[4,7168]{1,0:T(4,128)(2,1)S(1)}, u32[]{:S(2)}, u32[]{:S(2)}) %collective-permute-start.13) | collective-permute-done | bytes 57376 | tf_op jit(solution)/shard_map/ppermute | solution.py:22
  72.0 0.4 collective-permute-start.14
  72.5 4.4 %collective-permute-done.14 = bf16[2,7168]{1,0:T(2,128)(2,1)S(1)} collective-permute-done((bf16[2,7168]{1,0:T(2,128)(2,1)S(1)}, bf16[2,7168]{1,0:T(2,128)(2,1)S(1)}, u32[]{:S(2)}, u32[]{:S(2)}) %collective-permute-start.14) | collective-permute-done | bytes 28704 | tf_op jit(solution)/shard_map/ppermute | solution.py:22
  76.9 0.7 add_convert_fusion
  (8 shorter events, 0.2 us)
Async XLA Ops:
  5.0 1.5 %collective-permute-start = (bf16[8,16,512]{2,1,0:T(8,128)(2,1)S(1)}, bf16[8,16,512]{2,1,0:T(8,128)(2,1)S(1)}, u32[]{:S(2)}, u32[]{:S(2)}) collective-permute-start(bf16[8,16,512]{2,1,0:T(8,128)(2,1)S(1)} %get-tuple-element.44), channel_id=1, source_target_pairs={{0,1},{1,0},{2,3},{3,2},{4,5},{5,4},{6,7},{7,6},{8,9},{9,8},{10,11... | collective-permute-start | bytes 393224 | tf_op jit(solution)/shard_map/ppermute | solution.py:22
  6.5 6.7 %collective-permute-start.1 = (bf16[8,16,512]{2,1,0:T(8,128)(2,1)S(1)}, bf16[8,16,512]{2,1,0:T(8,128)(2,1)S(1)}, u32[]{:S(2)}, u32[]{:S(2)}) collective-permute-start(bf16[8,16,512]{2,1,0:T(8,128)(2,1)S(1)} %get-tuple-element.46.after), channel_id=1, source_target_pairs={{0,2},{1,3},{2,0},{3,1},{4,6},{5,7},{6,4},{7,5},{8,10},{9,11},{10,... | collective-permute-start | bytes 393224 | tf_op jit(solution)/shard_map/ppermute | solution.py:22
  13.3 8.4 %collective-permute-start.2 = (bf16[4,16,512]{2,1,0:T(8,128)(2,1)S(1)}, bf16[4,16,512]{2,1,0:T(8,128)(2,1)S(1)}, u32[]{:S(2)}, u32[]{:S(2)}) collective-permute-start(bf16[4,16,512]{2,1,0:T(8,128)(2,1)S(1)} %get-tuple-element.49), channel_id=1, source_target_pairs={{0,8},{1,9},{2,10},{3,11},{4,12},{5,13},{6,14},{7,15},{8,0},{9,1},... | collective-permute-start | bytes 196616 | tf_op jit(solution)/shard_map/ppermute | solution.py:22
  16.2 5.5 %collective-permute-start.3 = (bf16[4,16,512]{2,1,0:T(8,128)(2,1)S(1)}, bf16[4,16,512]{2,1,0:T(8,128)(2,1)S(1)}, u32[]{:S(2)}, u32[]{:S(2)}) collective-permute-start(bf16[4,16,512]{2,1,0:T(8,128)(2,1)S(1)} %get-tuple-element.50), channel_id=1, source_target_pairs={{0,4},{1,5},{2,6},{3,7},{4,0},{5,1},{6,2},{7,3},{8,12},{9,13},{10,... | collective-permute-start | bytes 196616 | tf_op jit(solution)/shard_map/ppermute | solution.py:22
  17.7 6.1 %collective-permute-start.4 = (bf16[4,16,512]{2,1,0:T(8,128)(2,1)S(1)}, bf16[4,16,512]{2,1,0:T(8,128)(2,1)S(1)}, u32[]{:S(2)}, u32[]{:S(2)}) collective-permute-start(bf16[4,16,512]{2,1,0:T(8,128)(2,1)S(1)} %get-tuple-element.51), channel_id=1, source_target_pairs={{0,12},{1,13},{2,14},{3,15},{4,8},{5,9},{6,10},{7,11},{8,4},{9,5},... | collective-permute-start | bytes 196616 | tf_op jit(solution)/shard_map/ppermute | solution.py:22
  17.8 6.0 %copy-start = (bf16[2,7168]{1,0:T(2,128)(2,1)S(1)}, bf16[2,7168]{1,0:T(2,128)(2,1)}, u32[]{:S(2)}) copy-start(bf16[2,7168]{1,0:T(2,128)(2,1)} %refs_8_.1) | copy-start | bytes 86020
  17.8 6.0 %copy-start.2 = (s32[32,1]{1,0:T(8,128)S(1)}, s32[32,1]{1,0:T(8,128)}, u32[]{:S(2)}) copy-start(s32[32,1]{1,0:T(8,128)} %constant.23.refs_4_) | copy-start | bytes 388
  27.1 1.5 %collective-permute-start.5 = (bf16[16,7296]{1,0:T(8,128)(2,1)S(1)}, bf16[16,7296]{1,0:T(8,128)(2,1)S(1)}, u32[]{:S(2)}, u32[]{:S(2)}) collective-permute-start(bf16[16,7296]{1,0:T(8,128)(2,1)S(1)} %get-tuple-element.56), channel_id=1, source_target_pairs={{0,1},{1,0},{2,3},{3,2},{4,5},{5,4},{6,7},{7,6},{8,9},{9,8},{10,11... | collective-permute-start | bytes 700424 | tf_op jit(solution)/shard_map/ppermute | solution.py:22
  28.7 5.3 %collective-permute-start.6 = (bf16[8,7296]{1,0:T(8,128)(2,1)S(1)}, bf16[8,7296]{1,0:T(8,128)(2,1)S(1)}, u32[]{:S(2)}, u32[]{:S(2)}) collective-permute-start(bf16[8,7296]{1,0:T(8,128)(2,1)S(1)} %get-tuple-element.58.after), channel_id=1, source_target_pairs={{0,2},{1,3},{2,0},{3,1},{4,6},{5,7},{6,4},{7,5},{8,10},{9,11},{10,... | collective-permute-start | bytes 350216 | tf_op jit(solution)/shard_map/ppermute | solution.py:22
  34.0 4.9 %collective-permute-start.7 = (bf16[8,7296]{1,0:T(8,128)(2,1)S(1)}, bf16[8,7296]{1,0:T(8,128)(2,1)S(1)}, u32[]{:S(2)}, u32[]{:S(2)}) collective-permute-start(bf16[8,7296]{1,0:T(8,128)(2,1)S(1)} %get-tuple-element.61.after), channel_id=1, source_target_pairs={{0,4},{1,5},{2,6},{3,7},{4,0},{5,1},{6,2},{7,3},{8,12},{9,13},{10,... | collective-permute-start | bytes 350216 | tf_op jit(solution)/shard_map/ppermute | solution.py:22
  39.0 6.9 %collective-permute-start.8 = (bf16[8,7296]{1,0:T(8,128)(2,1)S(1)}, bf16[8,7296]{1,0:T(8,128)(2,1)S(1)}, u32[]{:S(2)}, u32[]{:S(2)}) collective-permute-start(bf16[8,7296]{1,0:T(8,128)(2,1)S(1)} %get-tuple-element.64.after), channel_id=1, source_target_pairs={{0,8},{1,9},{2,10},{3,11},{4,12},{5,13},{6,14},{7,15},{8,0},{9,1},... | collective-permute-start | bytes 350216 | tf_op jit(solution)/shard_map/ppermute | solution.py:22
  39.8 6.0 %copy-start.1 = (f32[7168]{0:T(1024)S(1)}, f32[7168]{0:T(1024)}, u32[]{:S(2)}) copy-start(f32[7168]{0:T(1024)} %param.19) | copy-start | bytes 86020
  46.1 4.9 %collective-permute-start.9 = (bf16[8,7296]{1,0:T(8,128)(2,1)S(1)}, bf16[8,7296]{1,0:T(8,128)(2,1)S(1)}, u32[]{:S(2)}, u32[]{:S(2)}) collective-permute-start(bf16[8,7296]{1,0:T(8,128)(2,1)S(1)} %get-tuple-element.67.after.refs_0_), channel_id=1, source_target_pairs={{0,2},{1,3},{2,0},{3,1},{4,6},{5,7},{6,4},{7,5},{8,10},{9,11},{10,... | collective-permute-start | bytes 350216 | tf_op jit(solution)/shard_map/ppermute | solution.py:22
  51.0 1.6 %collective-permute-start.10 = (bf16[16,7296]{1,0:T(8,128)(2,1)S(1)}, bf16[16,7296]{1,0:T(8,128)(2,1)S(1)}, u32[]{:S(2)}, u32[]{:S(2)}) collective-permute-start(bf16[16,7296]{1,0:T(8,128)(2,1)S(1)} %shard_map.141.first), channel_id=1, source_target_pairs={{0,1},{1,0},{2,3},{3,2},{4,5},{5,4},{6,7},{7,6},{8,9},{9,8},{10,11... | collective-permute-start | bytes 700424 | tf_op jit(solution)/shard_map/ppermute | solution.py:22
  60.9 1.6 %collective-permute-start.11 = (bf16[16,7168]{1,0:T(8,128)(2,1)S(1)}, bf16[16,7168]{1,0:T(8,128)(2,1)S(1)}, u32[]{:S(2)}, u32[]{:S(2)}) collective-permute-start(bf16[16,7168]{1,0:T(8,128)(2,1)S(1)} %get-tuple-element.74), channel_id=1, source_target_pairs={{0,1},{1,0},{2,3},{3,2},{4,5},{5,4},{6,7},{7,6},{8,9},{9,8},{10,11... | collective-permute-start | bytes 688136 | tf_op jit(solution)/shard_map/ppermute | solution.py:22
  62.5 5.3 %collective-permute-start.12 = (bf16[8,7168]{1,0:T(8,128)(2,1)S(1)}, bf16[8,7168]{1,0:T(8,128)(2,1)S(1)}, u32[]{:S(2)}, u32[]{:S(2)}) collective-permute-start(bf16[8,7168]{1,0:T(8,128)(2,1)S(1)} %get-tuple-element.76), channel_id=1, source_target_pairs={{0,2},{1,3},{2,0},{3,1},{4,6},{5,7},{6,4},{7,5},{8,10},{9,11},{10,... | collective-permute-start | bytes 344072 | tf_op jit(solution)/shard_map/ppermute | solution.py:22
  67.8 4.2 %collective-permute-start.13 = (bf16[4,7168]{1,0:T(4,128)(2,1)S(1)}, bf16[4,7168]{1,0:T(4,128)(2,1)S(1)}, u32[]{:S(2)}, u32[]{:S(2)}) collective-permute-start(bf16[4,7168]{1,0:T(4,128)(2,1)S(1)} %get-tuple-element.78), channel_id=1, source_target_pairs={{0,4},{1,5},{2,6},{3,7},{4,0},{5,1},{6,2},{7,3},{8,12},{9,13},{10,... | collective-permute-start | bytes 172040 | tf_op jit(solution)/shard_map/ppermute | solution.py:22
  72.0 4.8 %collective-permute-start.14 = (bf16[2,7168]{1,0:T(2,128)(2,1)S(1)}, bf16[2,7168]{1,0:T(2,128)(2,1)S(1)}, u32[]{:S(2)}, u32[]{:S(2)}) collective-permute-start(bf16[2,7168]{1,0:T(2,128)(2,1)S(1)} %get-tuple-element.80), channel_id=1, source_target_pairs={{0,8},{1,9},{2,10},{3,11},{4,12},{5,13},{6,14},{7,15},{8,0},{9,1},... | collective-permute-start | bytes 86024 | tf_op jit(solution)/shard_map/ppermute | solution.py:22

commit v7 on v6

--- a/solution.py
+++ b/solution.py
@@ -29,7 +29,6 @@
 LANES = 128
 MIB = 1 << 20
 IN_VMEM = pl.BlockSpec(memory_space=pltpu.VMEM)
-IN_SMEM = pl.BlockSpec(memory_space=pltpu.SMEM)
 IN_HBM = pl.BlockSpec(memory_space=pltpu.HBM)
 VMEM_ARRAY = pltpu.VMEM
 
@@ -102,7 +101,7 @@
 
 
 def attend_kernel(
-    order, lengths_hbm, me, queries_hbm, cache, value_up, kept, sent, value_in, lengths, queries, held, wide, sems
+    order, lengths_hbm, queries_hbm, cache, value_up, kept, sent, value_in, lengths, queries, held, wide, sems
 ):
     rows_dev, _, heads = queries.shape
     context = cache.shape[2]
@@ -126,9 +125,8 @@
         scores = jnp.where(positions < lengths[r], scores, -jnp.inf)
         exp_scores = jnp.exp(scores - jnp.max(scores, axis=1, keepdims=True))
         inverse = 1.0 / jnp.sum(exp_scores, axis=1, keepdims=True)
-        soft_weights = (exp_scores * inverse).astype(jnp.bfloat16)
-        got = lax.dot_general(
-            soft_weights,
+        got = inverse * lax.dot_general(
+            exp_scores.astype(jnp.bfloat16),
             held[r, :latent],
             (((1,), (1,)), ((), ())),
             preferred_element_type=jnp.float32,
@@ -139,13 +137,14 @@
         else:
             kept[r] = got.astype(kept.dtype)
     half = len(order) // 2
+    me = lax.axis_index("ep")
     for p, s in enumerate(order):
         target = (kept, sent)[p // half]
-        target[p % half] = wide[me[0] ^ s].astype(target.dtype)
+        target[p % half] = wide[me ^ s].astype(target.dtype)
     weights.wait()
 
 
-def attend(queries, latent_cache, cache_lengths, value_up, order, me):
+def attend(queries, latent_cache, cache_lengths, value_up, order):
     rows_dev, heads, key_width = queries.shape
     context = latent_cache.shape[1]
     heads_dev, latent, _ = value_up.shape
@@ -159,7 +158,7 @@
             VMEM_ARRAY(spare, jnp.bfloat16),
             VMEM_ARRAY(value_up.shape, value_up.dtype),
         ),
-        in_specs=[IN_HBM, IN_SMEM, IN_HBM, IN_HBM, IN_HBM],
+        in_specs=[IN_HBM] * 4,
         out_specs=(IN_VMEM,) * 3,
         scratch_shapes=[
             pltpu.SMEM((rows_dev,), jnp.int32),
@@ -171,7 +170,6 @@
         compiler_params=pltpu.CompilerParams(vmem_limit_bytes=24 * MIB),
     )(
         in_hbm(cache_lengths),
-        me[None],
         in_hbm(queries.transpose(0, 2, 1)),
         in_hbm(latent_cache.transpose(0, 2, 1)),
         in_hbm(value_up),
@@ -329,7 +327,7 @@
 
 
 def expert_kernel(
-    me, first, second, gate_top, gate_bottom, up_top, up_bottom, down, kept, sent, moe_in, units, down_in, sems
+    first, second, gate_top, gate_bottom, up_top, up_bottom, down, kept, sent, moe_in, units, down_in, sems
 ):
     cut, inner = gate_top.shape
     width = 2 * cut
@@ -341,7 +339,7 @@
     moe_in[half:] = second[...]
     tail = moe_in[:, width:].astype(jnp.float32)
     column = lax.broadcasted_iota(jnp.int32, tail.shape, 1)
-    expert = lax.rem(me[0], EXPERTS)
+    expert = lax.rem(lax.axis_index("ep"), EXPERTS)
     mine = (column == expert) | (column == expert + EXPERTS)
     weight = jnp.sum(jnp.where(mine, tail, 0.0), axis=1, keepdims=True)
 
@@ -371,7 +369,7 @@
         sent[:, columns] = terms[half:].astype(sent.dtype)
 
 
-def run_expert(me, first, second, gate, up, down, limit):
+def run_expert(first, second, gate, up, down, limit):
     rows = 2 * first.shape[0]
     inner, width = down.shape
     shape = (rows // 2, width)
@@ -381,7 +379,7 @@
             jax.ShapeDtypeStruct(shape, jnp.float32),
             jax.ShapeDtypeStruct(shape, jnp.bfloat16),
         ),
-        in_specs=[IN_SMEM] + [IN_VMEM] * 6 + [IN_HBM],
+        in_specs=[IN_VMEM] * 6 + [IN_HBM],
         out_specs=(IN_VMEM, IN_VMEM),
         scratch_shapes=[
             pltpu.VMEM((rows, first.shape[1]), jnp.bfloat16),
@@ -390,7 +388,7 @@
             pltpu.SemaphoreType.DMA((4,)),
         ],
         compiler_params=pltpu.CompilerParams(vmem_limit_bytes=limit + 2 * down.size),
-    )(me, first, second, *[in_vmem(w) for w in gate + up], in_hbm(down))
+    )(first, second, *[in_vmem(w) for w in gate + up], in_hbm(down))
 
 
 def on_device(
@@ -428,7 +426,7 @@
     limit = grant(rows_in, width)
     gate, up, down = gate_proj[0], up_proj[0], down_proj[0]
     if heads_dev % 8 == 0:
-        kept, sent, value_up = attend(queries, latent_cache, cache_lengths, value_up, order, me)
+        kept, sent, value_up = attend(queries, latent_cache, cache_lengths, value_up, order)
         run = ep_size >> 2
         got = exchange(sent, 0)
         kept, sent = deal((kept, got), 2, run, limit)
@@ -441,7 +439,7 @@
         held = [mask | x << 1 | core for mask in masks for x in range(2) for core in range(2)]
         row_of = jnp.array([held.index(s) * rows_dev + r for s in order for r in range(rows_dev)])
     else:
-        out, _, value_up = attend(queries, latent_cache, cache_lengths, value_up, (), me)
+        out, _, value_up = attend(queries, latent_cache, cache_lengths, value_up, ())
         top, _ = load(out_proj, value_up, limit, 0)
         bottom, _ = load(out_proj, value_up, limit, 1)
         out = out.reshape(rows_dev, ep_size, heads_dev, latent).transpose(1, 0, 2, 3)
@@ -484,7 +482,7 @@
     if split_ways == 1:
         while later:
             beside(moe_in)
-        kept, sent = run_expert(me[None], moe_in, other, halves[:2], halves[2:], down, limit)
+        kept, sent = run_expert(moe_in, other, halves[:2], halves[2:], down, limit)
     else:
         moe_in = jnp.concatenate((moe_in, other), axis=0)
         expert = me % EXPERTS

time: 77.7 us -> 77.5 us (level)
  no operation moved by 1% of the time
where the time goes in v7:
time: 77.5 us; the launch traced here: 77.4 us
  Pallas kernels  36.7 us (47%)
  waiting for transfers between devices  24.7 us (32%)
  starting transfers between devices  14.3 us (18%)
  other arithmetic  1.51 us (2%)
    ppermute x15, waiting for transfers between devices, trade(): lax.ppermute(value, 'ep', [(i, i ^ mask) for i in range(lax.axis_size('ep...  24.7 us
    pallas_call x6, Pallas kernels, load(): pl.pallas_call(functools.partial(load_kernel, part * rows), out_shape=(VM...  19.7 us
    ppermute x15, starting transfers between devices, trade(): lax.ppermute(value, 'ep', [(i, i ^ mask) for i in range(lax.axis_size('ep...  14.3 us
    pallas_call x1, Pallas kernels, run_expert(): pl.pallas_call(expert_kernel, out_shape=(jax.ShapeDtypeStruct(shape, jnp....  8.3 us
    pallas_call x1, Pallas kernels, attend(): pl.pallas_call(functools.partial(attend_kernel, order), out_shape=(VMEM_A...  4.83 us
    pallas_call x1, Pallas kernels, project(): pl.pallas_call(functools.partial(project_kernel, width // 2, len(by_head)...  3.3 us
  transfers between devices with their start and end apart: 15, of which 13 were waited for; matrix products, arithmetic and copies ran while one was open for 1% of the time, Pallas kernels for 25%

profile of v7, /device:TPU:0, one launch (start us, length us, event | category | flops | bytes accessed | tf_op | source)
XLA Modules:
  0.0 77.4 jit_solution(15542483781390330814)
XLA Ops:
  0.0 4.8 %shard_map.127 = (bf16[8,16,512]{2,1,0:T(8,128)(2,1)S(1)}, bf16[8,16,512]{2,1,0:T(8,128)(2,1)S(1)}, bf16[8,512,128]{2,1,0:T(8,128)(2,1)S(1)}) custom-call(s32[2]{0:T(128)} %lengths_hbm.1, bf16[2,576,128]{2,1,0:T(8,128)(2,1)} %bitcast.13, bf16[2,576,2048]{2,1,0:T(8,128)(2,1)} %bitcast.12, bf16[8,512,128]{2,1,0:T(8,128)(2,1)} %value_up.1), custom_call_target="tpu_custom_call" | custom-call | tf_op jit(solution)/shard_map/pallas_call | solution.py:154
  4.8 0.5 collective-permute-start
  5.4 0.8 %select_reduce_fusion = f32[2,16]{1,0:T(2,128)S(1)} fusion(f32[2,8]{1,0:T(2,128)} %param.21, s32[2,8]{1,0:T(2,128)} %param.20), kind=kLoop, calls=%fused_computation.1 | loop fusion | flops 736 | bytes 256 | tf_op jit(solution)/shard_map/reduce_sum | solution.py:419
  6.1 0.2 collective-permute-done.refs_1_
  6.4 2.9 %collective-permute-start.1 = (bf16[8,16,512]{2,1,0:T(8,128)(2,1)S(1)}, bf16[8,16,512]{2,1,0:T(8,128)(2,1)S(1)}, u32[]{:S(2)}, u32[]{:S(2)}) collective-permute-start(bf16[8,16,512]{2,1,0:T(8,128)(2,1)S(1)} %get-tuple-element.46.after), channel_id=1, source_target_pairs={{0,2},{1,3},{2,0},{3,1},{4,6},{5,7},{6,4},{7,5},{8,10},{9,11},{10,... | collective-permute-start | bytes 393224 | tf_op jit(solution)/shard_map/ppermute | solution.py:22
  9.3 3.2 %shard_map.129 = (bf16[512,7168]{1,0:T(8,128)(2,1)S(1)}, f32[8,128]{1,0:T(8,128)S(1)}) custom-call(bf16[1024,7168]{1,0:T(8,128)(2,1)} %source.3, bf16[8,16,512]{2,1,0:T(8,128)(2,1)S(1)} %get-tuple-element.46.after), custom_call_target="tpu_custom_call" | custom-call | bytes 14680064 | tf_op jit(solution)/shard_map/pallas_call | solution.py:66
  12.5 0.6 collective-permute-done.1.refs_1_
  13.1 2.9 %collective-permute-start.2 = (bf16[4,16,512]{2,1,0:T(8,128)(2,1)S(1)}, bf16[4,16,512]{2,1,0:T(8,128)(2,1)S(1)}, u32[]{:S(2)}, u32[]{:S(2)}) collective-permute-start(bf16[4,16,512]{2,1,0:T(8,128)(2,1)S(1)} %get-tuple-element.49), channel_id=1, source_target_pairs={{0,8},{1,9},{2,10},{3,11},{4,12},{5,13},{6,14},{7,15},{8,0},{9,1},... | collective-permute-start | bytes 196616 | tf_op jit(solution)/shard_map/ppermute | solution.py:22
  16.0 1.6 %collective-permute-start.3 = (bf16[4,16,512]{2,1,0:T(8,128)(2,1)S(1)}, bf16[4,16,512]{2,1,0:T(8,128)(2,1)S(1)}, u32[]{:S(2)}, u32[]{:S(2)}) collective-permute-start(bf16[4,16,512]{2,1,0:T(8,128)(2,1)S(1)} %get-tuple-element.50), channel_id=1, source_target_pairs={{0,4},{1,5},{2,6},{3,7},{4,0},{5,1},{6,2},{7,3},{8,12},{9,13},{10,... | collective-permute-start | bytes 196616 | tf_op jit(solution)/shard_map/ppermute | solution.py:22
  17.6 0.0 collective-permute-start.4
  17.6 0.1 select_maximum_fusion.refs_9_
  17.7 0.0 copy-start
  17.7 0.0 copy-start.2
  17.7 3.8 %shard_map.131 = (bf16[512,7168]{1,0:T(8,128)(2,1)S(1)}, f32[8,128]{1,0:T(8,128)}) custom-call(bf16[1024,7168]{1,0:T(8,128)(2,1)} %source.3, bf16[4,16,512]{2,1,0:T(8,128)(2,1)S(1)} %get-tuple-element.48.after.refs_0_), custom_call_target="tpu_custom_call" | custom-call | bytes 14680064 | tf_op jit(solution)/shard_map/pallas_call | solution.py:66
  21.5 0.0 collective-permute-done.2.refs_1_
  21.5 0.0 collective-permute-done.3.refs_2_
  21.5 2.2 %collective-permute-done.4.refs_3_ = bf16[4,16,512]{2,1,0:T(8,128)(2,1)S(1)} collective-permute-done((bf16[4,16,512]{2,1,0:T(8,128)(2,1)S(1)}, bf16[4,16,512]{2,1,0:T(8,128)(2,1)S(1)}, u32[]{:S(2)}, u32[]{:S(2)}) %collective-permute-start.4) | collective-permute-done | bytes 65568 | tf_op jit(solution)/shard_map/ppermute | solution.py:22
  23.7 0.0 copy-done
  23.7 0.0 copy-done.2
  23.7 3.3 %shard_map.132 = (f32[16,7296]{1,0:T(8,128)S(1)}, bf16[16,7296]{1,0:T(8,128)(2,1)S(1)}) custom-call(bf16[4,16,512]{2,1,0:T(8,128)(2,1)S(1)} %get-tuple-element.48.after.refs_0_, bf16[4,16,512]{2,1,0:T(8,128)(2,1)S(1)} %collective-permute-done.2.refs_1_, bf16[4,16,512]{2,1,0:T(8,128)(2,1)S(1)} %collective-permute-done.3.refs_2_, ...), custom_call_target="tpu_custom_call" | custom-call | tf_op jit(solution)/shard_map/pallas_call | solution.py:247
  27.0 0.0 collective-permute-start.5
  27.0 1.5 %collective-permute-done.5.refs_1_ = bf16[16,7296]{1,0:T(8,128)(2,1)S(1)} collective-permute-done((bf16[16,7296]{1,0:T(8,128)(2,1)S(1)}, bf16[16,7296]{1,0:T(8,128)(2,1)S(1)}, u32[]{:S(2)}, u32[]{:S(2)}) %collective-permute-start.5) | collective-permute-done | bytes 233504 | tf_op jit(solution)/shard_map/ppermute | solution.py:22
  28.5 0.1 shard_map.133
  28.5 1.6 %collective-permute-start.6 = (bf16[8,7296]{1,0:T(8,128)(2,1)S(1)}, bf16[8,7296]{1,0:T(8,128)(2,1)S(1)}, u32[]{:S(2)}, u32[]{:S(2)}) collective-permute-start(bf16[8,7296]{1,0:T(8,128)(2,1)S(1)} %get-tuple-element.58.after), channel_id=1, source_target_pairs={{0,2},{1,3},{2,0},{3,1},{4,6},{5,7},{6,4},{7,5},{8,10},{9,11},{10,... | collective-permute-start | bytes 350216 | tf_op jit(solution)/shard_map/ppermute | solution.py:22
  30.1 3.2 %shard_map.134 = (bf16[3584,1024]{1,0:T(8,128)(2,1)S(1)}, f32[8,128]{1,0:T(8,128)S(1)}) custom-call(bf16[7168,1024]{1,0:T(8,128)(2,1)} %bitcast.7, bf16[8,7296]{1,0:T(8,128)(2,1)S(1)} %get-tuple-element.58.after), custom_call_target="tpu_custom_call" | custom-call | bytes 14680064 | tf_op jit(solution)/shard_map/pallas_call | solution.py:66
  33.3 0.5 collective-permute-done.6.refs_1_
  33.9 0.1 collective-permute-start.7
  34.0 3.2 %shard_map.136 = (bf16[3584,1024]{1,0:T(8,128)(2,1)S(1)}, f32[8,128]{1,0:T(8,128)S(1)}) custom-call(bf16[7168,1024]{1,0:T(8,128)(2,1)} %bitcast.8, bf16[8,7296]{1,0:T(8,128)(2,1)S(1)} %get-tuple-element.61.after), custom_call_target="tpu_custom_call" | custom-call | bytes 14680064 | tf_op jit(solution)/shard_map/pallas_call | solution.py:66
  37.2 1.6 %collective-permute-done.7.refs_1_ = bf16[8,7296]{1,0:T(8,128)(2,1)S(1)} collective-permute-done((bf16[8,7296]{1,0:T(8,128)(2,1)S(1)}, bf16[8,7296]{1,0:T(8,128)(2,1)S(1)}, u32[]{:S(2)}, u32[]{:S(2)}) %collective-permute-start.7) | collective-permute-done | bytes 116768 | tf_op jit(solution)/shard_map/ppermute | solution.py:22
  38.8 0.1 shard_map.137
  38.8 0.9 %collective-permute-start.8 = (bf16[8,7296]{1,0:T(8,128)(2,1)S(1)}, bf16[8,7296]{1,0:T(8,128)(2,1)S(1)}, u32[]{:S(2)}, u32[]{:S(2)}) collective-permute-start(bf16[8,7296]{1,0:T(8,128)(2,1)S(1)} %get-tuple-element.64.after), channel_id=1, source_target_pairs={{0,8},{1,9},{2,10},{3,11},{4,12},{5,13},{6,14},{7,15},{8,0},{9,1},... | collective-permute-start | bytes 350216 | tf_op jit(solution)/shard_map/ppermute | solution.py:22
  39.7 0.0 copy-start.1
  39.7 3.2 %shard_map.138 = (bf16[3584,1024]{1,0:T(8,128)(2,1)S(1)}, f32[8,128]{1,0:T(8,128)S(1)}) custom-call(bf16[7168,1024]{1,0:T(8,128)(2,1)} %bitcast.9, bf16[8,7296]{1,0:T(8,128)(2,1)S(1)} %get-tuple-element.64.after), custom_call_target="tpu_custom_call" | custom-call | bytes 14680064 | tf_op jit(solution)/shard_map/pallas_call | solution.py:66
  42.9 2.8 %collective-permute-done.8.refs_1_ = bf16[8,7296]{1,0:T(8,128)(2,1)S(1)} collective-permute-done((bf16[8,7296]{1,0:T(8,128)(2,1)S(1)}, bf16[8,7296]{1,0:T(8,128)(2,1)S(1)}, u32[]{:S(2)}, u32[]{:S(2)}) %collective-permute-start.8) | collective-permute-done | bytes 116768 | tf_op jit(solution)/shard_map/ppermute | solution.py:22
  45.7 0.0 copy-done.1
  45.7 0.2 shard_map.139
  45.9 1.6 %collective-permute-start.9 = (bf16[8,7296]{1,0:T(8,128)(2,1)S(1)}, bf16[8,7296]{1,0:T(8,128)(2,1)S(1)}, u32[]{:S(2)}, u32[]{:S(2)}) collective-permute-start(bf16[8,7296]{1,0:T(8,128)(2,1)S(1)} %get-tuple-element.67.after.refs_0_), channel_id=1, source_target_pairs={{0,2},{1,3},{2,0},{3,1},{4,6},{5,7},{6,4},{7,5},{8,10},{9,11},{10,... | collective-permute-start | bytes 350216 | tf_op jit(solution)/shard_map/ppermute | solution.py:22
  47.5 3.2 %shard_map.140 = (bf16[3584,1024]{1,0:T(8,128)(2,1)S(1)}, f32[8,128]{1,0:T(8,128)S(1)}) custom-call(bf16[7168,1024]{1,0:T(8,128)(2,1)} %bitcast.10, bf16[8,7296]{1,0:T(8,128)(2,1)S(1)} %get-tuple-element.67.after.refs_0_), custom_call_target="tpu_custom_call" | custom-call | bytes 14680064 | tf_op jit(solution)/shard_map/pallas_call | solution.py:66
  50.7 0.1 collective-permute-done.9.refs_1_
  50.8 0.1 collective-permute-start.10
  50.9 1.5 %collective-permute-done.10.second = bf16[16,7296]{1,0:T(8,128)(2,1)S(1)} collective-permute-done((bf16[16,7296]{1,0:T(8,128)(2,1)S(1)}, bf16[16,7296]{1,0:T(8,128)(2,1)S(1)}, u32[]{:S(2)}, u32[]{:S(2)}) %collective-permute-start.10) | collective-permute-done | bytes 233504 | tf_op jit(solution)/shard_map/ppermute | solution.py:22
  52.4 8.3 %shard_map.142 = (f32[16,7168]{1,0:T(8,128)S(1)}, bf16[16,7168]{1,0:T(8,128)(2,1)S(1)}) custom-call(bf16[16,7296]{1,0:T(8,128)(2,1)S(1)} %shard_map.141.first, bf16[16,7296]{1,0:T(8,128)(2,1)S(1)} %collective-permute-done.10.second, bf16[3584,1024]{1,0:T(8,128)(2,1)S(1)} %get-tuple-element.69.gate_top, bf16[3584,1024]{1,0:T(8,128)(2,1)S(1)} %get-tuple-element.70.gate_bottom, ...), custom_call_target="tpu_custom_call" | custom-call | tf_op jit(solution)/shard_map/pallas_call | solution.py:376
  60.7 0.2 collective-permute-start.11
  60.9 1.4 %collective-permute-done.11.refs_1_ = bf16[16,7168]{1,0:T(8,128)(2,1)S(1)} collective-permute-done((bf16[16,7168]{1,0:T(8,128)(2,1)S(1)}, bf16[16,7168]{1,0:T(8,128)(2,1)S(1)}, u32[]{:S(2)}, u32[]{:S(2)}) %collective-permute-start.11) | collective-permute-done | bytes 229408 | tf_op jit(solution)/shard_map/ppermute | solution.py:22
  62.2 0.1 shard_map.143
  62.3 1.6 %collective-permute-start.12 = (bf16[8,7168]{1,0:T(8,128)(2,1)S(1)}, bf16[8,7168]{1,0:T(8,128)(2,1)S(1)}, u32[]{:S(2)}, u32[]{:S(2)}) collective-permute-start(bf16[8,7168]{1,0:T(8,128)(2,1)S(1)} %get-tuple-element.76), channel_id=1, source_target_pairs={{0,2},{1,3},{2,0},{3,1},{4,6},{5,7},{6,4},{7,5},{8,10},{9,11},{10,... | collective-permute-start | bytes 344072 | tf_op jit(solution)/shard_map/ppermute | solution.py:22
  63.8 3.7 %collective-permute-done.12.refs_1_ = bf16[8,7168]{1,0:T(8,128)(2,1)S(1)} collective-permute-done((bf16[8,7168]{1,0:T(8,128)(2,1)S(1)}, bf16[8,7168]{1,0:T(8,128)(2,1)S(1)}, u32[]{:S(2)}, u32[]{:S(2)}) %collective-permute-start.12) | collective-permute-done | bytes 114720 | tf_op jit(solution)/shard_map/ppermute | solution.py:22
  67.6 0.1 collective-permute-start.13
  67.7 4.2 %collective-permute-done.13.refs_1_ = bf16[4,7168]{1,0:T(4,128)(2,1)S(1)} collective-permute-done((bf16[4,7168]{1,0:T(4,128)(2,1)S(1)}, bf16[4,7168]{1,0:T(4,128)(2,1)S(1)}, u32[]{:S(2)}, u32[]{:S(2)}) %collective-permute-start.13) | collective-permute-done | bytes 57376 | tf_op jit(solution)/shard_map/ppermute | solution.py:22
  71.9 0.4 collective-permute-start.14
  72.3 4.4 %collective-permute-done.14 = bf16[2,7168]{1,0:T(2,128)(2,1)S(1)} collective-permute-done((bf16[2,7168]{1,0:T(2,128)(2,1)S(1)}, bf16[2,7168]{1,0:T(2,128)(2,1)S(1)}, u32[]{:S(2)}, u32[]{:S(2)}) %collective-permute-start.14) | collective-permute-done | bytes 28704 | tf_op jit(solution)/shard_map/ppermute | solution.py:22
  76.7 0.7 add_convert_fusion
  (7 shorter events, 0.2 us)
Async XLA Ops:
  4.8 1.5 %collective-permute-start = (bf16[8,16,512]{2,1,0:T(8,128)(2,1)S(1)}, bf16[8,16,512]{2,1,0:T(8,128)(2,1)S(1)}, u32[]{:S(2)}, u32[]{:S(2)}) collective-permute-start(bf16[8,16,512]{2,1,0:T(8,128)(2,1)S(1)} %get-tuple-element.44), channel_id=1, source_target_pairs={{0,1},{1,0},{2,3},{3,2},{4,5},{5,4},{6,7},{7,6},{8,9},{9,8},{10,11... | collective-permute-start | bytes 393224 | tf_op jit(solution)/shard_map/ppermute | solution.py:22
  6.4 6.7 %collective-permute-start.1 = (bf16[8,16,512]{2,1,0:T(8,128)(2,1)S(1)}, bf16[8,16,512]{2,1,0:T(8,128)(2,1)S(1)}, u32[]{:S(2)}, u32[]{:S(2)}) collective-permute-start(bf16[8,16,512]{2,1,0:T(8,128)(2,1)S(1)} %get-tuple-element.46.after), channel_id=1, source_target_pairs={{0,2},{1,3},{2,0},{3,1},{4,6},{5,7},{6,4},{7,5},{8,10},{9,11},{10,... | collective-permute-start | bytes 393224 | tf_op jit(solution)/shard_map/ppermute | solution.py:22
  13.1 8.4 %collective-permute-start.2 = (bf16[4,16,512]{2,1,0:T(8,128)(2,1)S(1)}, bf16[4,16,512]{2,1,0:T(8,128)(2,1)S(1)}, u32[]{:S(2)}, u32[]{:S(2)}) collective-permute-start(bf16[4,16,512]{2,1,0:T(8,128)(2,1)S(1)} %get-tuple-element.49), channel_id=1, source_target_pairs={{0,8},{1,9},{2,10},{3,11},{4,12},{5,13},{6,14},{7,15},{8,0},{9,1},... | collective-permute-start | bytes 196616 | tf_op jit(solution)/shard_map/ppermute | solution.py:22
  16.0 5.5 %collective-permute-start.3 = (bf16[4,16,512]{2,1,0:T(8,128)(2,1)S(1)}, bf16[4,16,512]{2,1,0:T(8,128)(2,1)S(1)}, u32[]{:S(2)}, u32[]{:S(2)}) collective-permute-start(bf16[4,16,512]{2,1,0:T(8,128)(2,1)S(1)} %get-tuple-element.50), channel_id=1, source_target_pairs={{0,4},{1,5},{2,6},{3,7},{4,0},{5,1},{6,2},{7,3},{8,12},{9,13},{10,... | collective-permute-start | bytes 196616 | tf_op jit(solution)/shard_map/ppermute | solution.py:22
  17.6 6.1 %collective-permute-start.4 = (bf16[4,16,512]{2,1,0:T(8,128)(2,1)S(1)}, bf16[4,16,512]{2,1,0:T(8,128)(2,1)S(1)}, u32[]{:S(2)}, u32[]{:S(2)}) collective-permute-start(bf16[4,16,512]{2,1,0:T(8,128)(2,1)S(1)} %get-tuple-element.51), channel_id=1, source_target_pairs={{0,12},{1,13},{2,14},{3,15},{4,8},{5,9},{6,10},{7,11},{8,4},{9,5},... | collective-permute-start | bytes 196616 | tf_op jit(solution)/shard_map/ppermute | solution.py:22
  17.7 6.0 %copy-start = (bf16[2,7168]{1,0:T(2,128)(2,1)S(1)}, bf16[2,7168]{1,0:T(2,128)(2,1)}, u32[]{:S(2)}) copy-start(bf16[2,7168]{1,0:T(2,128)(2,1)} %refs_8_.1) | copy-start | bytes 86020
  17.7 6.0 %copy-start.2 = (s32[32,1]{1,0:T(8,128)S(1)}, s32[32,1]{1,0:T(8,128)}, u32[]{:S(2)}) copy-start(s32[32,1]{1,0:T(8,128)} %constant.19.refs_4_) | copy-start | bytes 388
  27.0 1.5 %collective-permute-start.5 = (bf16[16,7296]{1,0:T(8,128)(2,1)S(1)}, bf16[16,7296]{1,0:T(8,128)(2,1)S(1)}, u32[]{:S(2)}, u32[]{:S(2)}) collective-permute-start(bf16[16,7296]{1,0:T(8,128)(2,1)S(1)} %get-tuple-element.56), channel_id=1, source_target_pairs={{0,1},{1,0},{2,3},{3,2},{4,5},{5,4},{6,7},{7,6},{8,9},{9,8},{10,11... | collective-permute-start | bytes 700424 | tf_op jit(solution)/shard_map/ppermute | solution.py:22
  28.5 5.3 %collective-permute-start.6 = (bf16[8,7296]{1,0:T(8,128)(2,1)S(1)}, bf16[8,7296]{1,0:T(8,128)(2,1)S(1)}, u32[]{:S(2)}, u32[]{:S(2)}) collective-permute-start(bf16[8,7296]{1,0:T(8,128)(2,1)S(1)} %get-tuple-element.58.after), channel_id=1, source_target_pairs={{0,2},{1,3},{2,0},{3,1},{4,6},{5,7},{6,4},{7,5},{8,10},{9,11},{10,... | collective-permute-start | bytes 350216 | tf_op jit(solution)/shard_map/ppermute | solution.py:22
  33.9 4.9 %collective-permute-start.7 = (bf16[8,7296]{1,0:T(8,128)(2,1)S(1)}, bf16[8,7296]{1,0:T(8,128)(2,1)S(1)}, u32[]{:S(2)}, u32[]{:S(2)}) collective-permute-start(bf16[8,7296]{1,0:T(8,128)(2,1)S(1)} %get-tuple-element.61.after), channel_id=1, source_target_pairs={{0,4},{1,5},{2,6},{3,7},{4,0},{5,1},{6,2},{7,3},{8,12},{9,13},{10,... | collective-permute-start | bytes 350216 | tf_op jit(solution)/shard_map/ppermute | solution.py:22
  38.8 6.9 %collective-permute-start.8 = (bf16[8,7296]{1,0:T(8,128)(2,1)S(1)}, bf16[8,7296]{1,0:T(8,128)(2,1)S(1)}, u32[]{:S(2)}, u32[]{:S(2)}) collective-permute-start(bf16[8,7296]{1,0:T(8,128)(2,1)S(1)} %get-tuple-element.64.after), channel_id=1, source_target_pairs={{0,8},{1,9},{2,10},{3,11},{4,12},{5,13},{6,14},{7,15},{8,0},{9,1},... | collective-permute-start | bytes 350216 | tf_op jit(solution)/shard_map/ppermute | solution.py:22
  39.7 6.0 %copy-start.1 = (f32[7168]{0:T(1024)S(1)}, f32[7168]{0:T(1024)}, u32[]{:S(2)}) copy-start(f32[7168]{0:T(1024)} %param.19) | copy-start | bytes 86020
  45.9 4.9 %collective-permute-start.9 = (bf16[8,7296]{1,0:T(8,128)(2,1)S(1)}, bf16[8,7296]{1,0:T(8,128)(2,1)S(1)}, u32[]{:S(2)}, u32[]{:S(2)}) collective-permute-start(bf16[8,7296]{1,0:T(8,128)(2,1)S(1)} %get-tuple-element.67.after.refs_0_), channel_id=1, source_target_pairs={{0,2},{1,3},{2,0},{3,1},{4,6},{5,7},{6,4},{7,5},{8,10},{9,11},{10,... | collective-permute-start | bytes 350216 | tf_op jit(solution)/shard_map/ppermute | solution.py:22
  50.8 1.6 %collective-permute-start.10 = (bf16[16,7296]{1,0:T(8,128)(2,1)S(1)}, bf16[16,7296]{1,0:T(8,128)(2,1)S(1)}, u32[]{:S(2)}, u32[]{:S(2)}) collective-permute-start(bf16[16,7296]{1,0:T(8,128)(2,1)S(1)} %shard_map.141.first), channel_id=1, source_target_pairs={{0,1},{1,0},{2,3},{3,2},{4,5},{5,4},{6,7},{7,6},{8,9},{9,8},{10,11... | collective-permute-start | bytes 700424 | tf_op jit(solution)/shard_map/ppermute | solution.py:22
  60.7 1.6 %collective-permute-start.11 = (bf16[16,7168]{1,0:T(8,128)(2,1)S(1)}, bf16[16,7168]{1,0:T(8,128)(2,1)S(1)}, u32[]{:S(2)}, u32[]{:S(2)}) collective-permute-start(bf16[16,7168]{1,0:T(8,128)(2,1)S(1)} %get-tuple-element.74), channel_id=1, source_target_pairs={{0,1},{1,0},{2,3},{3,2},{4,5},{5,4},{6,7},{7,6},{8,9},{9,8},{10,11... | collective-permute-start | bytes 688136 | tf_op jit(solution)/shard_map/ppermute | solution.py:22
  62.3 5.3 %collective-permute-start.12 = (bf16[8,7168]{1,0:T(8,128)(2,1)S(1)}, bf16[8,7168]{1,0:T(8,128)(2,1)S(1)}, u32[]{:S(2)}, u32[]{:S(2)}) collective-permute-start(bf16[8,7168]{1,0:T(8,128)(2,1)S(1)} %get-tuple-element.76), channel_id=1, source_target_pairs={{0,2},{1,3},{2,0},{3,1},{4,6},{5,7},{6,4},{7,5},{8,10},{9,11},{10,... | collective-permute-start | bytes 344072 | tf_op jit(solution)/shard_map/ppermute | solution.py:22
  67.6 4.2 %collective-permute-start.13 = (bf16[4,7168]{1,0:T(4,128)(2,1)S(1)}, bf16[4,7168]{1,0:T(4,128)(2,1)S(1)}, u32[]{:S(2)}, u32[]{:S(2)}) collective-permute-start(bf16[4,7168]{1,0:T(4,128)(2,1)S(1)} %get-tuple-element.78), channel_id=1, source_target_pairs={{0,4},{1,5},{2,6},{3,7},{4,0},{5,1},{6,2},{7,3},{8,12},{9,13},{10,... | collective-permute-start | bytes 172040 | tf_op jit(solution)/shard_map/ppermute | solution.py:22
  71.9 4.8 %collective-permute-start.14 = (bf16[2,7168]{1,0:T(2,128)(2,1)S(1)}, bf16[2,7168]{1,0:T(2,128)(2,1)S(1)}, u32[]{:S(2)}, u32[]{:S(2)}) collective-permute-start(bf16[2,7168]{1,0:T(2,128)(2,1)S(1)} %get-tuple-element.80), channel_id=1, source_target_pairs={{0,8},{1,9},{2,10},{3,11},{4,12},{5,13},{6,14},{7,15},{8,0},{9,1},... | collective-permute-start | bytes 86024 | tf_op jit(solution)/shard_map/ppermute | solution.py:22
